TPU v7x, 128 devices: a whole 4x4x4 slice. The times are simulated.
128 devices in a mesh: seq: 8 (over y, z_hi), fsdp: 16 (over z_lo, x, core).
Axes of the slice: x: 4, y: 4, z: 4 (z_hi: 2, z_lo: 2; z = z_hi * 2 + z_lo), core: 2. Of those that a mesh axis runs over, the one named last changes fastest.
Arguments:
- hidden_in: bfloat16 [16, 1024, 5120], P('fsdp', 'seq'), may hold values from -6 to 6
- queries: bfloat16 [16, 1024, 4096], P('fsdp', 'seq'), may hold values from -48 to 48
- saved_keys: bfloat16 [16, 1024, 512], P('fsdp', 'seq'), may hold values from -6 to 6
- value_matrix: bfloat16 [5120, 512], P('fsdp'), may hold values from -0.078125 to 0.078125
- output_gradient: bfloat16 [16, 1024, 4096], P('fsdp', 'seq'), may hold values from -6 to 6
- passage_index: int32 [16, 1024], P('fsdp'), may hold values from 0 to 11, never falling along the last dimension, each value on 1 to 169 neighbouring positions
Outputs:
- query_gradients: bfloat16 [16, 1024, 4096], P('fsdp', 'seq')
- key_gradients: bfloat16 [16, 1024, 512], P('fsdp', 'seq')
- grad_input: bfloat16 [16, 1024, 5120], P('fsdp', 'seq')
- grad_weight: float32 [5120, 512], P('fsdp')
Inputs may be any that keep to these rules, and one draw needn't show every extreme that they name: `passage_index`: never falls along a list; passage 0 is the list's header, which every later token of the list sees; each passage has 1 to 169 tokens.
All inputs are finite; a program needn't handle non-finite values.
Results may differ from a plain program's by a relative error of at most 0.007.
Values may be sent and summed in bfloat16 or wider, within the bound.
No kernel may reach another device: no remote copies, remote signals or barrier semaphores. Data moves between devices by JAX's collectives and lax.ppermute only.
A program may use at most 128 MiB of HBM per device.

v0:
```python
import math

import jax
import jax.numpy as jnp
from jax import lax
from jax.sharding import PartitionSpec as P

QUERY_HEADS = 32
KEY_HEADS = 4
HEAD_WIDTH = 128


def block_grads(q_block, k_block, v_block, g_block, allowed):
    inv_root = 1.0 / math.sqrt(q_block.shape[-1])
    scores = (
        jnp.einsum("igcd,jgd->gcij", q_block, k_block, preferred_element_type=jnp.float32)
        * inv_root
    )
    scores = jnp.where(allowed[None, None], scores, -jnp.inf)
    highest = jnp.max(scores, axis=-1, keepdims=True)
    weights = jnp.exp(scores - highest)
    prob_full = weights / jnp.sum(weights, axis=-1, keepdims=True)
    dprobs = jnp.einsum("igcd,jgd->gcij", g_block, v_block, preferred_element_type=jnp.float32)
    row_delta = jnp.sum(prob_full * dprobs, axis=-1, keepdims=True)
    dscores = (prob_full * (dprobs - row_delta) * inv_root).astype(jnp.bfloat16)
    probs_half = prob_full.astype(jnp.bfloat16)
    query_gradient = jnp.einsum(
        "gcij,jgd->igcd", dscores, k_block, preferred_element_type=jnp.float32
    ).astype(jnp.bfloat16)
    key_part = jnp.einsum("gcij,igcd->jgd", dscores, q_block, preferred_element_type=jnp.float32)
    value_part = jnp.einsum(
        "gcij,igcd->jgd", probs_half, g_block, preferred_element_type=jnp.float32
    )
    return (query_gradient, key_part, value_part)


def mask_for(key_pos, query_pos, segments):
    key_seg = jnp.take(segments, jnp.clip(key_pos, 0, segments.shape[0] - 1))
    query_seg = jnp.take(segments, query_pos)
    return (key_pos[None, :] <= query_pos[:, None]) & (
        (key_seg[None, :] == query_seg[:, None]) | (key_seg[None, :] == 0)
    )


def on_device(hidden_in, queries, saved_keys, value_matrix, output_gradient, passage_index):
    sequence_parts = lax.axis_size("seq")
    passage_lists, token_rows, width = hidden_in.shape
    seqlen = token_rows * sequence_parts
    key_value_width = KEY_HEADS * HEAD_WIDTH
    flat_input = hidden_in.reshape(passage_lists * token_rows, width)
    whole_weight = lax.all_gather(value_matrix, "fsdp", axis=0, tiled=True)
    value_accumulator = jnp.dot(flat_input, whole_weight, preferred_element_type=jnp.float32)
    value_rows_all = value_accumulator.astype(jnp.bfloat16).reshape(
        passage_lists, token_rows, KEY_HEADS, HEAD_WIDTH
    )
    heads_local = QUERY_HEADS // sequence_parts
    head_copies = max(1, sequence_parts // KEY_HEADS)
    head_slots = KEY_HEADS * head_copies
    kv_local = head_slots // sequence_parts
    per_kv = heads_local // kv_local
    value_wide = jnp.repeat(value_rows_all, head_copies, axis=2)
    key_full_width = jnp.repeat(
        saved_keys.reshape(passage_lists, token_rows, KEY_HEADS, HEAD_WIDTH), head_copies, axis=2
    )
    query_heads = queries.reshape(passage_lists, token_rows, QUERY_HEADS, HEAD_WIDTH)
    grad_heads = output_gradient.reshape(passage_lists, token_rows, QUERY_HEADS, HEAD_WIDTH)
    q_all, k_all, v_all, g_all = (
        lax.all_to_all(query_heads, "seq", split_axis=2, concat_axis=1, tiled=True),
        lax.all_to_all(key_full_width, "seq", split_axis=2, concat_axis=1, tiled=True),
        lax.all_to_all(value_wide, "seq", split_axis=2, concat_axis=1, tiled=True),
        lax.all_to_all(grad_heads, "seq", split_axis=2, concat_axis=1, tiled=True),
    )
    block_rows = min(seqlen, max(512, seqlen // 8))
    position = jnp.arange(seqlen)
    segments = passage_index[0]
    q_list = q_all[0].reshape(seqlen, kv_local, per_kv, HEAD_WIDTH)
    g_list = g_all[0].reshape(seqlen, kv_local, per_kv, HEAD_WIDTH)
    k_list = k_all[0]
    v_list = v_all[0]
    key_total = jnp.zeros((seqlen, kv_local, HEAD_WIDTH), jnp.float32)
    value_total = jnp.zeros((seqlen, kv_local, HEAD_WIDTH), jnp.float32)
    dq_blocks = []
    for row_start in range(0, seqlen, block_rows):
        row_stop = row_start + block_rows
        query_pos = position[row_start:row_stop]
        allowed = mask_for(position, query_pos, segments)
        query_gradient, key_part, value_part = block_grads(
            q_list[row_start:row_stop], k_list, v_list, g_list[row_start:row_stop], allowed
        )
        key_total = key_total.at[:seqlen].add(key_part)
        value_total = value_total.at[:seqlen].add(value_part)
        dq_blocks.append(query_gradient)
    dq_lists = [jnp.concatenate(dq_blocks, axis=0).reshape(seqlen, heads_local, HEAD_WIDTH)]
    dk_lists = [key_total]
    dv_lists = [value_total]
    dq_heads = jnp.stack(dq_lists)
    dk_heads = jnp.stack(dk_lists)
    dv_heads = jnp.stack(dv_lists)
    dq_tokens = lax.all_to_all(dq_heads, "seq", split_axis=1, concat_axis=2, tiled=True)
    key_token_grads, value_token_grads = (
        lax.all_to_all(dk_heads, "seq", split_axis=1, concat_axis=2, tiled=True),
        lax.all_to_all(dv_heads, "seq", split_axis=1, concat_axis=2, tiled=True),
    )
    key_gradient_sum = key_token_grads.reshape(
        passage_lists, token_rows, KEY_HEADS, head_copies, HEAD_WIDTH
    ).sum(axis=3)
    value_gradient_sum = value_token_grads.reshape(
        passage_lists, token_rows, KEY_HEADS, head_copies, HEAD_WIDTH
    ).sum(axis=3)
    query_gradients = dq_tokens.reshape(passage_lists, token_rows, QUERY_HEADS * HEAD_WIDTH)
    key_gradients = key_gradient_sum.astype(jnp.bfloat16).reshape(
        passage_lists, token_rows, key_value_width
    )
    value_weight_gradient = value_gradient_sum.astype(jnp.bfloat16).reshape(
        passage_lists * token_rows, key_value_width
    )
    projected = jnp.dot(value_weight_gradient, whole_weight.T, preferred_element_type=jnp.float32)
    grad_input = projected.astype(jnp.bfloat16).reshape(passage_lists, token_rows, width)
    local_term = lax.dot_general(
        flat_input,
        value_weight_gradient,
        (((0,), (0,)), ((), ())),
        preferred_element_type=jnp.float32,
    )
    fsdp_devices = lax.axis_size("fsdp")
    rows_each = width // (sequence_parts * fsdp_devices)
    reordered = (
        local_term.reshape(fsdp_devices, sequence_parts, rows_each, -1)
        .transpose(1, 0, 2, 3)
        .reshape(width, -1)
    )
    piece_sum = lax.psum_scatter(reordered, ("seq", "fsdp"), scatter_dimension=0, tiled=True)
    grad_weight = lax.all_gather(piece_sum.astype(jnp.bfloat16), "seq", axis=0, tiled=True).astype(
        piece_sum.dtype
    )
    return (query_gradients, key_gradients, grad_input, grad_weight)


def solution(mesh):
    placed = (
        P("fsdp", "seq", None),
        P("fsdp", "seq", None),
        P("fsdp", "seq", None),
        P("fsdp", None),
        P("fsdp", "seq", None),
        P("fsdp", None),
    )
    return jax.shard_map(
        on_device,
        mesh=mesh,
        in_specs=placed,
        out_specs=(
            P("fsdp", "seq", None),
            P("fsdp", "seq", None),
            P("fsdp", "seq", None),
            P("fsdp", None),
        ),
        check_vma=False,
    )
```

profile of v0, /device:TPU:2, one launch (start us, length us, event | category | flops | bytes accessed | tf_op | source)
XLA Modules:
  0.0 818.9 jit_solution(16623430837112237822)
XLA Ops:
  8.8 2.3 copy.62
  11.1 7.8 all-to-all-start.1
  18.9 3.4 gather_fusion.2
  22.3 4.5 gather_fusion
  26.8 2.3 copy.67
  29.1 5.6 all-to-all-done.1
  34.7 4.2 all-to-all-start.3
  39.0 2.3 gather_fusion.1
  41.4 1.4 fusion.25
  42.8 1.3 copy.64
  44.1 1.3 fusion.58
  45.4 0.8 copy.72
  46.3 8.1 all-to-all-done.3
  55.2 4.2 all-to-all-start
  59.6 2.3 copy.69
  61.8 1.3 fusion.59
  64.8 3.0 all-to-all-done
  67.8 2.5 fusion.13
  70.3 1.9 fusion.12
  72.2 3.6 fusion.9
  76.0 2.3 fusion.30
  78.3 2.4 fusion.38
  80.8 14.1 %all_to_all.105 = f32[1,1024,1,128]{3,2,0,1:T(1,128)} all-to-all(f32[1,1024,1,128]{3,2,0,1:T(1,128)S(1)} %bitcast.254), channel_id=1, replica_groups=mesh['seq'=8,'fsdp'=16] {'seq'}, dimensions={1} | all-to-all | bytes 1048576 | tf_op jit(solution)/shard_map/all_to_all | solution.py:102
  94.8 1.1 reduce_sum.59
  96.1 5.5 convolution_bitcast_fusion
  101.6 11.4 %copy.81 = f32[5120,512]{1,0:T(8,128)} copy(f32[5120,512]{0,1:T(8,128)} %convolution_bitcast_fusion) | data formatting | bytes 20971520 | tf_op jit(solution)/shard_map/dot_general | solution.py:119
  113.0 9.8 %copy.82 = f32[8,16,40,512]{3,2,1,0:T(8,128)} copy(f32[8,16,40,512]{3,2,0,1:T(8,128)} %bitcast.230) | data formatting | bytes 20971520 | tf_op jit(solution)/shard_map/transpose | solution.py:129
  122.8 3.5 fusion.45
  126.4 11.5 %all_to_all.106 = bf16[1,128,8,128]{3,1,0,2:T(8,128)(2,1)S(1)} all-to-all(bf16[1,128,8,128]{3,1,0,2:T(8,128)(2,1)S(1)} %bitcast.248), channel_id=1, replica_groups=mesh['seq'=8,'fsdp'=16] {'seq'}, dimensions={2} | all-to-all | bytes 524288 | tf_op jit(solution)/shard_map/all_to_all | solution.py:70
  138.0 5.7 fusion
  143.7 4.3 fusion.16
  148.0 3.4 convolution_bitcast_fusion.1
  151.5 3.1 fusion.4
  154.6 2.9 fusion.15
  157.6 2.1 copy-done.5
  159.6 2.1 fusion.41
  161.7 3.5 all-to-all-start.5
  165.2 3.5 fusion.37
  168.8 3.5 fusion.36
  172.4 1.8 copy.75
  174.8 6.4 all-to-all-start.4
  181.3 5.4 fusion.14
  187.6 6.7 all-to-all-done.4
  194.6 1.6 reshape.480
  196.2 578.9 %reduce-scatter.2.cloned.1.call-done = f32[40,512]{1,0:T(8,128)} async-done(((f32[5120,512]{1,0:T(8,128)}), f32[40,512]{1,0:T(8,128)}) %reduce-scatter.2.cloned.1.call-update) | async-done | bytes 81936 | tf_op jit(solution)/shard_map/reduce_scatter | solution.py:132
  775.2 0.9 convert_element_type.99
  776.0 34.5 %all_gather.7 = bf16[320,512]{1,0:T(8,128)(2,1)S(1)} all-gather(bf16[40,512]{1,0:T(8,128)(2,1)S(1)} %convert_element_type.99), channel_id=1, replica_groups=mesh['seq'=8,'fsdp'=16] {'seq'}, dimensions={0}, use_global_device_ids=true | all-gather | bytes 368640 | tf_op jit(solution)/shard_map/all_gather | solution.py:133
  810.6 0.9 convert_element_type.100
  (61 shorter events, 6.0 us)
Async XLA Ops:
  8.0 88.1 %copy-start = (bf16[1,128,5120]{2,1,0:T(8,128)(2,1)S(1)}, bf16[1,128,5120]{2,1,0:T(8,128)(2,1)}, u32[]{:S(2)}) copy-start(bf16[1,128,5120]{2,1,0:T(8,128)(2,1)} %param.26) | copy-start | bytes 3932164
  8.0 14.3 %copy-start.2 = (s32[1,1024]{1,0:T(1,128)S(1)}, s32[1,1024]{1,0:T(1,128)}, u32[]{:S(2)}) copy-start(s32[1,1024]{1,0:T(1,128)} %param.31) | copy-start | bytes 12292
  8.0 114.8 %all-gather.2.cloned.1.call-start = ((), (), s32[]{:S(2)}) async-start(), calls=%async_computation.8 | async-start | bytes 5570560 | tf_op jit(solution)/shard_map/all_gather | solution.py:51
  8.8 32.5 %copy-start.10 = (bf16[1,128,512]{2,1,0:T(8,128)(2,1)S(1)}, bf16[1,128,512]{2,1,0:T(8,128)(2,1)}, u32[]{:S(2)}) copy-start(bf16[1,128,512]{2,1,0:T(8,128)(2,1)} %param.28) | copy-start | bytes 393220
  11.1 23.6 %all-to-all-start.1 = ((bf16[1,128,32,128]{1,3,0,2:T(8,128)(2,1)}), bf16[1,128,32,128]{1,3,0,2:T(8,128)(2,1)S(1)}, u32[]{:S(2)}, u32[]{:S(2)}) async-start(bf16[1,128,32,128]{1,3,0,2:T(8,128)(2,1)} %bitcast.234), calls=%async_computation.1 | async-start | bytes 2097152 | tf_op jit(solution)/shard_map/all_to_all | solution.py:68
  34.7 19.7 %all-to-all-start.3 = ((bf16[1,128,32,128]{1,3,0,2:T(8,128)(2,1)}), bf16[1,128,32,128]{1,3,0,2:T(8,128)(2,1)}, u32[]{:S(2)}, u32[]{:S(2)}) async-start(bf16[1,128,32,128]{1,3,0,2:T(8,128)(2,1)} %bitcast.233), calls=%async_computation.3 | async-start | bytes 2097152 | tf_op jit(solution)/shard_map/all_to_all | solution.py:71
  55.2 12.6 %all-to-all-start = ((bf16[1,128,8,128]{3,1,0,2:T(8,128)(2,1)}), bf16[1,128,8,128]{3,1,0,2:T(8,128)(2,1)S(1)}, u32[]{:S(2)}, u32[]{:S(2)}) async-start(bf16[1,128,8,128]{3,1,0,2:T(8,128)(2,1)} %bitcast.1), calls=%async_computation | async-start | bytes 524288 | tf_op jit(solution)/shard_map/all_to_all | solution.py:69
  59.3 715.8 %reduce-scatter.2.cloned.1.call-start = ((), (), s32[]{:S(2)}) async-start(), calls=%async_computation.9 | async-start | bytes 10567680 | tf_op jit(solution)/shard_map/reduce_scatter | solution.py:132
  70.3 8.0 copy-start.4
  72.2 3.8 copy-start.3
  72.2 3.8 copy-start.7
  76.0 2.3 copy-start.9
  122.8 28.6 %slice-start = ((s8[8388608]{0:T(1024)(128)(4,1)}), s8[4194304]{0:T(1024)(128)(4,1)S(1)}, s32[]{:S(2)}) async-start(s8[8388608]{0:T(1024)(128)(4,1)} %bitcast.225), calls=%async_computation.10 | async-start | bytes 8388608
  126.3 17.3 %slice-start.2 = ((s8[8388608]{0:T(1024)(128)(4,1)}), s8[4194304]{0:T(1024)(128)(4,1)S(1)}, s32[]{:S(2)}) async-start(s8[8388608]{0:T(1024)(128)(4,1)} %bitcast.227), calls=%async_computation.12 | async-start | bytes 8388608
  138.0 5.7 slice-start.3
  138.0 13.5 %slice-start.1 = ((s8[8388608]{0:T(1024)(128)(4,1)}), s8[4194304]{0:T(1024)(128)(4,1)S(1)}, s32[]{:S(2)}) async-start(s8[8388608]{0:T(1024)(128)(4,1)} %bitcast.225), calls=%async_computation.11 | async-start | bytes 8388608
  143.7 4.3 copy-start.6
  143.7 7.8 copy-start.8
  157.6 2.1 copy-start.5
  161.7 13.1 %all-to-all-start.5 = ((f32[1,1024,1,128]{3,2,0,1:T(1,128)}), f32[1,1024,1,128]{3,2,0,1:T(1,128)S(1)}, u32[]{:S(2)}, u32[]{:S(2)}) async-start(f32[1,1024,1,128]{3,2,0,1:T(1,128)} %bitcast.59), calls=%async_computation.5 | async-start | bytes 1048576 | tf_op jit(solution)/shard_map/all_to_all | solution.py:101
  172.3 639.2 %copy-start.1 = (bf16[1,128,5120]{2,1,0:T(8,128)(2,1)S(1)}, bf16[1,128,5120]{2,1,0:T(8,128)(2,1)}, u32[]{:S(2)}) copy-start(bf16[1,128,5120]{2,1,0:T(8,128)(2,1)} %param.26) | copy-start | bytes 3932164
  174.8 19.4 %all-to-all-start.4 = ((bf16[1,1024,4,128]{3,2,0,1:T(4,128)(2,1)}), bf16[1,1024,4,128]{3,2,0,1:T(4,128)(2,1)S(1)}, u32[]{:S(2)}, u32[]{:S(2)}) async-start(bf16[1,1024,4,128]{3,2,0,1:T(4,128)(2,1)} %copy.75), calls=%async_computation.4 | async-start | bytes 2097152 | tf_op jit(solution)/shard_map/all_to_all | solution.py:99
Sparse Core Ops, SparseCore 0:
  10.6 59.4 all-gather.1
Sparse Core Ops, SparseCore 1:
  122.9 652.2 reduce-scatter.1
where the time goes:
time: 828 us; the launch traced here: 819 us
  waiting for transfers between devices  604 us (73%)
  blocking collectives  60.1 us (7%)
  local copies, waits for them, and re-layouts  52.6 us (6%)
  matrix products  44.9 us (5%)
  starting transfers between devices  26.4 us (3%)
  between operations  15.9 us (2%)
  other arithmetic  15.3 us (2%)
    reduce_scatter x1, waiting for transfers between devices, on_device(): lax.psum_scatter(reordered, ('seq', 'fsdp'), scatter_dimension=0, tiled=T...  579 us
    all_gather x1, blocking collectives, on_device(): lax.all_gather(piece_sum.astype(jnp.bfloat16), 'seq', axis=0, tiled=True)  34.5 us
  transfers between devices with their start and end apart: 7, of which 6 were waited for; matrix products, arithmetic and copies ran while one was open for 13% of the time, Pallas kernels for 0%

commit v1 on v0

v1 whole, which is shorter than its diff:
```python
import math

import jax
import jax.numpy as jnp
from jax import lax
from jax.experimental import pallas as pl
from jax.experimental.pallas import tpu as pltpu
from jax.sharding import Mesh
from jax.sharding import PartitionSpec as P

KEY_HEADS = 4
GROUP = 8
HEAD = 128
ROWS = 128
BACK = 192
SLOTS = 2 * BACK + ROWS
SEQ = ("y", "zh")
FSDP = ("zl", "x", "c")
SWAP = ((0, 1), (1, 0))
ROOT = 1.0 / math.sqrt(HEAD)
BF = jnp.bfloat16
F32 = jnp.float32


def stacked(ref):
    return jnp.concatenate([ref[:, h * HEAD : (h + 1) * HEAD] for h in range(GROUP)], axis=0)


def probs_kernel(q_ref, k_ref, g_ref, bias_ref, p_ref, dv_ref):
    scores = lax.dot_general(
        k_ref[...], stacked(q_ref), (((1,), (1,)), ((), ())), preferred_element_type=F32
    )
    bias = bias_ref[...]
    scores = scores + jnp.concatenate([bias] * GROUP, axis=1)
    highest = jnp.max(scores, axis=0, keepdims=True)
    weights = jnp.exp((scores - highest) * ROOT)
    total = jnp.sum(weights, axis=0, keepdims=True)
    probs = (weights * (1.0 / total)).astype(BF)
    p_ref[0] = probs
    dv_ref[...] = jnp.dot(probs, stacked(g_ref), preferred_element_type=F32)


def scores_kernel(q_ref, k_ref, g_ref, v_ref, p_ref, dq_ref, dk_ref):
    dprobs = lax.dot_general(
        v_ref[...], stacked(g_ref), (((1,), (1,)), ((), ())), preferred_element_type=F32
    )
    probs = p_ref[0].astype(F32)
    delta = jnp.sum(probs * dprobs, axis=0, keepdims=True)
    dscores = (probs * (dprobs - delta) * ROOT).astype(BF)
    dk_ref[...] = jnp.dot(dscores, stacked(q_ref), preferred_element_type=F32)
    dq = lax.dot_general(
        k_ref[...], dscores, (((0,), (0,)), ((), ())), preferred_element_type=F32
    )
    for h in range(GROUP):
        part = slice(h * HEAD, (h + 1) * HEAD)
        dq_ref[:, part] = dq[:, part].T.astype(BF)


def column(rows, width):
    return pl.BlockSpec((rows, width), lambda g: (0, g))


def probs_call(q, k, g, bias):
    return pl.pallas_call(
        probs_kernel,
        grid=(KEY_HEADS,),
        in_specs=[
            column(ROWS, GROUP * HEAD),
            column(SLOTS, HEAD),
            column(ROWS, GROUP * HEAD),
            pl.BlockSpec((SLOTS, ROWS), lambda g: (0, 0)),
        ],
        out_specs=[
            pl.BlockSpec((1, SLOTS, GROUP * ROWS), lambda g: (g, 0, 0)),
            column(SLOTS, HEAD),
        ],
        out_shape=[
            jax.ShapeDtypeStruct((KEY_HEADS, SLOTS, GROUP * ROWS), BF),
            jax.ShapeDtypeStruct((SLOTS, KEY_HEADS * HEAD), F32),
        ],
        compiler_params=pltpu.CompilerParams(vmem_limit_bytes=40 << 20),
        cost_estimate=pl.CostEstimate(
            flops=4 * SLOTS * ROWS * 32 * HEAD, bytes_accessed=8 << 20, transcendentals=SLOTS * ROWS * 32
        ),
        name="probs",
    )(q, k, g, bias)


def scores_call(q, k, g, v, p):
    return pl.pallas_call(
        scores_kernel,
        grid=(KEY_HEADS,),
        in_specs=[
            column(ROWS, GROUP * HEAD),
            column(SLOTS, HEAD),
            column(ROWS, GROUP * HEAD),
            column(SLOTS, HEAD),
            pl.BlockSpec((1, SLOTS, GROUP * ROWS), lambda g: (g, 0, 0)),
        ],
        out_specs=[column(ROWS, GROUP * HEAD), column(SLOTS, HEAD)],
        out_shape=[
            jax.ShapeDtypeStruct((ROWS, KEY_HEADS * GROUP * HEAD), BF),
            jax.ShapeDtypeStruct((SLOTS, KEY_HEADS * HEAD), F32),
        ],
        compiler_params=pltpu.CompilerParams(vmem_limit_bytes=40 << 20),
        cost_estimate=pl.CostEstimate(
            flops=6 * SLOTS * ROWS * 32 * HEAD, bytes_accessed=8 << 20, transcendentals=0
        ),
        name="scores",
    )(q, k, g, v, p)


def spread(block, y, zh):
    other = lax.ppermute(block, "zh", SWAP)
    pair = jnp.where(
        zh == 0, jnp.concatenate([block, other]), jnp.concatenate([other, block])
    )
    before = lax.ppermute(pair, "y", ((0, 1), (1, 2), (2, 3)))
    to_last = lax.ppermute(pair[:BACK], "y", ((0, 3),))
    to_third = lax.ppermute(pair[:BACK], "y", ((0, 2),))
    header = jnp.where(
        y == 0,
        pair[:BACK],
        jnp.where(y == 1, before[:BACK], jnp.where(y == 2, to_third, to_last)),
    )
    window = jnp.where(
        zh == 0, before[2 * ROWS - BACK :], jnp.concatenate([before[BACK:], other])
    )
    return jnp.concatenate([header, window, block])


def collected(slots, y, zh):
    header, window, own = slots[:BACK], slots[BACK : 2 * BACK], slots[2 * BACK :]
    tail = 2 * ROWS - BACK
    zeros = jnp.zeros((2 * ROWS, slots.shape[1]), F32)
    before = jnp.where(
        zh == 0,
        zeros.at[tail:].set(window),
        zeros.at[BACK:].set(window[:tail]),
    ) + jnp.where(y == 1, zeros.at[:BACK].set(header), 0.0)
    half_header = header.astype(BF)
    from_next = lax.ppermute(before.astype(BF), "y", ((1, 0), (2, 1), (3, 2)))
    from_last = lax.ppermute(half_header, "y", ((3, 0),))
    from_third = lax.ppermute(half_header, "y", ((2, 0),))
    first = header + from_last.astype(F32) + from_third.astype(F32)
    pair = from_next.astype(F32) + jnp.where(y == 0, zeros.at[:BACK].set(first), 0.0)
    low, high = pair[:ROWS], pair[ROWS:]
    low = low + jnp.where(zh == 1, window[tail:], 0.0)
    sent = lax.ppermute(jnp.where(zh == 0, high, low).astype(BF), "zh", SWAP)
    return own + jnp.where(zh == 0, low, high) + sent.astype(F32)


def slot_bias(passages, s):
    token = s * ROWS + jnp.arange(ROWS)
    mine = lax.dynamic_slice(passages, (s * ROWS,), (ROWS,))
    padded = jnp.concatenate([jnp.zeros((BACK,), passages.dtype), passages])
    near = lax.dynamic_slice(padded, (s * ROWS,), (BACK + ROWS,))
    head_ok = (passages[:BACK, None] == 0) & (jnp.arange(BACK)[:, None] <= token[None])
    near_token = s * ROWS - BACK + jnp.arange(BACK + ROWS)
    near_ok = (
        (near[:, None] == mine[None])
        & (near[:, None] != 0)
        & (near_token[:, None] <= token[None])
    )
    return jnp.where(jnp.concatenate([head_ok, near_ok]), 0.0, -1e30).astype(F32)


def on_device(hidden_in, queries, saved_keys, value_matrix, output_gradient, passage_index):
    y, zh, c = lax.axis_index("y"), lax.axis_index("zh"), lax.axis_index("c")
    s = lax.axis_index(SEQ)
    hidden, q, k, g = hidden_in[0], queries[0], saved_keys[0], output_gradient[0]
    width = hidden.shape[1]
    kv = k.shape[1]
    each = width // 16
    weight = lax.all_gather(value_matrix, FSDP, axis=0, tiled=True)
    by_x = hidden.reshape(ROWS, 2, 4, 2, each).transpose(2, 0, 1, 3, 4).reshape(4, ROWS, 4 * each)
    crossed = lax.all_to_all(by_x, "x", 0, 0)
    bias = slot_bias(passage_index[0], s)
    k_slots = spread(k, y, zh)
    probs, dv_slots = probs_call(q, k_slots, g, bias)
    value_grad = collected(dv_slots, y, zh).astype(BF)
    gathered = lax.all_to_all(jnp.broadcast_to(value_grad[None], (4, ROWS, kv)), "x", 0, 0)
    term = lax.dot_general(
        crossed.reshape(4 * ROWS, 4 * each),
        gathered.reshape(4 * ROWS, kv),
        (((0,), (0,)), ((), ())),
        preferred_element_type=F32,
    ).reshape(2, 2, each, kv)
    kept = lax.dynamic_index_in_dim(term, c, 1, keepdims=False)
    given = lax.dynamic_index_in_dim(term, 1 - c, 1, keepdims=False).astype(BF)
    term = kept + lax.ppermute(given, "c", SWAP).astype(F32)
    pieces = term.astype(BF).reshape(2, 8, each // 8, kv).transpose(1, 0, 2, 3)
    pieces = lax.all_to_all(
        pieces.reshape(16, each // 8, kv), ("y", "zh", "zl"), 0, 0
    )
    piece = jnp.sum(pieces.astype(F32), axis=0).astype(BF)
    grad_weight = lax.all_to_all(
        jnp.broadcast_to(piece[None], (8,) + piece.shape), SEQ, 0, 0
    )
    grad_weight = grad_weight.reshape(each, kv).astype(F32)

    values = jnp.dot(hidden, weight, preferred_element_type=F32).astype(BF)
    v_slots = spread(values, y, zh)
    dq, dk_slots = scores_call(q, k_slots, g, v_slots, probs)
    key_grad = collected(dk_slots, y, zh).astype(BF)
    grad_input = lax.dot_general(
        value_grad, weight, (((1,), (1,)), ((), ())), preferred_element_type=F32
    ).astype(BF)
    return dq[None], key_grad[None], grad_input[None], grad_weight


def solution(mesh):
    fine = Mesh(mesh.devices.reshape(4, 2, 2, 4, 2), ("y", "zh", "zl", "x", "c"))
    tokens = P(FSDP, SEQ, None)
    return jax.shard_map(
        on_device,
        mesh=fine,
        in_specs=(tokens, tokens, tokens, P(FSDP, None), tokens, P(FSDP, None)),
        out_specs=(tokens, tokens, tokens, P(FSDP, None)),
        check_vma=False,
    )
```

time: 828 us -> 182 us (0.22)
  waiting for transfers between devices: 604 us -> 47 us
  blocking collectives: 60.1 us -> 0 us
  starting transfers between devices: 26.4 us -> 62.1 us
  matrix products: 44.9 us -> 12.3 us
  local copies, waits for them, and re-layouts: 52.6 us -> 22.3 us
  Pallas kernels: 0 us -> 11.6 us
    reduce_scatter x1 -> x0, waiting for transfers between devices: 579 us -> none  [on_device(): lax.psum_scatter(reordered, ('seq', 'fsdp'), scatter_dimension=0, tiled=T...]
    ppermute x0 -> x17, starting transfers between devices: none -> 38.4 us  [the longest x2 9.79 us: spread(): to_third = lax.ppermute(pair[:BACK], 'y', ((0, 2),))]
    all_gather x1 -> x0, blocking collectives: 34.5 us -> none  [on_device(): lax.all_gather(piece_sum.astype(jnp.bfloat16), 'seq', axis=0, tiled=True)]
    dot_general x13 -> x3, matrix products: 44.9 us -> 12.3 us  [the longest x1 5.35 us: on_device(): lax.dot_general(value_grad, weight, (((1,), (1,)), ((), ())), preferred_e...]
    ppermute x0 -> x17, waiting for transfers between devices: none -> 32.4 us  [the longest x2 9.12 us: spread(): other = lax.ppermute(block, 'zh', SWAP)]
    all_to_all x2 -> x0, blocking collectives: 25.6 us -> none  [the longest x1 14.1 us: on_device(): lax.all_to_all(dv_heads, 'seq', split_axis=1, concat_axis=2, tiled=True)]
    pallas_call x0 -> x2, Pallas kernels: none -> 11.6 us  [the longest x1 6.05 us: scores_call(): pl.pallas_call(scores_kernel, grid=(KEY_HEADS,), in_specs=[column(ROWS, G...]
    gather x3 -> x0, local copies, waits for them, and re-layouts: 10.2 us -> none  [the longest x2 5.66 us: mask_for(): query_seg = jnp.take(segments, query_pos)]
  transfers between devices with their start and end apart: 7 -> 22, of which waited for: 6 -> 11; matrix products, arithmetic and copies ran while one was open for 13% -> 20% of each run, Pallas kernels for 0% -> 6%
where the time goes in v1:
time: 182 us; the launch traced here: 179 us
  starting transfers between devices  62.1 us (34%)
  waiting for transfers between devices  47 us (26%)
  local copies, waits for them, and re-layouts  22.3 us (12%)
  between operations  14.6 us (8%)
  matrix products  12.3 us (7%)
  Pallas kernels  11.6 us (6%)
  other arithmetic  8.84 us (5%)
    all_to_all x1, starting transfers between devices, on_device(): lax.all_to_all(pieces.reshape(16, each // 8, kv), ('y', 'zh', 'zl'), 0, 0)  10.5 us
    ppermute x2, starting transfers between devices, spread(): to_third = lax.ppermute(pair[:BACK], 'y', ((0, 2),))  9.79 us
    ppermute x2, waiting for transfers between devices, spread(): other = lax.ppermute(block, 'zh', SWAP)  9.12 us
    unnamed x27, local copies, waits for them, and re-layouts  8.65 us
    ppermute x2, starting transfers between devices, spread(): other = lax.ppermute(block, 'zh', SWAP)  7.46 us
    all_to_all x1, waiting for transfers between devices, on_device(): crossed = lax.all_to_all(by_x, 'x', 0, 0)  7.3 us
    all_to_all x1, waiting for transfers between devices, on_device(): lax.all_to_all(jnp.broadcast_to(value_grad[None], (4, ROWS, kv)), 'x', 0, 0)  6.63 us
    ppermute x2, waiting for transfers between devices, spread(): before = lax.ppermute(pair, 'y', ((0, 1), (1, 2), (2, 3)))  6.47 us
  transfers between devices with their start and end apart: 22, of which 11 were waited for; matrix products, arithmetic and copies ran while one was open for 20% of the time, Pallas kernels for 6%

profile of v1, /device:TPU:2, one launch (start us, length us, event | category | flops | bytes accessed | tf_op | source)
XLA Modules:
  0.0 178.7 jit_solution(16883083148308139881)
XLA Ops:
  7.9 4.0 %collective-permute-start = (bf16[128,512]{1,0:T(8,128)(2,1)}, bf16[128,512]{1,0:T(8,128)(2,1)S(1)}, u32[]{:S(2)}, u32[]{:S(2)}) collective-permute-start(bf16[128,512]{1,0:T(8,128)(2,1)} %bitcast.53), channel_id=1, source_target_pairs={{0,16},{16,0},{1,17},{17,1},{2,18},{18,2},{3,19},{19,3},{4,20},{20... | collective-permute-start | bytes 393224 | tf_op jit(solution)/shard_map/ppermute | solution.py:114
  14.2 1.4 collective-permute-done
  15.6 1.0 maximum_select_fusion
  16.7 5.2 %collective-permute-start.2 = (bf16[192,512]{1,0:T(8,128)(2,1)S(1)}, bf16[192,512]{1,0:T(8,128)(2,1)S(1)}, u32[]{:S(2)}, u32[]{:S(2)}) collective-permute-start(bf16[192,512]{1,0:T(8,128)(2,1)S(1)} %slice.235), channel_id=1, source_target_pairs={{0,64},{1,65},{2,66},{3,67},{4,68},{5,69},{6,70},{7,71},{8,72},{9,... | collective-permute-start | bytes 589832 | tf_op jit(solution)/shard_map/ppermute | solution.py:120
  21.9 1.3 collective-permute-start.3
  23.2 1.3 collective-permute-start.1
  24.7 6.5 %collective-permute-done.1 = bf16[256,512]{1,0:T(8,128)(2,1)S(1)} collective-permute-done((bf16[256,512]{1,0:T(8,128)(2,1)S(1)}, bf16[256,512]{1,0:T(8,128)(2,1)S(1)}, u32[]{:S(2)}, u32[]{:S(2)}) %collective-permute-start.1) | collective-permute-done | bytes 262176 | tf_op jit(solution)/shard_map/ppermute | solution.py:118
  31.4 1.0 copy-done.2
  32.7 5.6 %probs.1 = (bf16[4,512,1024]{2,1,0:T(8,128)(2,1)S(1)}, f32[512,512]{1,0:T(8,128)S(1)}) custom-call(bf16[128,4096]{1,0:T(8,128)(2,1)S(1)} %bitcast.43, bf16[512,512]{1,0:T(8,128)(2,1)S(1)} %pad_maximum_fusion.k_ref, bf16[128,4096]{1,0:T(8,128)(2,1)S(1)} %bitcast.45, f32[512,128]{1,0:T(8,128)S(1)} %add_select_fusion.bias_ref), custom_call_target="tpu_custom_call" | custom-call | flops 1073741824 | bytes 8388608 | tf_op jit(solution)/shard_map/probs/pallas_call | solution.py:64
  38.3 2.0 %copy-done = bf16[4,512,1024]{2,1,0:T(8,128)(2,1)} copy-done((bf16[4,512,1024]{2,1,0:T(8,128)(2,1)}, bf16[4,512,1024]{2,1,0:T(8,128)(2,1)S(1)}, u32[]{:S(2)}) %copy-start) | copy-done | bytes 4194328
  40.6 1.3 collective-permute-start.12
  42.6 1.3 collective-permute-start.13
  43.8 1.3 collective-permute-start.14
  45.1 2.4 %copy.13 = bf16[1,128,5120]{1,2,0:T(8,128)(2,1)} copy(bf16[1,128,5120]{2,1,0:T(8,128)(2,1)} %param.22) | data formatting | bytes 2621440 | tf_op args[0]
  47.6 2.5 %copy.14 = bf16[4,128,2,2,320]{1,4,3,2,0:T(8,128)(2,1)} copy(bf16[4,128,2,2,320]{1,4,3,0,2:T(8,128)(2,1)} %bitcast.50) | data formatting | bytes 2621440 | tf_op jit(solution)/shard_map/transpose | solution.py:176
  50.1 2.4 %copy.15 = bf16[4,128,1280]{2,1,0:T(8,128)(2,1)} copy(bf16[4,128,1280]{1,2,0:T(8,128)(2,1)} %bitcast.49) | data formatting | bytes 2621440 | tf_op jit(solution)/shard_map/reshape | solution.py:176
  52.5 4.9 %all-to-all-start.1 = ((bf16[4,128,1280]{2,1,0:T(8,128)(2,1)}), bf16[4,128,1280]{2,1,0:T(8,128)(2,1)}, u32[]{:S(2)}, u32[]{:S(2)}) async-start(bf16[4,128,1280]{2,1,0:T(8,128)(2,1)} %copy.15), calls=%async_computation.1 | async-start | bytes 2621440 | tf_op jit(solution)/shard_map/all_to_all | solution.py:177
  58.6 3.0 %collective-permute-start.15 = (bf16[128,512]{1,0:T(8,128)(2,1)S(1)}, bf16[128,512]{1,0:T(8,128)(2,1)S(1)}, u32[]{:S(2)}, u32[]{:S(2)}) collective-permute-start(bf16[128,512]{1,0:T(8,128)(2,1)S(1)} %select_convert_fusion), channel_id=1, source_target_pairs={{0,16},{16,0},{1,17},{17,1},{2,18},{18,2},{3,19},{19,3},{4,20},{20... | collective-permute-start | bytes 393224 | tf_op jit(solution)/shard_map/ppermute | solution.py:149
  61.6 3.6 %collective-permute-done.15 = bf16[128,512]{1,0:T(8,128)(2,1)S(1)} collective-permute-done((bf16[128,512]{1,0:T(8,128)(2,1)S(1)}, bf16[128,512]{1,0:T(8,128)(2,1)S(1)}, u32[]{:S(2)}, u32[]{:S(2)}) %collective-permute-start.15) | collective-permute-done | bytes 131104 | tf_op jit(solution)/shard_map/ppermute | solution.py:149
  65.5 7.3 %all-to-all-done.1 = bf16[4,128,1280]{2,1,0:T(8,128)(2,1)} async-done(((bf16[4,128,1280]{2,1,0:T(8,128)(2,1)}), bf16[4,128,1280]{2,1,0:T(8,128)(2,1)}, u32[]{:S(2)}, u32[]{:S(2)}) %all-to-all-start.1) | async-done | bytes 1310752 | tf_op jit(solution)/shard_map/all_to_all | solution.py:177
  73.7 4.9 %all-to-all-start = ((bf16[4,128,512]{1,2,0:T(8,128)(2,1)}), bf16[4,128,512]{1,2,0:T(8,128)(2,1)S(1)}, u32[]{:S(2)}, u32[]{:S(2)}) async-start(bf16[4,128,512]{1,2,0:T(8,128)(2,1)} %broadcast_in_dim.54), calls=%async_computation | async-start | bytes 1048576 | tf_op jit(solution)/shard_map/all_to_all | solution.py:182
  78.6 6.6 %all-to-all-done = bf16[4,128,512]{1,2,0:T(8,128)(2,1)S(1)} async-done(((bf16[4,128,512]{1,2,0:T(8,128)(2,1)}), bf16[4,128,512]{1,2,0:T(8,128)(2,1)S(1)}, u32[]{:S(2)}, u32[]{:S(2)}) %all-to-all-start) | async-done | bytes 524320 | tf_op jit(solution)/shard_map/all_to_all | solution.py:182
  85.2 3.7 %convolution_bitcast_fusion = f32[1280,512]{0,1:T(8,128)} fusion(bf16[4,128,512]{1,2,0:T(8,128)(2,1)S(1)} %all-to-all-done, bf16[4,128,1280]{2,1,0:T(8,128)(2,1)} %all-to-all-done.1), kind=kOutput, calls=%fused_computation.2 | convolution fusion | flops 671088640 | bytes 4456448 | tf_op jit(solution)/shard_map/dot_general | solution.py:183
  88.8 3.2 %copy.16 = f32[1280,512]{1,0:T(8,128)} copy(f32[1280,512]{0,1:T(8,128)} %convolution_bitcast_fusion) | data formatting | bytes 5242880 | tf_op jit(solution)/shard_map/dot_general | solution.py:183
  92.1 1.4 fusion.7
  93.6 2.1 %collective-permute-done.16 = bf16[2,320,512]{2,1,0:T(8,128)(2,1)S(1)} collective-permute-done((bf16[2,320,512]{2,1,0:T(8,128)(2,1)S(1)}, bf16[2,320,512]{2,1,0:T(8,128)(2,1)S(1)}, u32[]{:S(2)}, u32[]{:S(2)}) %collective-permute-start.16) | collective-permute-done | bytes 655392 | tf_op jit(solution)/shard_map/ppermute | solution.py:191
  95.6 1.5 fusion.1
  97.2 0.9 copy.17
  98.1 10.5 %all-to-all-start.2 = ((bf16[16,40,512]{2,1,0:T(8,128)(2,1)}), bf16[16,40,512]{2,1,0:T(8,128)(2,1)S(1)}, u32[]{:S(2)}, u32[]{:S(2)}) async-start(bf16[16,40,512]{2,1,0:T(8,128)(2,1)} %bitcast.51), calls=%async_computation.2 | async-start | bytes 1310720 | tf_op jit(solution)/shard_map/all_to_all | solution.py:193
  108.6 3.3 %fusion.4 = bf16[128,512]{1,0:T(8,128)(2,1)S(1)} fusion(bf16[5120,512]{1,0:T(8,128)(2,1)} %all-gather.2.cloned.1.call-done, bf16[1,128,5120]{2,1,0:T(8,128)(2,1)S(1)} %copy-done.5), kind=kOutput, calls=%fused_computation.8 | convolution fusion | flops 671154176 | bytes 6684672 | tf_op jit(solution)/shard_map/dot_general | solution.py:202
  112.0 3.5 %collective-permute-start.4 = (bf16[128,512]{1,0:T(8,128)(2,1)S(1)}, bf16[128,512]{1,0:T(8,128)(2,1)S(1)}, u32[]{:S(2)}, u32[]{:S(2)}) collective-permute-start(bf16[128,512]{1,0:T(8,128)(2,1)S(1)} %fusion.4), channel_id=1, source_target_pairs={{0,16},{16,0},{1,17},{17,1},{2,18},{18,2},{3,19},{19,3},{4,20},{20... | collective-permute-start | bytes 393224 | tf_op jit(solution)/shard_map/ppermute | solution.py:114
  115.5 7.7 %collective-permute-done.4 = bf16[128,512]{1,0:T(8,128)(2,1)S(1)} collective-permute-done((bf16[128,512]{1,0:T(8,128)(2,1)S(1)}, bf16[128,512]{1,0:T(8,128)(2,1)S(1)}, u32[]{:S(2)}, u32[]{:S(2)}) %collective-permute-start.4) | collective-permute-done | bytes 131104 | tf_op jit(solution)/shard_map/ppermute | solution.py:114
  123.3 2.7 %collective-permute-start.5 = (bf16[256,512]{1,0:T(8,128)(2,1)S(1)}, bf16[256,512]{1,0:T(8,128)(2,1)S(1)}, u32[]{:S(2)}, u32[]{:S(2)}) collective-permute-start(bf16[256,512]{1,0:T(8,128)(2,1)S(1)} %maximum_select_fusion.1), channel_id=1, source_target_pairs={{0,32},{32,64},{64,96},{1,33},{33,65},{65,97},{2,34},{34,66},{66,9... | collective-permute-start | bytes 786440 | tf_op jit(solution)/shard_map/ppermute | solution.py:118
  126.0 4.6 %collective-permute-start.6 = (bf16[192,512]{1,0:T(8,128)(2,1)S(1)}, bf16[192,512]{1,0:T(8,128)(2,1)S(1)}, u32[]{:S(2)}, u32[]{:S(2)}) collective-permute-start(bf16[192,512]{1,0:T(8,128)(2,1)S(1)} %slice.239), channel_id=1, source_target_pairs={{0,64},{1,65},{2,66},{3,67},{4,68},{5,69},{6,70},{7,71},{8,72},{9,... | collective-permute-start | bytes 589832 | tf_op jit(solution)/shard_map/ppermute | solution.py:120
  130.5 2.0 %collective-permute-start.7 = (bf16[192,512]{1,0:T(8,128)(2,1)S(1)}, bf16[192,512]{1,0:T(8,128)(2,1)}, u32[]{:S(2)}, u32[]{:S(2)}) collective-permute-start(bf16[192,512]{1,0:T(8,128)(2,1)S(1)} %slice.239), channel_id=1, source_target_pairs={{0,96},{1,97},{2,98},{3,99},{4,100},{5,101},{6,102},{7,103},{8,104... | collective-permute-start | bytes 589832 | tf_op jit(solution)/shard_map/ppermute | solution.py:119
  133.4 3.4 %all-to-all-start.3 = ((bf16[8,40,512]{2,1,0:T(8,128)(2,1)}), bf16[8,40,512]{2,1,0:T(8,128)(2,1)S(1)}, u32[]{:S(2)}, u32[]{:S(2)}) async-start(bf16[8,40,512]{2,1,0:T(8,128)(2,1)} %broadcast_in_dim.55), calls=%async_computation.3 | async-start | bytes 655360 | tf_op jit(solution)/shard_map/all_to_all | solution.py:197
  137.6 1.1 fusion.10
  138.8 2.2 %copy-done.1 = bf16[4,512,1024]{2,1,0:T(8,128)(2,1)S(1)} copy-done((bf16[4,512,1024]{2,1,0:T(8,128)(2,1)S(1)}, bf16[4,512,1024]{2,1,0:T(8,128)(2,1)}, u32[]{:S(2)}) %copy-start.1) | copy-done | bytes 4194328
  141.0 6.0 %scores.1 = (bf16[128,4096]{1,0:T(8,128)(2,1)}, f32[512,512]{1,0:T(8,128)S(1)}) custom-call(bf16[128,4096]{1,0:T(8,128)(2,1)S(1)} %bitcast.44, bf16[512,512]{1,0:T(8,128)(2,1)S(1)} %pad_maximum_fusion.k_ref, bf16[128,4096]{1,0:T(8,128)(2,1)S(1)} %bitcast.46, bf16[512,512]{1,0:T(8,128)(2,1)S(1)} %pad_maximum_fusion.1.v_ref, bf16[4,512,1024]{2,1,0:T(8,128)(2,1)S(1)} %copy-done.1), custom_call_target="tpu_custom_call" | custom-call | flops 1610612736 | bytes 8388608 | tf_op jit(solution)/shard_map/scores/pallas_call | solution.py:90
  147.3 1.3 collective-permute-start.8
  148.6 1.3 collective-permute-start.10
  149.9 1.3 collective-permute-start.9
  151.2 0.9 bitcast_convert_fusion
  152.2 4.4 %collective-permute-done.8 = bf16[256,512]{1,0:T(8,128)(2,1)S(1)} collective-permute-done((bf16[256,512]{1,0:T(8,128)(2,1)S(1)}, bf16[256,512]{1,0:T(8,128)(2,1)S(1)}, u32[]{:S(2)}, u32[]{:S(2)}) %collective-permute-start.8) | collective-permute-done | bytes 262176 | tf_op jit(solution)/shard_map/ppermute | solution.py:142
  156.6 1.6 collective-permute-done.10
  158.3 4.1 %collective-permute-done.9 = bf16[192,512]{1,0:T(8,128)(2,1)S(1)} collective-permute-done((bf16[192,512]{1,0:T(8,128)(2,1)S(1)}, bf16[192,512]{1,0:T(8,128)(2,1)S(1)}, u32[]{:S(2)}, u32[]{:S(2)}) %collective-permute-start.9) | collective-permute-done | bytes 196640 | tf_op jit(solution)/shard_map/ppermute | solution.py:143
  162.7 3.1 %collective-permute-start.11 = (bf16[128,512]{1,0:T(8,128)(2,1)S(1)}, bf16[128,512]{1,0:T(8,128)(2,1)S(1)}, u32[]{:S(2)}, u32[]{:S(2)}) collective-permute-start(bf16[128,512]{1,0:T(8,128)(2,1)S(1)} %select_convert_fusion.1), channel_id=1, source_target_pairs={{0,16},{16,0},{1,17},{17,1},{2,18},{18,2},{3,19},{19,3},{4,20},{20... | collective-permute-start | bytes 393224 | tf_op jit(solution)/shard_map/ppermute | solution.py:149
  165.8 5.3 %fusion = bf16[1,128,5120]{2,1,0:T(8,128)(2,1)} fusion(bf16[128,512]{1,0:T(8,128)(2,1)S(1)} %copy-done.7, bf16[5120,512]{1,0:T(8,128)(2,1)} %all-gather.2.cloned.1.call-done), kind=kOutput, calls=%fused_computation.1 | convolution fusion | flops 671744000 | bytes 6684672 | tf_op jit(solution)/shard_map/dot_general | solution.py:206
  (78 shorter events, 10.2 us)
Async XLA Ops:
  7.2 101.4 %all-gather.2.cloned.1.call-start = ((), (), s32[]{:S(2)}) async-start(), calls=%async_computation.4 | async-start | bytes 5570560 | tf_op jit(solution)/shard_map/all_gather | solution.py:175
  7.9 7.7 %collective-permute-start = (bf16[128,512]{1,0:T(8,128)(2,1)}, bf16[128,512]{1,0:T(8,128)(2,1)S(1)}, u32[]{:S(2)}, u32[]{:S(2)}) collective-permute-start(bf16[128,512]{1,0:T(8,128)(2,1)} %bitcast.53), channel_id=1, source_target_pairs={{0,16},{16,0},{1,17},{17,1},{2,18},{18,2},{3,19},{19,3},{4,20},{20... | collective-permute-start | bytes 393224 | tf_op jit(solution)/shard_map/ppermute | solution.py:114
  16.6 14.7 %copy-start.11 = (bf16[1,128,512]{2,1,0:T(8,128)(2,1)S(1)}, bf16[1,128,512]{2,1,0:T(8,128)(2,1)}, u32[]{:S(2)}) copy-start(bf16[1,128,512]{2,1,0:T(8,128)(2,1)} %param.24) | copy-start | bytes 393220
  16.7 14.5 %collective-permute-start.2 = (bf16[192,512]{1,0:T(8,128)(2,1)S(1)}, bf16[192,512]{1,0:T(8,128)(2,1)S(1)}, u32[]{:S(2)}, u32[]{:S(2)}) collective-permute-start(bf16[192,512]{1,0:T(8,128)(2,1)S(1)} %slice.235), channel_id=1, source_target_pairs={{0,64},{1,65},{2,66},{3,67},{4,68},{5,69},{6,70},{7,71},{8,72},{9,... | collective-permute-start | bytes 589832 | tf_op jit(solution)/shard_map/ppermute | solution.py:120
  21.9 9.3 %collective-permute-start.3 = (bf16[192,512]{1,0:T(8,128)(2,1)S(1)}, bf16[192,512]{1,0:T(8,128)(2,1)S(1)}, u32[]{:S(2)}, u32[]{:S(2)}) collective-permute-start(bf16[192,512]{1,0:T(8,128)(2,1)S(1)} %slice.235), channel_id=1, source_target_pairs={{0,96},{1,97},{2,98},{3,99},{4,100},{5,101},{6,102},{7,103},{8,104... | collective-permute-start | bytes 589832 | tf_op jit(solution)/shard_map/ppermute | solution.py:119
  23.2 7.9 %collective-permute-start.1 = (bf16[256,512]{1,0:T(8,128)(2,1)S(1)}, bf16[256,512]{1,0:T(8,128)(2,1)S(1)}, u32[]{:S(2)}, u32[]{:S(2)}) collective-permute-start(bf16[256,512]{1,0:T(8,128)(2,1)S(1)} %maximum_select_fusion), channel_id=1, source_target_pairs={{0,32},{32,64},{64,96},{1,33},{33,65},{65,97},{2,34},{34,66},{66,9... | collective-permute-start | bytes 786440 | tf_op jit(solution)/shard_map/ppermute | solution.py:118
  31.1 1.2 copy-start.2
  31.1 1.6 copy-start.3
  38.3 2.0 %copy-start = (bf16[4,512,1024]{2,1,0:T(8,128)(2,1)}, bf16[4,512,1024]{2,1,0:T(8,128)(2,1)S(1)}, u32[]{:S(2)}) copy-start(bf16[4,512,1024]{2,1,0:T(8,128)(2,1)S(1)} %get-tuple-element.104.p_ref) | copy-start | bytes 12582916
  40.6 16.8 %collective-permute-start.12 = (bf16[256,512]{1,0:T(8,128)(2,1)S(1)}, bf16[256,512]{1,0:T(8,128)(2,1)S(1)}, u32[]{:S(2)}, u32[]{:S(2)}) collective-permute-start(bf16[256,512]{1,0:T(8,128)(2,1)S(1)} %convert_element_type.88), channel_id=1, source_target_pairs={{32,0},{64,32},{96,64},{33,1},{65,33},{97,65},{34,2},{66,34},{98,6... | collective-permute-start | bytes 786440 | tf_op jit(solution)/shard_map/ppermute | solution.py:142
  42.6 15.7 %collective-permute-start.13 = (bf16[192,512]{1,0:T(8,128)(2,1)}, bf16[192,512]{1,0:T(8,128)(2,1)S(1)}, u32[]{:S(2)}, u32[]{:S(2)}) collective-permute-start(bf16[192,512]{1,0:T(8,128)(2,1)} %slice.294), channel_id=1, source_target_pairs={{96,0},{97,1},{98,2},{99,3},{100,4},{101,5},{102,6},{103,7},{104,8... | collective-permute-start | bytes 589832 | tf_op jit(solution)/shard_map/ppermute | solution.py:143
  43.8 14.4 %collective-permute-start.14 = (bf16[192,512]{1,0:T(8,128)(2,1)}, bf16[192,512]{1,0:T(8,128)(2,1)S(1)}, u32[]{:S(2)}, u32[]{:S(2)}) collective-permute-start(bf16[192,512]{1,0:T(8,128)(2,1)} %slice.294), channel_id=1, source_target_pairs={{64,0},{65,1},{66,2},{67,3},{68,4},{69,5},{70,6},{71,7},{72,8},{73... | collective-permute-start | bytes 589832 | tf_op jit(solution)/shard_map/ppermute | solution.py:144
  52.5 20.3 %all-to-all-start.1 = ((bf16[4,128,1280]{2,1,0:T(8,128)(2,1)}), bf16[4,128,1280]{2,1,0:T(8,128)(2,1)}, u32[]{:S(2)}, u32[]{:S(2)}) async-start(bf16[4,128,1280]{2,1,0:T(8,128)(2,1)} %copy.15), calls=%async_computation.1 | async-start | bytes 2621440 | tf_op jit(solution)/shard_map/all_to_all | solution.py:177
  58.6 6.6 %collective-permute-start.15 = (bf16[128,512]{1,0:T(8,128)(2,1)S(1)}, bf16[128,512]{1,0:T(8,128)(2,1)S(1)}, u32[]{:S(2)}, u32[]{:S(2)}) collective-permute-start(bf16[128,512]{1,0:T(8,128)(2,1)S(1)} %select_convert_fusion), channel_id=1, source_target_pairs={{0,16},{16,0},{1,17},{17,1},{2,18},{18,2},{3,19},{19,3},{4,20},{20... | collective-permute-start | bytes 393224 | tf_op jit(solution)/shard_map/ppermute | solution.py:149
  65.4 23.5 %copy-start.6 = (bf16[128,512]{1,0:T(8,128)(2,1)}, bf16[128,512]{1,0:T(8,128)(2,1)S(1)}, u32[]{:S(2)}) copy-start(bf16[128,512]{1,0:T(8,128)(2,1)S(1)} %add_convert_fusion) | copy-start | bytes 393220
  73.7 11.5 %all-to-all-start = ((bf16[4,128,512]{1,2,0:T(8,128)(2,1)}), bf16[4,128,512]{1,2,0:T(8,128)(2,1)S(1)}, u32[]{:S(2)}, u32[]{:S(2)}) async-start(bf16[4,128,512]{1,2,0:T(8,128)(2,1)} %broadcast_in_dim.54), calls=%async_computation | async-start | bytes 1048576 | tf_op jit(solution)/shard_map/all_to_all | solution.py:182
  93.5 2.2 %collective-permute-start.16 = (bf16[2,320,512]{2,1,0:T(8,128)(2,1)S(1)}, bf16[2,320,512]{2,1,0:T(8,128)(2,1)S(1)}, u32[]{:S(2)}, u32[]{:S(2)}) collective-permute-start(bf16[2,320,512]{2,1,0:T(8,128)(2,1)S(1)} %fusion.7), channel_id=1, source_target_pairs={{0,1},{1,0},{2,3},{3,2},{4,5},{5,4},{6,7},{7,6},{8,9},{9,8},{10,11... | collective-permute-start | bytes 1966088 | tf_op jit(solution)/shard_map/ppermute | solution.py:191
  97.2 11.5 %copy-start.5 = (bf16[1,128,5120]{2,1,0:T(8,128)(2,1)S(1)}, bf16[1,128,5120]{2,1,0:T(8,128)(2,1)}, u32[]{:S(2)}) copy-start(bf16[1,128,5120]{2,1,0:T(8,128)(2,1)} %param.22) | copy-start | bytes 3932164
  98.1 34.4 %all-to-all-start.2 = ((bf16[16,40,512]{2,1,0:T(8,128)(2,1)}), bf16[16,40,512]{2,1,0:T(8,128)(2,1)S(1)}, u32[]{:S(2)}, u32[]{:S(2)}) async-start(bf16[16,40,512]{2,1,0:T(8,128)(2,1)} %bitcast.51), calls=%async_computation.2 | async-start | bytes 1310720 | tf_op jit(solution)/shard_map/all_to_all | solution.py:193
  112.0 18.6 %copy-start.8 = (bf16[128,512]{1,0:T(8,128)(2,1)}, bf16[128,512]{1,0:T(8,128)(2,1)S(1)}, u32[]{:S(2)}) copy-start(bf16[128,512]{1,0:T(8,128)(2,1)S(1)} %fusion.4) | copy-start | bytes 393220
  112.0 11.2 %collective-permute-start.4 = (bf16[128,512]{1,0:T(8,128)(2,1)S(1)}, bf16[128,512]{1,0:T(8,128)(2,1)S(1)}, u32[]{:S(2)}, u32[]{:S(2)}) collective-permute-start(bf16[128,512]{1,0:T(8,128)(2,1)S(1)} %fusion.4), channel_id=1, source_target_pairs={{0,16},{16,0},{1,17},{17,1},{2,18},{18,2},{3,19},{19,3},{4,20},{20... | collective-permute-start | bytes 393224 | tf_op jit(solution)/shard_map/ppermute | solution.py:114
  123.2 9.3 %copy-start.10 = (bf16[128,512]{1,0:T(8,128)(2,1)}, bf16[128,512]{1,0:T(8,128)(2,1)S(1)}, u32[]{:S(2)}) copy-start(bf16[128,512]{1,0:T(8,128)(2,1)S(1)} %collective-permute-done.4) | copy-start | bytes 393220
  123.3 13.5 %collective-permute-start.5 = (bf16[256,512]{1,0:T(8,128)(2,1)S(1)}, bf16[256,512]{1,0:T(8,128)(2,1)S(1)}, u32[]{:S(2)}, u32[]{:S(2)}) collective-permute-start(bf16[256,512]{1,0:T(8,128)(2,1)S(1)} %maximum_select_fusion.1), channel_id=1, source_target_pairs={{0,32},{32,64},{64,96},{1,33},{33,65},{65,97},{2,34},{34,66},{66,9... | collective-permute-start | bytes 786440 | tf_op jit(solution)/shard_map/ppermute | solution.py:118
  126.0 10.9 %collective-permute-start.6 = (bf16[192,512]{1,0:T(8,128)(2,1)S(1)}, bf16[192,512]{1,0:T(8,128)(2,1)S(1)}, u32[]{:S(2)}, u32[]{:S(2)}) collective-permute-start(bf16[192,512]{1,0:T(8,128)(2,1)S(1)} %slice.239), channel_id=1, source_target_pairs={{0,64},{1,65},{2,66},{3,67},{4,68},{5,69},{6,70},{7,71},{8,72},{9,... | collective-permute-start | bytes 589832 | tf_op jit(solution)/shard_map/ppermute | solution.py:120
  130.5 7.0 %collective-permute-start.7 = (bf16[192,512]{1,0:T(8,128)(2,1)S(1)}, bf16[192,512]{1,0:T(8,128)(2,1)}, u32[]{:S(2)}, u32[]{:S(2)}) collective-permute-start(bf16[192,512]{1,0:T(8,128)(2,1)S(1)} %slice.239), channel_id=1, source_target_pairs={{0,96},{1,97},{2,98},{3,99},{4,100},{5,101},{6,102},{7,103},{8,104... | collective-permute-start | bytes 589832 | tf_op jit(solution)/shard_map/ppermute | solution.py:119
  132.6 6.1 %copy-start.9 = (bf16[128,512]{1,0:T(8,128)(2,1)S(1)}, bf16[128,512]{1,0:T(8,128)(2,1)}, u32[]{:S(2)}) copy-start(bf16[128,512]{1,0:T(8,128)(2,1)} %copy-done.8) | copy-start | bytes 393220
  133.4 17.8 %all-to-all-start.3 = ((bf16[8,40,512]{2,1,0:T(8,128)(2,1)}), bf16[8,40,512]{2,1,0:T(8,128)(2,1)S(1)}, u32[]{:S(2)}, u32[]{:S(2)}) async-start(bf16[8,40,512]{2,1,0:T(8,128)(2,1)} %broadcast_in_dim.55), calls=%async_computation.3 | async-start | bytes 655360 | tf_op jit(solution)/shard_map/all_to_all | solution.py:197
  136.8 1.9 %copy-start.4 = (bf16[1,128,4096]{2,1,0:T(8,128)(2,1)S(1)}, bf16[1,128,4096]{2,1,0:T(8,128)(2,1)}, u32[]{:S(2)}) copy-start(bf16[1,128,4096]{2,1,0:T(8,128)(2,1)} %param.26) | copy-start | bytes 3145732
  136.9 0.7 copy-start.12
  138.8 2.2 %copy-start.1 = (bf16[4,512,1024]{2,1,0:T(8,128)(2,1)S(1)}, bf16[4,512,1024]{2,1,0:T(8,128)(2,1)}, u32[]{:S(2)}) copy-start(bf16[4,512,1024]{2,1,0:T(8,128)(2,1)} %copy-done) | copy-start | bytes 12582916
  147.3 9.3 %collective-permute-start.8 = (bf16[256,512]{1,0:T(8,128)(2,1)S(1)}, bf16[256,512]{1,0:T(8,128)(2,1)S(1)}, u32[]{:S(2)}, u32[]{:S(2)}) collective-permute-start(bf16[256,512]{1,0:T(8,128)(2,1)S(1)} %convert_element_type.79), channel_id=1, source_target_pairs={{32,0},{64,32},{96,64},{33,1},{65,33},{97,65},{34,2},{66,34},{98,6... | collective-permute-start | bytes 786440 | tf_op jit(solution)/shard_map/ppermute | solution.py:142
  148.6 9.7 %collective-permute-start.10 = (bf16[192,512]{1,0:T(8,128)(2,1)S(1)}, bf16[192,512]{1,0:T(8,128)(2,1)S(1)}, u32[]{:S(2)}, u32[]{:S(2)}) collective-permute-start(bf16[192,512]{1,0:T(8,128)(2,1)S(1)} %slice.295), channel_id=1, source_target_pairs={{64,0},{65,1},{66,2},{67,3},{68,4},{69,5},{70,6},{71,7},{72,8},{73... | collective-permute-start | bytes 589832 | tf_op jit(solution)/shard_map/ppermute | solution.py:144
  149.9 12.5 %collective-permute-start.9 = (bf16[192,512]{1,0:T(8,128)(2,1)S(1)}, bf16[192,512]{1,0:T(8,128)(2,1)S(1)}, u32[]{:S(2)}, u32[]{:S(2)}) collective-permute-start(bf16[192,512]{1,0:T(8,128)(2,1)S(1)} %slice.295), channel_id=1, source_target_pairs={{96,0},{97,1},{98,2},{99,3},{100,4},{101,5},{102,6},{103,7},{104,8... | collective-permute-start | bytes 589832 | tf_op jit(solution)/shard_map/ppermute | solution.py:143
  156.6 9.1 %copy-start.7 = (bf16[128,512]{1,0:T(8,128)(2,1)S(1)}, bf16[128,512]{1,0:T(8,128)(2,1)}, u32[]{:S(2)}) copy-start(bf16[128,512]{1,0:T(8,128)(2,1)} %copy-done.6) | copy-start | bytes 393220
  162.7 8.4 %collective-permute-start.11 = (bf16[128,512]{1,0:T(8,128)(2,1)S(1)}, bf16[128,512]{1,0:T(8,128)(2,1)S(1)}, u32[]{:S(2)}, u32[]{:S(2)}) collective-permute-start(bf16[128,512]{1,0:T(8,128)(2,1)S(1)} %select_convert_fusion.1), channel_id=1, source_target_pairs={{0,16},{16,0},{1,17},{17,1},{2,18},{18,2},{3,19},{19,3},{4,20},{20... | collective-permute-start | bytes 393224 | tf_op jit(solution)/shard_map/ppermute | solution.py:149
Sparse Core Ops, SparseCore 0:
  9.7 40.9 all-gather.1

commit v2 on v1

--- a/solution.py
+++ b/solution.py
@@ -78,7 +78,7 @@
             jax.ShapeDtypeStruct((KEY_HEADS, SLOTS, GROUP * ROWS), BF),
             jax.ShapeDtypeStruct((SLOTS, KEY_HEADS * HEAD), F32),
         ],
-        compiler_params=pltpu.CompilerParams(vmem_limit_bytes=40 << 20),
+        compiler_params=pltpu.CompilerParams(vmem_limit_bytes=24 << 20),
         cost_estimate=pl.CostEstimate(
             flops=4 * SLOTS * ROWS * 32 * HEAD, bytes_accessed=8 << 20, transcendentals=SLOTS * ROWS * 32
         ),
@@ -102,52 +102,12 @@
             jax.ShapeDtypeStruct((ROWS, KEY_HEADS * GROUP * HEAD), BF),
             jax.ShapeDtypeStruct((SLOTS, KEY_HEADS * HEAD), F32),
         ],
-        compiler_params=pltpu.CompilerParams(vmem_limit_bytes=40 << 20),
+        compiler_params=pltpu.CompilerParams(vmem_limit_bytes=24 << 20),
         cost_estimate=pl.CostEstimate(
             flops=6 * SLOTS * ROWS * 32 * HEAD, bytes_accessed=8 << 20, transcendentals=0
         ),
         name="scores",
     )(q, k, g, v, p)
-
-
-def spread(block, y, zh):
-    other = lax.ppermute(block, "zh", SWAP)
-    pair = jnp.where(
-        zh == 0, jnp.concatenate([block, other]), jnp.concatenate([other, block])
-    )
-    before = lax.ppermute(pair, "y", ((0, 1), (1, 2), (2, 3)))
-    to_last = lax.ppermute(pair[:BACK], "y", ((0, 3),))
-    to_third = lax.ppermute(pair[:BACK], "y", ((0, 2),))
-    header = jnp.where(
-        y == 0,
-        pair[:BACK],
-        jnp.where(y == 1, before[:BACK], jnp.where(y == 2, to_third, to_last)),
-    )
-    window = jnp.where(
-        zh == 0, before[2 * ROWS - BACK :], jnp.concatenate([before[BACK:], other])
-    )
-    return jnp.concatenate([header, window, block])
-
-
-def collected(slots, y, zh):
-    header, window, own = slots[:BACK], slots[BACK : 2 * BACK], slots[2 * BACK :]
-    tail = 2 * ROWS - BACK
-    zeros = jnp.zeros((2 * ROWS, slots.shape[1]), F32)
-    before = jnp.where(
-        zh == 0,
-        zeros.at[tail:].set(window),
-        zeros.at[BACK:].set(window[:tail]),
-    ) + jnp.where(y == 1, zeros.at[:BACK].set(header), 0.0)
-    half_header = header.astype(BF)
-    from_next = lax.ppermute(before.astype(BF), "y", ((1, 0), (2, 1), (3, 2)))
-    from_last = lax.ppermute(half_header, "y", ((3, 0),))
-    from_third = lax.ppermute(half_header, "y", ((2, 0),))
-    first = header + from_last.astype(F32) + from_third.astype(F32)
-    pair = from_next.astype(F32) + jnp.where(y == 0, zeros.at[:BACK].set(first), 0.0)
-    low, high = pair[:ROWS], pair[ROWS:]
-    low = low + jnp.where(zh == 1, window[tail:], 0.0)
-    sent = lax.ppermute(jnp.where(zh == 0, high, low).astype(BF), "zh", SWAP)
-    return own + jnp.where(zh == 0, low, high) + sent.astype(F32)
 
 
 def slot_bias(passages, s):
@@ -165,47 +125,170 @@
     return jnp.where(jnp.concatenate([head_ok, near_ok]), 0.0, -1e30).astype(F32)
 
 
+def turned(count, step):
+    return tuple((i, (i + step) % count) for i in range(count))
+
+
+def block_at(array, index):
+    return lax.dynamic_index_in_dim(array, index, 0, keepdims=False)
+
+
+def after(value, *others):
+    return lax.optimization_barrier((value,) + others)[0]
+
+
+def paired(block, zh):
+    other = lax.ppermute(block, "zh", SWAP)
+    pair = jnp.where(
+        zh == 0, jnp.concatenate([block, other]), jnp.concatenate([other, block])
+    )
+    return other, pair
+
+
+def spread(block, other, pair, y, zh):
+    before = lax.ppermute(pair, "y", turned(4, 1))
+    to_third = lax.ppermute(pair[:BACK], "y", turned(4, 2))
+    to_last = lax.ppermute(pair[:BACK], "y", turned(4, 3))
+    header = jnp.where(
+        y == 0,
+        pair[:BACK],
+        jnp.where(y == 1, before[:BACK], jnp.where(y == 2, to_third, to_last)),
+    )
+    window = jnp.where(
+        zh == 0, before[2 * ROWS - BACK :], jnp.concatenate([before[BACK:], other])
+    )
+    return jnp.concatenate([header, window, block])
+
+
+def parted(slots, y, zh):
+    header, window = slots[:BACK], slots[BACK : 2 * BACK]
+    tail = 2 * ROWS - BACK
+    zeros = jnp.zeros((2 * ROWS, slots.shape[1]), F32)
+    before = jnp.where(
+        zh == 0,
+        zeros.at[tail:].set(window),
+        zeros.at[BACK:].set(window[:tail]),
+    ) + jnp.where(y == 1, zeros.at[:BACK].set(header), 0.0)
+    return before.astype(BF), header.astype(BF)
+
+
+def collected(slots, before, half_header, y, zh):
+    header, window, own = slots[:BACK], slots[BACK : 2 * BACK], slots[2 * BACK :]
+    tail = 2 * ROWS - BACK
+    zeros = jnp.zeros((2 * ROWS, slots.shape[1]), F32)
+    from_next = lax.ppermute(before, "y", turned(4, 3))
+    from_last = lax.ppermute(half_header, "y", turned(4, 1))
+    from_third = lax.ppermute(half_header, "y", turned(4, 2))
+    first = header + from_last.astype(F32) + from_third.astype(F32)
+    pair = from_next.astype(F32) + jnp.where(y == 0, zeros.at[:BACK].set(first), 0.0)
+    low, high = pair[:ROWS], pair[ROWS:]
+    low = low + jnp.where(zh == 1, window[tail:], 0.0)
+    sent = lax.ppermute(jnp.where(zh == 0, high, low).astype(BF), "zh", SWAP)
+    return own + jnp.where(zh == 0, low, high) + sent.astype(F32)
+
+
 def on_device(hidden_in, queries, saved_keys, value_matrix, output_gradient, passage_index):
-    y, zh, c = lax.axis_index("y"), lax.axis_index("zh"), lax.axis_index("c")
-    s = lax.axis_index(SEQ)
+    y, zh, zl = lax.axis_index("y"), lax.axis_index("zh"), lax.axis_index("zl")
+    x, c = lax.axis_index("x"), lax.axis_index("c")
+    z, s = lax.axis_index(("zh", "zl")), lax.axis_index(SEQ)
     hidden, q, k, g = hidden_in[0], queries[0], saved_keys[0], output_gradient[0]
-    width = hidden.shape[1]
-    kv = k.shape[1]
-    each = width // 16
-    weight = lax.all_gather(value_matrix, FSDP, axis=0, tiled=True)
-    by_x = hidden.reshape(ROWS, 2, 4, 2, each).transpose(2, 0, 1, 3, 4).reshape(4, ROWS, 4 * each)
-    crossed = lax.all_to_all(by_x, "x", 0, 0)
+    width, kv = hidden.shape[1], k.shape[1]
+    each, half = width // 16, width // 2
+    two = 2 * each
+
+    k_other, k_pair = paired(k, zh)
+    k_slots = spread(k, k_other, k_pair, y, zh)
+
+    by_x = jnp.stack(
+        [
+            jnp.concatenate(
+                [hidden[:, i * two : (i + 1) * two], hidden[:, half + i * two : half + (i + 1) * two]],
+                axis=1,
+            )
+            for i in range(4)
+        ]
+    )
+    crossed = lax.all_to_all(by_x, "x", 0, 0).reshape(4 * ROWS, 4 * each)
+    across = lax.ppermute(value_matrix, "zl", SWAP)
+    planes = jnp.where(
+        zl == 0, jnp.stack([value_matrix, across]), jnp.stack([across, value_matrix])
+    )
+    sibling = lax.ppermute(planes, "c", SWAP)
+    weight = jnp.where(
+        c == 0, jnp.stack([planes, sibling], 1), jnp.stack([sibling, planes], 1)
+    ).reshape(4 * each, kv)
+
     bias = slot_bias(passage_index[0], s)
-    k_slots = spread(k, y, zh)
     probs, dv_slots = probs_call(q, k_slots, g, bias)
-    value_grad = collected(dv_slots, y, zh).astype(BF)
-    gathered = lax.all_to_all(jnp.broadcast_to(value_grad[None], (4, ROWS, kv)), "x", 0, 0)
+    dv_slots = after(dv_slots, crossed)
+    dv_before, dv_header = parted(dv_slots, y, zh)
+
+    part = jnp.dot(
+        after(crossed, dv_before, dv_header), weight, preferred_element_type=F32
+    ).reshape(4, ROWS, kv)
+    values = block_at(part, x)
+    for step in (1, 2, 3):
+        sent = block_at(part, (x + step) % 4).astype(BF)
+        values = values + lax.ppermute(sent, "x", turned(4, step)).astype(F32)
+    values = values.astype(BF)
+    v_other, v_pair = paired(values, zh)
+
+    value_grad = collected(dv_slots, dv_before, dv_header, y, zh).astype(BF)
+
+    v_slots = spread(values, v_other, after(v_pair, value_grad), y, zh)
+
+    near = [value_grad] + [lax.ppermute(value_grad, "x", turned(4, n)) for n in (1, 2, 3)]
+    gathered = jnp.concatenate(
+        [
+            jnp.where(
+                x == i,
+                near[0],
+                jnp.where(
+                    x == (i + 1) % 4, near[1], jnp.where(x == (i + 2) % 4, near[2], near[3])
+                ),
+            )
+            for i in range(4)
+        ]
+    )
     term = lax.dot_general(
-        crossed.reshape(4 * ROWS, 4 * each),
-        gathered.reshape(4 * ROWS, kv),
-        (((0,), (0,)), ((), ())),
-        preferred_element_type=F32,
+        crossed, gathered, (((0,), (0,)), ((), ())), preferred_element_type=F32
     ).reshape(2, 2, each, kv)
     kept = lax.dynamic_index_in_dim(term, c, 1, keepdims=False)
     given = lax.dynamic_index_in_dim(term, 1 - c, 1, keepdims=False).astype(BF)
+    back = lax.dot_general(
+        gathered, weight, (((1,), (1,)), ((), ())), preferred_element_type=F32
+    ).astype(BF)
+
     term = kept + lax.ppermute(given, "c", SWAP).astype(F32)
-    pieces = term.astype(BF).reshape(2, 8, each // 8, kv).transpose(1, 0, 2, 3)
-    pieces = lax.all_to_all(
-        pieces.reshape(16, each // 8, kv), ("y", "zh", "zl"), 0, 0
-    )
-    piece = jnp.sum(pieces.astype(F32), axis=0).astype(BF)
-    grad_weight = lax.all_to_all(
-        jnp.broadcast_to(piece[None], (8,) + piece.shape), SEQ, 0, 0
-    )
-    grad_weight = grad_weight.reshape(each, kv).astype(F32)
-
-    values = jnp.dot(hidden, weight, preferred_element_type=F32).astype(BF)
-    v_slots = spread(values, y, zh)
+    term = term.reshape(2, 2, each // 2, kv)
+
+    def quarter(at):
+        return lax.dynamic_slice(term, (at % 2, at // 2, 0, 0), (1, 1, each // 2, kv))[0, 0]
+
+    own_quarter = quarter(z)
+    quarters = [quarter((z + step) % 4).astype(BF) for step in (1, 2, 3)]
+
+    v_slots = after(v_slots, back, *quarters)
     dq, dk_slots = scores_call(q, k_slots, g, v_slots, probs)
-    key_grad = collected(dk_slots, y, zh).astype(BF)
-    grad_input = lax.dot_general(
-        value_grad, weight, (((1,), (1,)), ((), ())), preferred_element_type=F32
-    ).astype(BF)
+    dk_before, dk_header = parted(dk_slots, y, zh)
+
+    total = own_quarter
+    for step, sent in zip((1, 2, 3), quarters):
+        total = total + lax.ppermute(sent, ("zh", "zl"), turned(4, step)).astype(F32)
+    mine = total.astype(BF)
+    first, second, third = (lax.ppermute(mine, "y", turned(4, n)).astype(F32) for n in (1, 2, 3))
+    total = ((mine.astype(F32) + second) + (first + third)).astype(BF)
+    other = lax.ppermute(total, "zh", SWAP)
+    grad_weight = jnp.where(
+        zh == 0, jnp.concatenate([total, other]), jnp.concatenate([other, total])
+    ).astype(F32)
+
+    back = lax.all_to_all(back.reshape(4, ROWS, 4 * each), "x", 0, 0)
+    grad_input = jnp.concatenate(
+        [back[i][:, p * two : (p + 1) * two] for p in range(2) for i in range(4)], axis=1
+    )
+
+    key_grad = collected(dk_slots, dk_before, dk_header, y, zh).astype(BF)
     return dq[None], key_grad[None], grad_input[None], grad_weight
 
 

time: 182 us -> 123 us (0.68); the launches traced: 179 us -> 122 us
  waiting for transfers between devices: 47 us -> 19.4 us
  between operations: 14.6 us -> 1.28 us
  local copies, waits for them, and re-layouts: 22.3 us -> 12.5 us
  matrix products: 12.3 us -> 5.39 us
  other arithmetic: 8.84 us -> 13.6 us
  starting transfers between devices: 62.1 us -> 58.6 us
    all_to_all x4 -> x2, waiting for transfers between devices: 13.9 us -> 0.01 us  [the longest x1 0.01 us: on_device(): crossed = lax.all_to_all(by_x, 'x', 0, 0).reshape(4 * ROWS, 4 * each)]
    all_to_all x4 -> x2, starting transfers between devices: 23.7 us -> 11 us  [the longest x1 6.03 us: on_device(): back = lax.all_to_all(back.reshape(4, ROWS, 4 * each), 'x', 0, 0)]
    ppermute x14 -> x29, starting transfers between devices: 32.2 us -> 43.3 us  [the longest x2 5.74 us: spread(): to_third = lax.ppermute(pair[:BACK], 'y', turned(4, 2))]
    ppermute x14 -> x29, waiting for transfers between devices: 26.7 us -> 17.3 us  [the longest x2 4.49 us: spread(): to_third = lax.ppermute(pair[:BACK], 'y', turned(4, 2))]
    dot_general x3, matrix products: 12.3 us -> 5.39 us  [the longest x1 2.63 us: on_device(): jnp.dot(after(crossed, dv_before, dv_header), weight, preferred_element_t...]
    transpose x2 -> x0, local copies, waits for them, and re-layouts: 3.4 us -> none  [the longest x1 2.51 us: on_device(): hidden.reshape(ROWS, 2, 4, 2, each).transpose(2, 0, 1, 3, 4)]
    dot_general x1 -> x0, local copies, waits for them, and re-layouts: 3.21 us -> none  [on_device(): lax.dot_general(crossed.reshape(4 * ROWS, 4 * each), gathered.reshape(4 *...]
    select_n x4 -> x8, other arithmetic: 1.2 us -> 4 us  [the longest x1 1.59 us: on_device(): jnp.where(c == 0, jnp.stack([planes, sibling], 1), jnp.stack([sibling, pl...]
  transfers between devices with their start and end apart: 22 -> 34, of which waited for: 11 -> 11; matrix products, arithmetic and copies ran while one was open for 20% -> 19% of each run, Pallas kernels for 6% -> 9%
where the time goes in v2:
time: 123 us; the launch traced here: 122 us
  starting transfers between devices  58.6 us (48%)
  waiting for transfers between devices  19.4 us (16%)
  other arithmetic  13.6 us (11%)
  local copies, waits for them, and re-layouts  12.5 us (10%)
  Pallas kernels  11.6 us (9%)
  matrix products  5.39 us (4%)
  between operations  1.28 us (1%)
    unnamed x37, local copies, waits for them, and re-layouts  6.98 us
    pallas_call x1, Pallas kernels, scores_call(): pl.pallas_call(scores_kernel, grid=(KEY_HEADS,), in_specs=[column(ROWS, G...  6.05 us
    all_to_all x1, starting transfers between devices, on_device(): back = lax.all_to_all(back.reshape(4, ROWS, 4 * each), 'x', 0, 0)  6.03 us
    ppermute x2, starting transfers between devices, spread(): to_third = lax.ppermute(pair[:BACK], 'y', turned(4, 2))  5.74 us
    pallas_call x1, Pallas kernels, probs_call(): pl.pallas_call(probs_kernel, grid=(KEY_HEADS,), in_specs=[column(ROWS, GR...  5.57 us
    ppermute x2, starting transfers between devices, paired(): other = lax.ppermute(block, 'zh', SWAP)  5.19 us
    all_to_all x1, starting transfers between devices, on_device(): crossed = lax.all_to_all(by_x, 'x', 0, 0).reshape(4 * ROWS, 4 * each)  4.96 us
    ppermute x3, starting transfers between devices, on_device(): lax.ppermute(value_grad, 'x', turned(4, n))  4.93 us
  transfers between devices with their start and end apart: 34, of which 11 were waited for; matrix products, arithmetic and copies ran while one was open for 19% of the time, Pallas kernels for 9%

profile of v2, /device:TPU:2, one launch (start us, length us, event | category | flops | bytes accessed | tf_op | source)
XLA Modules:
  0.0 122.5 jit_solution(7938013452516885926)
XLA Ops:
  0.6 4.0 %collective-permute-start = (bf16[128,512]{1,0:T(8,128)(2,1)}, bf16[128,512]{1,0:T(8,128)(2,1)S(1)}, u32[]{:S(2)}, u32[]{:S(2)}) collective-permute-start(bf16[128,512]{1,0:T(8,128)(2,1)} %bitcast.97), channel_id=1, source_target_pairs={{0,16},{16,0},{1,17},{17,1},{2,18},{18,2},{3,19},{19,3},{4,20},{20... | collective-permute-start | bytes 393224 | tf_op jit(solution)/shard_map/ppermute | solution.py:141
  4.6 1.5 %fusion.25 = (bf16[128,640]{1,0:T(8,128)(2,1)S(1)}, bf16[128,640]{1,0:T(8,128)(2,1)S(1)}, bf16[128,640]{1,0:T(8,128)(2,1)S(1)}, bf16[128,640]{1,0:T(8,128)(2,1)S...) fusion(bf16[128,5120]{1,0:T(8,128)(2,1)} %bitcast.89), kind=kLoop, calls=%fused_computation.96 | loop fusion | bytes 2621440 | tf_op jit(solution)/shard_map/slice | solution.py:205
  6.2 1.2 pad_maximum_fusion
  7.4 5.0 %all-to-all-start = ((bf16[4,128,1280]{2,1,0:T(8,128)(2,1)}), bf16[4,128,1280]{2,1,0:T(8,128)(2,1)}, u32[]{:S(2)}, u32[]{:S(2)}) async-start(bf16[4,128,1280]{2,1,0:T(8,128)(2,1)} %pad_maximum_fusion), calls=%async_computation | async-start | bytes 2621440 | tf_op jit(solution)/shard_map/all_to_all | solution.py:211
  14.0 1.6 %collective-permute-start.1 = (bf16[256,512]{1,0:T(8,128)(2,1)S(1)}, bf16[256,512]{1,0:T(8,128)(2,1)S(1)}, u32[]{:S(2)}, u32[]{:S(2)}) collective-permute-start(bf16[256,512]{1,0:T(8,128)(2,1)S(1)} %maximum_select_fusion.4), channel_id=1, source_target_pairs={{0,32},{32,64},{64,96},{96,0},{1,33},{33,65},{65,97},{97,1},{2,34}... | collective-permute-start | bytes 786440 | tf_op jit(solution)/shard_map/ppermute | solution.py:149
  15.7 3.0 %collective-permute-start.2 = (bf16[192,512]{1,0:T(8,128)(2,1)S(1)}, bf16[192,512]{1,0:T(8,128)(2,1)S(1)}, u32[]{:S(2)}, u32[]{:S(2)}) collective-permute-start(bf16[192,512]{1,0:T(8,128)(2,1)S(1)} %slice.323), channel_id=1, source_target_pairs={{0,64},{32,96},{64,0},{96,32},{1,65},{33,97},{65,1},{97,33},{2,66}... | collective-permute-start | bytes 589832 | tf_op jit(solution)/shard_map/ppermute | solution.py:150
  18.7 1.3 %collective-permute-start.3 = (bf16[192,512]{1,0:T(8,128)(2,1)S(1)}, bf16[192,512]{1,0:T(8,128)(2,1)S(1)}, u32[]{:S(2)}, u32[]{:S(2)}) collective-permute-start(bf16[192,512]{1,0:T(8,128)(2,1)S(1)} %slice.323), channel_id=1, source_target_pairs={{0,96},{32,0},{64,32},{96,64},{1,97},{33,1},{65,33},{97,65},{2,98}... | collective-permute-start | bytes 589832 | tf_op jit(solution)/shard_map/ppermute | solution.py:151
  20.1 1.2 collective-permute-done.4
  22.3 1.0 collective-permute-done.1
  23.4 4.5 %collective-permute-done.2 = bf16[192,512]{1,0:T(8,128)(2,1)S(1)} collective-permute-done((bf16[192,512]{1,0:T(8,128)(2,1)S(1)}, bf16[192,512]{1,0:T(8,128)(2,1)S(1)}, u32[]{:S(2)}, u32[]{:S(2)}) %collective-permute-start.2) | collective-permute-done | bytes 196640 | tf_op jit(solution)/shard_map/ppermute | solution.py:150
  28.1 5.6 %probs.1 = (bf16[4,512,1024]{2,1,0:T(8,128)(2,1)S(1)}, f32[512,512]{1,0:T(8,128)S(1)}) custom-call(bf16[128,4096]{1,0:T(8,128)(2,1)S(1)} %bitcast.83, bf16[512,512]{1,0:T(8,128)(2,1)S(1)} %pad_maximum_fusion.1.k_ref, bf16[128,4096]{1,0:T(8,128)(2,1)S(1)} %bitcast.85, f32[512,128]{1,0:T(8,128)S(1)} %add_select_fusion.bias_ref), custom_call_target="tpu_custom_call" | custom-call | flops 1073741824 | bytes 8388608 | tf_op jit(solution)/shard_map/probs/pallas_call | solution.py:64
  33.7 2.0 %copy-done = bf16[4,512,1024]{2,1,0:T(8,128)(2,1)} copy-done((bf16[4,512,1024]{2,1,0:T(8,128)(2,1)}, bf16[4,512,1024]{2,1,0:T(8,128)(2,1)S(1)}, u32[]{:S(2)}) %copy-start) | copy-done | bytes 4194328
  36.9 1.3 %collective-permute-start.12 = (bf16[192,512]{1,0:T(8,128)(2,1)S(1)}, bf16[192,512]{1,0:T(8,128)(2,1)S(1)}, u32[]{:S(2)}, u32[]{:S(2)}) collective-permute-start(bf16[192,512]{1,0:T(8,128)(2,1)S(1)} %slice.414), channel_id=1, source_target_pairs={{0,64},{32,96},{64,0},{96,32},{1,65},{33,97},{65,1},{97,33},{2,66}... | collective-permute-start | bytes 589832 | tf_op jit(solution)/shard_map/ppermute | solution.py:181
  38.2 1.3 %collective-permute-start.11 = (bf16[192,512]{1,0:T(8,128)(2,1)S(1)}, bf16[192,512]{1,0:T(8,128)(2,1)S(1)}, u32[]{:S(2)}, u32[]{:S(2)}) collective-permute-start(bf16[192,512]{1,0:T(8,128)(2,1)S(1)} %slice.414), channel_id=1, source_target_pairs={{0,32},{32,64},{64,96},{96,0},{1,33},{33,65},{65,97},{97,1},{2,34}... | collective-permute-start | bytes 589832 | tf_op jit(solution)/shard_map/ppermute | solution.py:180
  39.5 1.6 %maximum_select_fusion = bf16[2,2,320,512]{3,2,1,0:T(8,128)(2,1)S(1)} fusion(bf16[2,1,320,512]{3,2,1,0:T(8,128)(2,1)} %bitcast.16, bf16[2,1,320,512]{3,2,1,0:T(8,128)(2,1)S(1)} %maximum_select_fusion.1, pred[]{:T(512)S(6)} %eq.110), kind=kLoop, calls=%fused_computation.2 | loop fusion | flops 1966080 | bytes 2621441 | tf_op jit(solution)/shard_map/jit(_where)/select_n | solution.py:217
  41.1 2.6 %fusion.26 = f32[4,128,512]{2,1,0:T(8,128)S(1)} fusion(bf16[4,128,1280]{2,1,0:T(8,128)(2,1)} %bitcast.11, bf16[1280,512,1]{1,0,2:T(8,128)(2,1)S(1)} %bitcast.91), kind=kOutput, calls=%fused_computation.97 | convolution fusion | flops 671088640 | bytes 3670016 | tf_op jit(solution)/shard_map/dot_general | solution.py:226
  44.3 2.5 %collective-permute-start.7 = (bf16[128,512]{1,0:T(8,128)(2,1)S(1)}, bf16[128,512]{1,0:T(8,128)(2,1)S(1)}, u32[]{:S(2)}, u32[]{:S(2)}) collective-permute-start(bf16[128,512]{1,0:T(8,128)(2,1)S(1)} %get-tuple-element.139), channel_id=1, source_target_pairs={{0,4},{2,6},{4,0},{6,2},{1,5},{3,7},{5,1},{7,3},{8,12},{10,14},{12... | collective-permute-start | bytes 393224 | tf_op jit(solution)/shard_map/ppermute | solution.py:232
  46.8 1.8 %collective-permute-start.6 = (bf16[128,512]{1,0:T(8,128)(2,1)S(1)}, bf16[128,512]{1,0:T(8,128)(2,1)S(1)}, u32[]{:S(2)}, u32[]{:S(2)}) collective-permute-start(bf16[128,512]{1,0:T(8,128)(2,1)S(1)} %get-tuple-element.137), channel_id=1, source_target_pairs={{0,2},{2,4},{4,6},{6,0},{1,3},{3,5},{5,7},{7,1},{8,10},{10,12},{12... | collective-permute-start | bytes 393224 | tf_op jit(solution)/shard_map/ppermute | solution.py:232
  49.0 1.2 %collective-permute-start.13 = (bf16[128,512]{1,0:T(8,128)(2,1)S(1)}, bf16[128,512]{1,0:T(8,128)(2,1)S(1)}, u32[]{:S(2)}, u32[]{:S(2)}) collective-permute-start(bf16[128,512]{1,0:T(8,128)(2,1)S(1)} %select_convert_fusion.1), channel_id=1, source_target_pairs={{0,16},{16,0},{1,17},{17,1},{2,18},{18,2},{3,19},{19,3},{4,20},{20... | collective-permute-start | bytes 393224 | tf_op jit(solution)/shard_map/ppermute | solution.py:186
  51.2 1.2 collective-permute-done.6
  52.4 1.2 %collective-permute-start.9 = (bf16[128,512]{1,0:T(8,128)(2,1)S(1)}, bf16[128,512]{1,0:T(8,128)(2,1)S(1)}, u32[]{:S(2)}, u32[]{:S(2)}) collective-permute-start(bf16[128,512]{1,0:T(8,128)(2,1)S(1)} %fusion.11), channel_id=1, source_target_pairs={{0,16},{16,0},{1,17},{17,1},{2,18},{18,2},{3,19},{19,3},{4,20},{20... | collective-permute-start | bytes 393224 | tf_op jit(solution)/shard_map/ppermute | solution.py:141
  53.7 2.1 %collective-permute-done.13 = bf16[128,512]{1,0:T(8,128)(2,1)S(1)} collective-permute-done((bf16[128,512]{1,0:T(8,128)(2,1)S(1)}, bf16[128,512]{1,0:T(8,128)(2,1)S(1)}, u32[]{:S(2)}, u32[]{:S(2)}) %collective-permute-start.13) | collective-permute-done | bytes 131104 | tf_op jit(solution)/shard_map/ppermute | solution.py:186
  56.6 1.5 %collective-permute-start.17 = (bf16[128,512]{1,0:T(8,128)(2,1)}, bf16[128,512]{1,0:T(8,128)(2,1)}, u32[]{:S(2)}, u32[]{:S(2)}) collective-permute-start(bf16[128,512]{1,0:T(8,128)(2,1)} %add_convert_fusion.2), channel_id=1, source_target_pairs={{0,2},{2,4},{4,6},{6,0},{1,3},{3,5},{5,7},{7,1},{8,10},{10,12},{12... | collective-permute-start | bytes 393224 | tf_op jit(solution)/shard_map/ppermute | solution.py:240
  58.0 1.4 %collective-permute-start.18 = (bf16[128,512]{1,0:T(8,128)(2,1)}, bf16[128,512]{1,0:T(8,128)(2,1)}, u32[]{:S(2)}, u32[]{:S(2)}) collective-permute-start(bf16[128,512]{1,0:T(8,128)(2,1)} %add_convert_fusion.2), channel_id=1, source_target_pairs={{0,4},{2,6},{4,0},{6,2},{1,5},{3,7},{5,1},{7,3},{8,12},{10,14},{12... | collective-permute-start | bytes 393224 | tf_op jit(solution)/shard_map/ppermute | solution.py:240
  59.4 2.1 %collective-permute-start.19 = (bf16[128,512]{1,0:T(8,128)(2,1)}, bf16[128,512]{1,0:T(8,128)(2,1)}, u32[]{:S(2)}, u32[]{:S(2)}) collective-permute-start(bf16[128,512]{1,0:T(8,128)(2,1)} %add_convert_fusion.2), channel_id=1, source_target_pairs={{0,6},{2,0},{4,2},{6,4},{1,7},{3,1},{5,3},{7,5},{8,14},{10,8},{12,... | collective-permute-start | bytes 393224 | tf_op jit(solution)/shard_map/ppermute | solution.py:240
  61.5 1.6 %copy.10 = bf16[512,1280]{0,1:T(8,128)(2,1)S(1)} copy(bf16[512,1280]{1,0:T(8,128)(2,1)} %bitcast.8) | data formatting | bytes 2621440 | tf_op jit(solution)/shard_map/reshape | solution.py:211
  63.8 1.2 %collective-permute-start.14 = (bf16[256,512]{1,0:T(8,128)(2,1)S(1)}, bf16[256,512]{1,0:T(8,128)(2,1)S(1)}, u32[]{:S(2)}, u32[]{:S(2)}) collective-permute-start(bf16[256,512]{1,0:T(8,128)(2,1)S(1)} %maximum_select_fusion.5), channel_id=1, source_target_pairs={{0,32},{32,64},{64,96},{96,0},{1,33},{33,65},{65,97},{97,1},{2,34}... | collective-permute-start | bytes 786440 | tf_op jit(solution)/shard_map/ppermute | solution.py:149
  65.8 2.8 %collective-permute-start.15 = (bf16[192,512]{1,0:T(8,128)(2,1)}, bf16[192,512]{1,0:T(8,128)(2,1)}, u32[]{:S(2)}, u32[]{:S(2)}) collective-permute-start(bf16[192,512]{1,0:T(8,128)(2,1)} %slice.300), channel_id=1, source_target_pairs={{0,64},{32,96},{64,0},{96,32},{1,65},{33,97},{65,1},{97,33},{2,66}... | collective-permute-start | bytes 589832 | tf_op jit(solution)/shard_map/ppermute | solution.py:150
  69.2 1.2 select_select_fusion.3
  71.2 1.5 %copy-done.6 = f32[2,2,320,512]{3,2,1,0:T(8,128)} copy-done((f32[2,2,320,512]{3,2,1,0:T(8,128)}, f32[2,2,320,512]{3,2,1,0:T(8,128)S(1)}, u32[]{:S(2)}) %copy-start.6) | copy-done | bytes 2621464
  72.9 1.1 copy-done.8
  74.0 1.9 %convolution_convert_fusion = bf16[512,1280]{1,0:T(8,128)(2,1)} fusion(bf16[1280,512]{1,0:T(8,128)(2,1)S(1)} %bitcast.92, bf16[128,512]{1,0:T(8,128)(2,1)S(1)} %get-tuple-element.141, bf16[128,512]{1,0:T(8,128)(2,1)S(1)} %get-tuple-element.142, bf16[128,512]{1,0:T(8,128)(2,1)S(1)} %get-tuple-element.143, bf16[128,512]{1,0:T(8,128)(2,1)S(1)} %get-tuple-element.140), kind=kOutput, calls=%fused_computation | convolution fusion | flops 673841152 | bytes 3145728 | tf_op jit(solution)/shard_map/dot_general | solution.py:258
  76.0 6.0 %all-to-all-start.1 = ((bf16[4,128,1280]{2,1,0:T(8,128)(2,1)}), bf16[4,128,1280]{2,1,0:T(8,128)(2,1)}, u32[]{:S(2)}, u32[]{:S(2)}) async-start(bf16[4,128,1280]{2,1,0:T(8,128)(2,1)} %bitcast.35), calls=%async_computation.1 | async-start | bytes 2621440 | tf_op jit(solution)/shard_map/all_to_all | solution.py:286
  82.0 1.1 fusion.12
  83.2 1.9 %bitcast_add_fusion = f32[2,320,512]{2,1,0:T(8,128)S(1)} fusion(bf16[2,320,512]{2,1,0:T(8,128)(2,1)} %collective-permute-done.20, f32[2,2,320,512]{3,2,1,0:T(8,128)} %copy-done.6, s32[]{:T(128)S(6)} %select_n.399), kind=kLoop, calls=%fused_computation.3 | loop fusion | flops 655360 | bytes 3276804 | tf_op jit(solution)/shard_map/add | solution.py:262
  86.7 6.0 %scores.1 = (bf16[128,4096]{1,0:T(8,128)(2,1)}, f32[512,512]{1,0:T(8,128)S(1)}) custom-call(bf16[128,4096]{1,0:T(8,128)(2,1)S(1)} %bitcast.84, bf16[512,512]{1,0:T(8,128)(2,1)S(1)} %pad_maximum_fusion.1.k_ref, bf16[128,4096]{1,0:T(8,128)(2,1)S(1)} %bitcast.86, bf16[512,512]{1,0:T(8,128)(2,1)S(1)} %pad_maximum_fusion.2.v_ref, bf16[4,512,1024]{2,1,0:T(8,128)(2,1)S(1)} %copy-done.1), custom_call_target="tpu_custom_call" | custom-call | flops 1610612736 | bytes 8388608 | tf_op jit(solution)/shard_map/scores/pallas_call | solution.py:90
  93.6 2.4 %collective-permute-start.26 = (bf16[160,512]{1,0:T(8,128)(2,1)S(1)}, bf16[160,512]{1,0:T(8,128)(2,1)S(1)}, u32[]{:S(2)}, u32[]{:S(2)}) collective-permute-start(bf16[160,512]{1,0:T(8,128)(2,1)S(1)} %get-tuple-element.127), channel_id=1, source_target_pairs={{0,16},{8,24},{16,0},{24,8},{1,17},{9,25},{17,1},{25,9},{2,18},{10... | collective-permute-start | bytes 491528 | tf_op jit(solution)/shard_map/ppermute | solution.py:277
  96.5 2.8 %collective-permute-start.23 = (bf16[192,512]{1,0:T(8,128)(2,1)S(1)}, bf16[192,512]{1,0:T(8,128)(2,1)S(1)}, u32[]{:S(2)}, u32[]{:S(2)}) collective-permute-start(bf16[192,512]{1,0:T(8,128)(2,1)S(1)} %slice.413), channel_id=1, source_target_pairs={{0,64},{32,96},{64,0},{96,32},{1,65},{33,97},{65,1},{97,33},{2,66}... | collective-permute-start | bytes 589832 | tf_op jit(solution)/shard_map/ppermute | solution.py:181
  100.7 1.2 collective-permute-done.26
  101.8 1.7 %collective-permute-done.25 = bf16[160,512]{1,0:T(8,128)(2,1)S(1)} collective-permute-done((bf16[160,512]{1,0:T(8,128)(2,1)S(1)}, bf16[160,512]{1,0:T(8,128)(2,1)S(1)}, u32[]{:S(2)}, u32[]{:S(2)}) %collective-permute-start.25) | collective-permute-done | bytes 163872 | tf_op jit(solution)/shard_map/ppermute | solution.py:277
  103.5 1.1 fusion.8
  104.9 1.8 %collective-permute-start.29 = (bf16[160,512]{1,0:T(8,128)(2,1)S(1)}, bf16[160,512]{1,0:T(8,128)(2,1)S(1)}, u32[]{:S(2)}, u32[]{:S(2)}) collective-permute-start(bf16[160,512]{1,0:T(8,128)(2,1)S(1)} %fusion.8), channel_id=1, source_target_pairs={{0,32},{32,64},{64,96},{96,0},{1,33},{33,65},{65,97},{97,1},{2,34}... | collective-permute-start | bytes 491528 | tf_op jit(solution)/shard_map/ppermute | solution.py:279
  106.7 1.2 collective-permute-start.28
  108.2 2.9 %collective-permute-start.24 = (bf16[128,512]{1,0:T(8,128)(2,1)S(1)}, bf16[128,512]{1,0:T(8,128)(2,1)S(1)}, u32[]{:S(2)}, u32[]{:S(2)}) collective-permute-start(bf16[128,512]{1,0:T(8,128)(2,1)S(1)} %select_convert_fusion), channel_id=1, source_target_pairs={{0,16},{16,0},{1,17},{17,1},{2,18},{18,2},{3,19},{19,3},{4,20},{20... | collective-permute-start | bytes 393224 | tf_op jit(solution)/shard_map/ppermute | solution.py:186
  111.2 1.4 %slice_bitcast_fusion = (bf16[128,1280]{1,0:T(8,128)(2,1)S(1)}, bf16[128,1280]{1,0:T(8,128)(2,1)S(1)}, bf16[128,1280]{1,0:T(8,128)(2,1)S(1)}, bf16[128,1280]{1,0:T(8,128)(2,1)S(1)}) fusion(bf16[4,128,1280]{2,1,0:T(8,128)(2,1)} %all-to-all-done.1), kind=kLoop, calls=%fused_computation.23 | loop fusion | bytes 2621440 | tf_op jit(solution)/shard_map/squeeze | solution.py:288
  112.8 1.7 %collective-permute-done.29 = bf16[160,512]{1,0:T(8,128)(2,1)S(1)} collective-permute-done((bf16[160,512]{1,0:T(8,128)(2,1)S(1)}, bf16[160,512]{1,0:T(8,128)(2,1)S(1)}, u32[]{:S(2)}, u32[]{:S(2)}) %collective-permute-start.29) | collective-permute-done | bytes 163872 | tf_op jit(solution)/shard_map/ppermute | solution.py:279
  114.6 2.8 %collective-permute-start.31 = (bf16[160,512]{1,0:T(8,128)(2,1)S(1)}, bf16[160,512]{1,0:T(8,128)(2,1)S(1)}, u32[]{:S(2)}, u32[]{:S(2)}) collective-permute-start(bf16[160,512]{1,0:T(8,128)(2,1)S(1)} %add_convert_fusion), channel_id=1, source_target_pairs={{0,16},{16,0},{1,17},{17,1},{2,18},{18,2},{3,19},{19,3},{4,20},{20... | collective-permute-start | bytes 491528 | tf_op jit(solution)/shard_map/ppermute | solution.py:281
  118.2 3.4 %collective-permute-done.31 = bf16[160,512]{1,0:T(8,128)(2,1)S(1)} collective-permute-done((bf16[160,512]{1,0:T(8,128)(2,1)S(1)}, bf16[160,512]{1,0:T(8,128)(2,1)S(1)}, u32[]{:S(2)}, u32[]{:S(2)}) %collective-permute-start.31) | collective-permute-done | bytes 163872 | tf_op jit(solution)/shard_map/ppermute | solution.py:281
  (119 shorter events, 16.9 us)
Async XLA Ops:
  0.6 13.2 %collective-permute-start = (bf16[128,512]{1,0:T(8,128)(2,1)}, bf16[128,512]{1,0:T(8,128)(2,1)S(1)}, u32[]{:S(2)}, u32[]{:S(2)}) collective-permute-start(bf16[128,512]{1,0:T(8,128)(2,1)} %bitcast.97), channel_id=1, source_target_pairs={{0,16},{16,0},{1,17},{17,1},{2,18},{18,2},{3,19},{19,3},{4,20},{20... | collective-permute-start | bytes 393224 | tf_op jit(solution)/shard_map/ppermute | solution.py:141
  7.4 5.0 %copy-start.9 = (bf16[320,512]{1,0:T(8,128)(2,1)S(1)}, bf16[320,512]{1,0:T(8,128)(2,1)}, u32[]{:S(2)}) copy-start(bf16[320,512]{1,0:T(8,128)(2,1)} %param.25) | copy-start | bytes 983044
  7.4 6.0 %copy-start.14 = (s32[1,1024]{1,0:T(1,128)S(1)}, s32[1,1024]{1,0:T(1,128)}, u32[]{:S(2)}) copy-start(s32[1,1024]{1,0:T(1,128)} %param.27) | copy-start | bytes 12292
  7.4 6.4 %copy-start.12 = (bf16[1,128,512]{2,1,0:T(8,128)(2,1)S(1)}, bf16[1,128,512]{2,1,0:T(8,128)(2,1)}, u32[]{:S(2)}) copy-start(bf16[1,128,512]{2,1,0:T(8,128)(2,1)} %param.24) | copy-start | bytes 393220
  7.4 28.2 %all-to-all-start = ((bf16[4,128,1280]{2,1,0:T(8,128)(2,1)}), bf16[4,128,1280]{2,1,0:T(8,128)(2,1)}, u32[]{:S(2)}, u32[]{:S(2)}) async-start(bf16[4,128,1280]{2,1,0:T(8,128)(2,1)} %pad_maximum_fusion), calls=%async_computation | async-start | bytes 2621440 | tf_op jit(solution)/shard_map/all_to_all | solution.py:211
  12.4 8.9 %collective-permute-start.4 = (bf16[320,512]{1,0:T(8,128)(2,1)S(1)}, bf16[320,512]{1,0:T(8,128)(2,1)S(1)}, u32[]{:S(2)}, u32[]{:S(2)}) collective-permute-start(bf16[320,512]{1,0:T(8,128)(2,1)S(1)} %copy-done.9), channel_id=1, source_target_pairs={{0,8},{8,0},{1,9},{9,1},{2,10},{10,2},{3,11},{11,3},{4,12},{12,4},... | collective-permute-start | bytes 983048 | tf_op jit(solution)/shard_map/ppermute | solution.py:212
  14.0 9.4 %collective-permute-start.1 = (bf16[256,512]{1,0:T(8,128)(2,1)S(1)}, bf16[256,512]{1,0:T(8,128)(2,1)S(1)}, u32[]{:S(2)}, u32[]{:S(2)}) collective-permute-start(bf16[256,512]{1,0:T(8,128)(2,1)S(1)} %maximum_select_fusion.4), channel_id=1, source_target_pairs={{0,32},{32,64},{64,96},{96,0},{1,33},{33,65},{65,97},{97,1},{2,34}... | collective-permute-start | bytes 786440 | tf_op jit(solution)/shard_map/ppermute | solution.py:149
  15.7 12.2 %collective-permute-start.2 = (bf16[192,512]{1,0:T(8,128)(2,1)S(1)}, bf16[192,512]{1,0:T(8,128)(2,1)S(1)}, u32[]{:S(2)}, u32[]{:S(2)}) collective-permute-start(bf16[192,512]{1,0:T(8,128)(2,1)S(1)} %slice.323), channel_id=1, source_target_pairs={{0,64},{32,96},{64,0},{96,32},{1,65},{33,97},{65,1},{97,33},{2,66}... | collective-permute-start | bytes 589832 | tf_op jit(solution)/shard_map/ppermute | solution.py:150
  18.7 9.2 %collective-permute-start.3 = (bf16[192,512]{1,0:T(8,128)(2,1)S(1)}, bf16[192,512]{1,0:T(8,128)(2,1)S(1)}, u32[]{:S(2)}, u32[]{:S(2)}) collective-permute-start(bf16[192,512]{1,0:T(8,128)(2,1)S(1)} %slice.323), channel_id=1, source_target_pairs={{0,96},{32,0},{64,32},{96,64},{1,97},{33,1},{65,33},{97,65},{2,98}... | collective-permute-start | bytes 589832 | tf_op jit(solution)/shard_map/ppermute | solution.py:151
  22.2 17.3 %collective-permute-start.5 = (bf16[2,320,512]{2,1,0:T(8,128)(2,1)}, bf16[2,320,512]{2,1,0:T(8,128)(2,1)}, u32[]{:S(2)}, u32[]{:S(2)}) collective-permute-start(bf16[2,320,512]{2,1,0:T(8,128)(2,1)} %maximum_select_fusion.2), channel_id=1, source_target_pairs={{0,1},{1,0},{2,3},{3,2},{4,5},{5,4},{6,7},{7,6},{8,9},{9,8},{10,11... | collective-permute-start | bytes 1966088 | tf_op jit(solution)/shard_map/ppermute | solution.py:216
  23.4 4.7 %copy-start.2 = (bf16[1,128,4096]{2,1,0:T(8,128)(2,1)S(1)}, bf16[1,128,4096]{2,1,0:T(8,128)(2,1)}, u32[]{:S(2)}) copy-start(bf16[1,128,4096]{2,1,0:T(8,128)(2,1)} %param.23) | copy-start | bytes 3145732
  23.4 4.7 %copy-start.3 = (bf16[1,128,4096]{2,1,0:T(8,128)(2,1)S(1)}, bf16[1,128,4096]{2,1,0:T(8,128)(2,1)}, u32[]{:S(2)}) copy-start(bf16[1,128,4096]{2,1,0:T(8,128)(2,1)} %param.26) | copy-start | bytes 3145732
  33.7 2.0 %copy-start = (bf16[4,512,1024]{2,1,0:T(8,128)(2,1)}, bf16[4,512,1024]{2,1,0:T(8,128)(2,1)S(1)}, u32[]{:S(2)}) copy-start(bf16[4,512,1024]{2,1,0:T(8,128)(2,1)S(1)} %get-tuple-element.113.p_ref) | copy-start | bytes 12582916
  36.0 10.9 %collective-permute-start.10 = (bf16[256,512]{1,0:T(8,128)(2,1)S(1)}, bf16[256,512]{1,0:T(8,128)(2,1)S(1)}, u32[]{:S(2)}, u32[]{:S(2)}) collective-permute-start(bf16[256,512]{1,0:T(8,128)(2,1)S(1)} %convert_element_type.142), channel_id=1, source_target_pairs={{0,96},{32,0},{64,32},{96,64},{1,97},{33,1},{65,33},{97,65},{2,98}... | collective-permute-start | bytes 786440 | tf_op jit(solution)/shard_map/ppermute | solution.py:179
  36.9 11.8 %collective-permute-start.12 = (bf16[192,512]{1,0:T(8,128)(2,1)S(1)}, bf16[192,512]{1,0:T(8,128)(2,1)S(1)}, u32[]{:S(2)}, u32[]{:S(2)}) collective-permute-start(bf16[192,512]{1,0:T(8,128)(2,1)S(1)} %slice.414), channel_id=1, source_target_pairs={{0,64},{32,96},{64,0},{96,32},{1,65},{33,97},{65,1},{97,33},{2,66}... | collective-permute-start | bytes 589832 | tf_op jit(solution)/shard_map/ppermute | solution.py:181
  38.2 10.5 %collective-permute-start.11 = (bf16[192,512]{1,0:T(8,128)(2,1)S(1)}, bf16[192,512]{1,0:T(8,128)(2,1)S(1)}, u32[]{:S(2)}, u32[]{:S(2)}) collective-permute-start(bf16[192,512]{1,0:T(8,128)(2,1)S(1)} %slice.414), channel_id=1, source_target_pairs={{0,32},{32,64},{64,96},{96,0},{1,33},{33,65},{65,97},{97,1},{2,34}... | collective-permute-start | bytes 589832 | tf_op jit(solution)/shard_map/ppermute | solution.py:180
  41.1 2.6 %copy-start.7 = (bf16[2,2,320,512]{3,2,1,0:T(8,128)(2,1)}, bf16[2,2,320,512]{3,2,1,0:T(8,128)(2,1)S(1)}, u32[]{:S(2)}) copy-start(bf16[2,2,320,512]{3,2,1,0:T(8,128)(2,1)S(1)} %maximum_select_fusion) | copy-start | bytes 3932164
  43.8 6.4 %collective-permute-start.8 = (bf16[128,512]{1,0:T(8,128)(2,1)S(1)}, bf16[128,512]{1,0:T(8,128)(2,1)S(1)}, u32[]{:S(2)}, u32[]{:S(2)}) collective-permute-start(bf16[128,512]{1,0:T(8,128)(2,1)S(1)} %get-tuple-element.138), channel_id=1, source_target_pairs={{0,6},{2,0},{4,2},{6,4},{1,7},{3,1},{5,3},{7,5},{8,14},{10,8},{12,... | collective-permute-start | bytes 393224 | tf_op jit(solution)/shard_map/ppermute | solution.py:232
  44.3 6.9 %collective-permute-start.7 = (bf16[128,512]{1,0:T(8,128)(2,1)S(1)}, bf16[128,512]{1,0:T(8,128)(2,1)S(1)}, u32[]{:S(2)}, u32[]{:S(2)}) collective-permute-start(bf16[128,512]{1,0:T(8,128)(2,1)S(1)} %get-tuple-element.139), channel_id=1, source_target_pairs={{0,4},{2,6},{4,0},{6,2},{1,5},{3,7},{5,1},{7,3},{8,12},{10,14},{12... | collective-permute-start | bytes 393224 | tf_op jit(solution)/shard_map/ppermute | solution.py:232
  46.8 5.5 %collective-permute-start.6 = (bf16[128,512]{1,0:T(8,128)(2,1)S(1)}, bf16[128,512]{1,0:T(8,128)(2,1)S(1)}, u32[]{:S(2)}, u32[]{:S(2)}) collective-permute-start(bf16[128,512]{1,0:T(8,128)(2,1)S(1)} %get-tuple-element.137), channel_id=1, source_target_pairs={{0,2},{2,4},{4,6},{6,0},{1,3},{3,5},{5,7},{7,1},{8,10},{10,12},{12... | collective-permute-start | bytes 393224 | tf_op jit(solution)/shard_map/ppermute | solution.py:232
  49.0 6.8 %collective-permute-start.13 = (bf16[128,512]{1,0:T(8,128)(2,1)S(1)}, bf16[128,512]{1,0:T(8,128)(2,1)S(1)}, u32[]{:S(2)}, u32[]{:S(2)}) collective-permute-start(bf16[128,512]{1,0:T(8,128)(2,1)S(1)} %select_convert_fusion.1), channel_id=1, source_target_pairs={{0,16},{16,0},{1,17},{17,1},{2,18},{18,2},{3,19},{19,3},{4,20},{20... | collective-permute-start | bytes 393224 | tf_op jit(solution)/shard_map/ppermute | solution.py:186
  52.4 10.7 %collective-permute-start.9 = (bf16[128,512]{1,0:T(8,128)(2,1)S(1)}, bf16[128,512]{1,0:T(8,128)(2,1)S(1)}, u32[]{:S(2)}, u32[]{:S(2)}) collective-permute-start(bf16[128,512]{1,0:T(8,128)(2,1)S(1)} %fusion.11), channel_id=1, source_target_pairs={{0,16},{16,0},{1,17},{17,1},{2,18},{18,2},{3,19},{19,3},{4,20},{20... | collective-permute-start | bytes 393224 | tf_op jit(solution)/shard_map/ppermute | solution.py:141
  56.6 12.0 %collective-permute-start.17 = (bf16[128,512]{1,0:T(8,128)(2,1)}, bf16[128,512]{1,0:T(8,128)(2,1)}, u32[]{:S(2)}, u32[]{:S(2)}) collective-permute-start(bf16[128,512]{1,0:T(8,128)(2,1)} %add_convert_fusion.2), channel_id=1, source_target_pairs={{0,2},{2,4},{4,6},{6,0},{1,3},{3,5},{5,7},{7,1},{8,10},{10,12},{12... | collective-permute-start | bytes 393224 | tf_op jit(solution)/shard_map/ppermute | solution.py:240
  58.0 11.2 %collective-permute-start.18 = (bf16[128,512]{1,0:T(8,128)(2,1)}, bf16[128,512]{1,0:T(8,128)(2,1)}, u32[]{:S(2)}, u32[]{:S(2)}) collective-permute-start(bf16[128,512]{1,0:T(8,128)(2,1)} %add_convert_fusion.2), channel_id=1, source_target_pairs={{0,4},{2,6},{4,0},{6,2},{1,5},{3,7},{5,1},{7,3},{8,12},{10,14},{12... | collective-permute-start | bytes 393224 | tf_op jit(solution)/shard_map/ppermute | solution.py:240
  59.4 9.8 %collective-permute-start.19 = (bf16[128,512]{1,0:T(8,128)(2,1)}, bf16[128,512]{1,0:T(8,128)(2,1)}, u32[]{:S(2)}, u32[]{:S(2)}) collective-permute-start(bf16[128,512]{1,0:T(8,128)(2,1)} %add_convert_fusion.2), channel_id=1, source_target_pairs={{0,6},{2,0},{4,2},{6,4},{1,7},{3,1},{5,3},{7,5},{8,14},{10,8},{12,... | collective-permute-start | bytes 393224 | tf_op jit(solution)/shard_map/ppermute | solution.py:240
  63.8 18.1 %collective-permute-start.14 = (bf16[256,512]{1,0:T(8,128)(2,1)S(1)}, bf16[256,512]{1,0:T(8,128)(2,1)S(1)}, u32[]{:S(2)}, u32[]{:S(2)}) collective-permute-start(bf16[256,512]{1,0:T(8,128)(2,1)S(1)} %maximum_select_fusion.5), channel_id=1, source_target_pairs={{0,32},{32,64},{64,96},{96,0},{1,33},{33,65},{65,97},{97,1},{2,34}... | collective-permute-start | bytes 786440 | tf_op jit(solution)/shard_map/ppermute | solution.py:149
  65.8 16.2 %collective-permute-start.15 = (bf16[192,512]{1,0:T(8,128)(2,1)}, bf16[192,512]{1,0:T(8,128)(2,1)}, u32[]{:S(2)}, u32[]{:S(2)}) collective-permute-start(bf16[192,512]{1,0:T(8,128)(2,1)} %slice.300), channel_id=1, source_target_pairs={{0,64},{32,96},{64,0},{96,32},{1,65},{33,97},{65,1},{97,33},{2,66}... | collective-permute-start | bytes 589832 | tf_op jit(solution)/shard_map/ppermute | solution.py:150
  68.5 13.5 %collective-permute-start.16 = (bf16[192,512]{1,0:T(8,128)(2,1)}, bf16[192,512]{1,0:T(8,128)(2,1)}, u32[]{:S(2)}, u32[]{:S(2)}) collective-permute-start(bf16[192,512]{1,0:T(8,128)(2,1)} %slice.300), channel_id=1, source_target_pairs={{0,96},{32,0},{64,32},{96,64},{1,97},{33,1},{65,33},{97,65},{2,98}... | collective-permute-start | bytes 589832 | tf_op jit(solution)/shard_map/ppermute | solution.py:151
  71.2 1.5 %copy-start.6 = (f32[2,2,320,512]{3,2,1,0:T(8,128)}, f32[2,2,320,512]{3,2,1,0:T(8,128)S(1)}, u32[]{:S(2)}) copy-start(f32[2,2,320,512]{3,2,1,0:T(8,128)S(1)} %fusion.1) | copy-start | bytes 7864324
  72.7 1.3 %copy-start.8 = (bf16[2,2,320,512]{3,2,1,0:T(8,128)(2,1)S(1)}, bf16[2,2,320,512]{3,2,1,0:T(8,128)(2,1)}, u32[]{:S(2)}) copy-start(bf16[2,2,320,512]{3,2,1,0:T(8,128)(2,1)} %copy-done.7) | copy-start | bytes 3932164
  72.8 10.4 %collective-permute-start.20 = (bf16[2,320,512]{2,1,0:T(8,128)(2,1)S(1)}, bf16[2,320,512]{2,1,0:T(8,128)(2,1)}, u32[]{:S(2)}, u32[]{:S(2)}) collective-permute-start(bf16[2,320,512]{2,1,0:T(8,128)(2,1)S(1)} %fusion), channel_id=1, source_target_pairs={{0,1},{1,0},{2,3},{3,2},{4,5},{5,4},{6,7},{7,6},{8,9},{9,8},{10,11... | collective-permute-start | bytes 1966088 | tf_op jit(solution)/shard_map/ppermute | solution.py:262
  76.0 6.1 %copy-start.11 = (bf16[128,512]{1,0:T(8,128)(2,1)S(1)}, bf16[128,512]{1,0:T(8,128)(2,1)}, u32[]{:S(2)}) copy-start(bf16[128,512]{1,0:T(8,128)(2,1)} %copy-done.10) | copy-start | bytes 393220
  76.0 35.2 %all-to-all-start.1 = ((bf16[4,128,1280]{2,1,0:T(8,128)(2,1)}), bf16[4,128,1280]{2,1,0:T(8,128)(2,1)}, u32[]{:S(2)}, u32[]{:S(2)}) async-start(bf16[4,128,1280]{2,1,0:T(8,128)(2,1)} %bitcast.35), calls=%async_computation.1 | async-start | bytes 2621440 | tf_op jit(solution)/shard_map/all_to_all | solution.py:286
  83.1 3.1 %copy-start.4 = (bf16[1,128,4096]{2,1,0:T(8,128)(2,1)S(1)}, bf16[1,128,4096]{2,1,0:T(8,128)(2,1)}, u32[]{:S(2)}) copy-start(bf16[1,128,4096]{2,1,0:T(8,128)(2,1)} %param.26) | copy-start | bytes 3145732
  83.2 3.5 %copy-start.1 = (bf16[4,512,1024]{2,1,0:T(8,128)(2,1)S(1)}, bf16[4,512,1024]{2,1,0:T(8,128)(2,1)}, u32[]{:S(2)}) copy-start(bf16[4,512,1024]{2,1,0:T(8,128)(2,1)} %copy-done) | copy-start | bytes 12582916
  85.1 1.1 copy-start.5
  92.8 7.0 %collective-permute-start.27 = (bf16[160,512]{1,0:T(8,128)(2,1)S(1)}, bf16[160,512]{1,0:T(8,128)(2,1)S(1)}, u32[]{:S(2)}, u32[]{:S(2)}) collective-permute-start(bf16[160,512]{1,0:T(8,128)(2,1)S(1)} %get-tuple-element.126), channel_id=1, source_target_pairs={{0,24},{8,0},{16,8},{24,16},{1,25},{9,1},{17,9},{25,17},{2,26},{10... | collective-permute-start | bytes 491528 | tf_op jit(solution)/shard_map/ppermute | solution.py:277
  93.6 8.3 %collective-permute-start.26 = (bf16[160,512]{1,0:T(8,128)(2,1)S(1)}, bf16[160,512]{1,0:T(8,128)(2,1)S(1)}, u32[]{:S(2)}, u32[]{:S(2)}) collective-permute-start(bf16[160,512]{1,0:T(8,128)(2,1)S(1)} %get-tuple-element.127), channel_id=1, source_target_pairs={{0,16},{8,24},{16,0},{24,8},{1,17},{9,25},{17,1},{25,9},{2,18},{10... | collective-permute-start | bytes 491528 | tf_op jit(solution)/shard_map/ppermute | solution.py:277
  95.9 7.6 %collective-permute-start.25 = (bf16[160,512]{1,0:T(8,128)(2,1)S(1)}, bf16[160,512]{1,0:T(8,128)(2,1)S(1)}, u32[]{:S(2)}, u32[]{:S(2)}) collective-permute-start(bf16[160,512]{1,0:T(8,128)(2,1)S(1)} %get-tuple-element.128), channel_id=1, source_target_pairs={{0,8},{8,16},{16,24},{24,0},{1,9},{9,17},{17,25},{25,1},{2,10},{10... | collective-permute-start | bytes 491528 | tf_op jit(solution)/shard_map/ppermute | solution.py:277
  96.1 10.5 %collective-permute-start.21 = (bf16[256,512]{1,0:T(8,128)(2,1)S(1)}, bf16[256,512]{1,0:T(8,128)(2,1)S(1)}, u32[]{:S(2)}, u32[]{:S(2)}) collective-permute-start(bf16[256,512]{1,0:T(8,128)(2,1)S(1)} %convert_element_type.171), channel_id=1, source_target_pairs={{0,96},{32,0},{64,32},{96,64},{1,97},{33,1},{65,33},{97,65},{2,98}... | collective-permute-start | bytes 786440 | tf_op jit(solution)/shard_map/ppermute | solution.py:179
  96.5 11.4 %collective-permute-start.23 = (bf16[192,512]{1,0:T(8,128)(2,1)S(1)}, bf16[192,512]{1,0:T(8,128)(2,1)S(1)}, u32[]{:S(2)}, u32[]{:S(2)}) collective-permute-start(bf16[192,512]{1,0:T(8,128)(2,1)S(1)} %slice.413), channel_id=1, source_target_pairs={{0,64},{32,96},{64,0},{96,32},{1,65},{33,97},{65,1},{97,33},{2,66}... | collective-permute-start | bytes 589832 | tf_op jit(solution)/shard_map/ppermute | solution.py:181
  99.8 8.1 %collective-permute-start.22 = (bf16[192,512]{1,0:T(8,128)(2,1)S(1)}, bf16[192,512]{1,0:T(8,128)(2,1)S(1)}, u32[]{:S(2)}, u32[]{:S(2)}) collective-permute-start(bf16[192,512]{1,0:T(8,128)(2,1)S(1)} %slice.413), channel_id=1, source_target_pairs={{0,32},{32,64},{64,96},{96,0},{1,33},{33,65},{65,97},{97,1},{2,34}... | collective-permute-start | bytes 589832 | tf_op jit(solution)/shard_map/ppermute | solution.py:180
  104.6 8.3 %collective-permute-start.30 = (bf16[160,512]{1,0:T(8,128)(2,1)S(1)}, bf16[160,512]{1,0:T(8,128)(2,1)S(1)}, u32[]{:S(2)}, u32[]{:S(2)}) collective-permute-start(bf16[160,512]{1,0:T(8,128)(2,1)S(1)} %fusion.8), channel_id=1, source_target_pairs={{0,96},{32,0},{64,32},{96,64},{1,97},{33,1},{65,33},{97,65},{2,98}... | collective-permute-start | bytes 491528 | tf_op jit(solution)/shard_map/ppermute | solution.py:279
  104.9 9.7 %collective-permute-start.29 = (bf16[160,512]{1,0:T(8,128)(2,1)S(1)}, bf16[160,512]{1,0:T(8,128)(2,1)S(1)}, u32[]{:S(2)}, u32[]{:S(2)}) collective-permute-start(bf16[160,512]{1,0:T(8,128)(2,1)S(1)} %fusion.8), channel_id=1, source_target_pairs={{0,32},{32,64},{64,96},{96,0},{1,33},{33,65},{65,97},{97,1},{2,34}... | collective-permute-start | bytes 491528 | tf_op jit(solution)/shard_map/ppermute | solution.py:279
  106.7 7.9 %collective-permute-start.28 = (bf16[160,512]{1,0:T(8,128)(2,1)S(1)}, bf16[160,512]{1,0:T(8,128)(2,1)S(1)}, u32[]{:S(2)}, u32[]{:S(2)}) collective-permute-start(bf16[160,512]{1,0:T(8,128)(2,1)S(1)} %fusion.8), channel_id=1, source_target_pairs={{0,64},{32,96},{64,0},{96,32},{1,65},{33,97},{65,1},{97,33},{2,66}... | collective-permute-start | bytes 491528 | tf_op jit(solution)/shard_map/ppermute | solution.py:279
  108.2 9.2 %collective-permute-start.24 = (bf16[128,512]{1,0:T(8,128)(2,1)S(1)}, bf16[128,512]{1,0:T(8,128)(2,1)S(1)}, u32[]{:S(2)}, u32[]{:S(2)}) collective-permute-start(bf16[128,512]{1,0:T(8,128)(2,1)S(1)} %select_convert_fusion), channel_id=1, source_target_pairs={{0,16},{16,0},{1,17},{17,1},{2,18},{18,2},{3,19},{19,3},{4,20},{20... | collective-permute-start | bytes 393224 | tf_op jit(solution)/shard_map/ppermute | solution.py:186
  112.8 9.7 %copy-start.13 = (bf16[128,5120]{1,0:T(8,128)(2,1)}, bf16[128,5120]{1,0:T(8,128)(2,1)S(1)}, u32[]{:S(2)}) copy-start(bf16[128,5120]{1,0:T(8,128)(2,1)S(1)} %slice_dynamic-update-slice_fusion) | copy-start | bytes 3932164
  114.6 6.9 %collective-permute-start.31 = (bf16[160,512]{1,0:T(8,128)(2,1)S(1)}, bf16[160,512]{1,0:T(8,128)(2,1)S(1)}, u32[]{:S(2)}, u32[]{:S(2)}) collective-permute-start(bf16[160,512]{1,0:T(8,128)(2,1)S(1)} %add_convert_fusion), channel_id=1, source_target_pairs={{0,16},{16,0},{1,17},{17,1},{2,18},{18,2},{3,19},{19,3},{4,20},{20... | collective-permute-start | bytes 491528 | tf_op jit(solution)/shard_map/ppermute | solution.py:281
  (1 other events, 0.7 us)

commit v3 on v2

--- a/solution.py
+++ b/solution.py
@@ -56,6 +56,10 @@
         dq_ref[:, part] = dq[:, part].T.astype(BF)
 
 
+def far(value):
+    return pltpu.with_memory_space_constraint(value, pltpu.HBM)
+
+
 def column(rows, width):
     return pl.BlockSpec((rows, width), lambda g: (0, g))
 
@@ -75,7 +79,7 @@
             column(SLOTS, HEAD),
         ],
         out_shape=[
-            jax.ShapeDtypeStruct((KEY_HEADS, SLOTS, GROUP * ROWS), BF),
+            pltpu.HBM((KEY_HEADS, SLOTS, GROUP * ROWS), BF),
             jax.ShapeDtypeStruct((SLOTS, KEY_HEADS * HEAD), F32),
         ],
         compiler_params=pltpu.CompilerParams(vmem_limit_bytes=24 << 20),
@@ -107,7 +111,7 @@
             flops=6 * SLOTS * ROWS * 32 * HEAD, bytes_accessed=8 << 20, transcendentals=0
         ),
         name="scores",
-    )(q, k, g, v, p)
+    )(far(q), k, far(g), v, far(p))
 
 
 def slot_bias(passages, s):
@@ -125,6 +129,54 @@
     return jnp.where(jnp.concatenate([head_ok, near_ok]), 0.0, -1e30).astype(F32)
 
 
+def grads_kernel(at_ref, crossed_ref, weight_ref, *refs):
+    nears, (back_ref, kept_ref, given_ref, gathered_ref) = refs[:4], refs[4:]
+    x, c = at_ref[0], at_ref[1]
+    for n in range(4):
+        row = pl.multiple_of((x + 4 - n) % 4 * ROWS, ROWS)
+        gathered_ref[pl.ds(row, ROWS), :] = nears[n][...]
+    gathered = gathered_ref[...]
+    term = lax.dot_general(
+        crossed_ref[...], gathered, (((0,), (0,)), ((), ())), preferred_element_type=F32
+    )
+    each = term.shape[0] // 2
+    kept_ref[0] = jnp.where(c == 0, term[:each], term[each:])
+    given_ref[0] = jnp.where(c == 0, term[each:], term[:each]).astype(BF)
+    back_ref[...] = lax.dot_general(
+        gathered, weight_ref[...], (((1,), (1,)), ((), ())), preferred_element_type=F32
+    ).astype(BF)
+
+
+def grads_call(at, crossed, weight, nears):
+    rows, columns = crossed.shape
+    kv, half, each = weight.shape[1], columns // 2, columns // 4
+    piece = pl.BlockSpec((1, each, kv), lambda i, at: (i, 0, 0))
+    return pl.pallas_call(
+        grads_kernel,
+        grid_spec=pltpu.PrefetchScalarGridSpec(
+            num_scalar_prefetch=1,
+            grid=(2,),
+            in_specs=[
+                pl.BlockSpec((rows, half), lambda i, at: (0, i)),
+                pl.BlockSpec((half, kv), lambda i, at: (i, 0)),
+            ]
+            + [pl.BlockSpec((ROWS, kv), lambda i, at: (0, 0))] * 4,
+            out_specs=[pl.BlockSpec((rows, half), lambda i, at: (0, i)), piece, piece],
+            scratch_shapes=[pltpu.VMEM((rows, kv), BF)],
+        ),
+        out_shape=[
+            pltpu.HBM((rows, columns), BF),
+            pltpu.HBM((2, each, kv), F32),
+            jax.ShapeDtypeStruct((2, each, kv), BF),
+        ],
+        compiler_params=pltpu.CompilerParams(vmem_limit_bytes=24 << 20),
+        cost_estimate=pl.CostEstimate(
+            flops=4 * rows * columns * kv, bytes_accessed=8 << 20, transcendentals=0
+        ),
+        name="grads",
+    )(at, crossed, weight, *nears)
+
+
 def turned(count, step):
     return tuple((i, (i + step) % count) for i in range(count))
 
@@ -137,54 +189,59 @@
     return lax.optimization_barrier((value,) + others)[0]
 
 
-def paired(block, zh):
-    other = lax.ppermute(block, "zh", SWAP)
-    pair = jnp.where(
-        zh == 0, jnp.concatenate([block, other]), jnp.concatenate([other, block])
-    )
-    return other, pair
-
-
-def spread(block, other, pair, y, zh):
-    before = lax.ppermute(pair, "y", turned(4, 1))
-    to_third = lax.ppermute(pair[:BACK], "y", turned(4, 2))
-    to_last = lax.ppermute(pair[:BACK], "y", turned(4, 3))
+def held(values, others):
+    return lax.optimization_barrier((tuple(values), tuple(others)))[0]
+
+
+def turns(value, axis, count, steps=(1, 2, 3)):
+    return [lax.ppermute(value, axis, turned(count, n)) for n in steps]
+
+
+def nearby(block, y, zh):
+    before, third, last = turns(block, "y", 4)
     header = jnp.where(
-        y == 0,
-        pair[:BACK],
-        jnp.where(y == 1, before[:BACK], jnp.where(y == 2, to_third, to_last)),
-    )
-    window = jnp.where(
-        zh == 0, before[2 * ROWS - BACK :], jnp.concatenate([before[BACK:], other])
-    )
-    return jnp.concatenate([header, window, block])
-
-
-def parted(slots, y, zh):
-    header, window = slots[:BACK], slots[BACK : 2 * BACK]
+        y == 0, block, jnp.where(y == 1, before, jnp.where(y == 2, third, last))
+    )
+    return before, header, jnp.concatenate([jnp.where(zh == 0, block, before), header])
+
+
+def placed(block, before, header, other, zh):
     tail = 2 * ROWS - BACK
-    zeros = jnp.zeros((2 * ROWS, slots.shape[1]), F32)
-    before = jnp.where(
-        zh == 0,
-        zeros.at[tail:].set(window),
-        zeros.at[BACK:].set(window[:tail]),
-    ) + jnp.where(y == 1, zeros.at[:BACK].set(header), 0.0)
-    return before.astype(BF), header.astype(BF)
-
-
-def collected(slots, before, half_header, y, zh):
-    header, window, own = slots[:BACK], slots[BACK : 2 * BACK], slots[2 * BACK :]
-    tail = 2 * ROWS - BACK
-    zeros = jnp.zeros((2 * ROWS, slots.shape[1]), F32)
-    from_next = lax.ppermute(before, "y", turned(4, 3))
-    from_last = lax.ppermute(half_header, "y", turned(4, 1))
-    from_third = lax.ppermute(half_header, "y", turned(4, 2))
-    first = header + from_last.astype(F32) + from_third.astype(F32)
-    pair = from_next.astype(F32) + jnp.where(y == 0, zeros.at[:BACK].set(first), 0.0)
-    low, high = pair[:ROWS], pair[ROWS:]
-    low = low + jnp.where(zh == 1, window[tail:], 0.0)
-    sent = lax.ppermute(jnp.where(zh == 0, high, low).astype(BF), "zh", SWAP)
-    return own + jnp.where(zh == 0, low, high) + sent.astype(F32)
+    nearest, header_too = other[:ROWS], other[ROWS:]
+    low = jnp.where(zh == 0, header, header_too)
+    high = jnp.where(zh == 0, header_too, header)
+    return jnp.concatenate([low, high[:tail], before[tail:], nearest, block])
+
+
+def parted(slots, zh):
+    low = slots[:ROWS]
+    high = jnp.concatenate([slots[ROWS:BACK], jnp.zeros_like(slots[BACK:2 * ROWS])])
+    nearest = slots[2 * BACK - ROWS : 2 * BACK]
+    sent = jnp.concatenate([nearest, jnp.where(zh == 0, high, low)]).astype(BF)
+    return jnp.where(zh == 0, low, high), sent
+
+
+def joined(slots, header, other, y, zh):
+    nearest, header_too = other[:ROWS].astype(F32), other[ROWS:].astype(F32)
+    header = header + header_too
+    tail = slots[BACK : 2 * BACK - ROWS]
+    before = jnp.concatenate([jnp.zeros_like(tail), tail])
+    before = before + jnp.where(zh == 1, nearest, 0.0) + jnp.where(y == 1, header, 0.0)
+    own = slots[2 * BACK :] + jnp.where(zh == 0, nearest, 0.0) + jnp.where(y == 0, header, 0.0)
+    return own, before.astype(BF), header.astype(BF)
+
+
+def returned(before, header):
+    return [
+        lax.ppermute(before, "y", turned(4, 3)),
+        lax.ppermute(header, "y", turned(4, 2)),
+        lax.ppermute(header, "y", turned(4, 1)),
+    ]
+
+
+def summed(own, got, y):
+    from_next, third, last = (value.astype(F32) for value in got)
+    return (own + from_next + jnp.where(y == 0, third + last, 0.0)).astype(BF)
 
 
 def on_device(hidden_in, queries, saved_keys, value_matrix, output_gradient, passage_index):
@@ -196,8 +253,9 @@
     each, half = width // 16, width // 2
     two = 2 * each
 
-    k_other, k_pair = paired(k, zh)
-    k_slots = spread(k, k_other, k_pair, y, zh)
+    k_before, k_header, k_sent = nearby(k, y, zh)
+    k_other = lax.ppermute(k_sent, "zh", SWAP)
+    k_slots = placed(k, k_before, k_header, k_other, zh)
 
     by_x = jnp.stack(
         [
@@ -208,7 +266,7 @@
             for i in range(4)
         ]
     )
-    crossed = lax.all_to_all(by_x, "x", 0, 0).reshape(4 * ROWS, 4 * each)
+    crossed = lax.all_to_all(after(by_x, k_sent), "x", 0, 0).reshape(4 * ROWS, 4 * each)
     across = lax.ppermute(value_matrix, "zl", SWAP)
     planes = jnp.where(
         zl == 0, jnp.stack([value_matrix, across]), jnp.stack([across, value_matrix])
@@ -220,65 +278,70 @@
 
     bias = slot_bias(passage_index[0], s)
     probs, dv_slots = probs_call(q, k_slots, g, bias)
-    dv_slots = after(dv_slots, crossed)
-    dv_before, dv_header = parted(dv_slots, y, zh)
+    dv_header, dv_sent = parted(dv_slots, zh)
+    dv_sent = after(dv_sent, crossed)
+    dv_other = lax.ppermute(dv_sent, "zh", SWAP)
 
     part = jnp.dot(
-        after(crossed, dv_before, dv_header), weight, preferred_element_type=F32
+        after(crossed, dv_sent), weight, preferred_element_type=F32
     ).reshape(4, ROWS, kv)
     values = block_at(part, x)
-    for step in (1, 2, 3):
-        sent = block_at(part, (x + step) % 4).astype(BF)
-        values = values + lax.ppermute(sent, "x", turned(4, step)).astype(F32)
+    sends = [block_at(part, (x + step) % 4).astype(BF) for step in (1, 2, 3)]
+    v_terms = [
+        lax.ppermute(sent, "x", turned(4, step)) for step, sent in zip((1, 2, 3), sends)
+    ]
+
+    (dv_other,) = held([dv_other], sends)
+    dv_own, dv_before, dv_header = joined(dv_slots, dv_header, dv_other, y, zh)
+    dv_got = returned(dv_before, dv_header)
+
+    for term in held(v_terms, [dv_before, dv_header]):
+        values = values + term.astype(F32)
     values = values.astype(BF)
-    v_other, v_pair = paired(values, zh)
-
-    value_grad = collected(dv_slots, dv_before, dv_header, y, zh).astype(BF)
-
-    v_slots = spread(values, v_other, after(v_pair, value_grad), y, zh)
-
-    near = [value_grad] + [lax.ppermute(value_grad, "x", turned(4, n)) for n in (1, 2, 3)]
-    gathered = jnp.concatenate(
-        [
-            jnp.where(
-                x == i,
-                near[0],
-                jnp.where(
-                    x == (i + 1) % 4, near[1], jnp.where(x == (i + 2) % 4, near[2], near[3])
-                ),
-            )
-            for i in range(4)
-        ]
-    )
-    term = lax.dot_general(
-        crossed, gathered, (((0,), (0,)), ((), ())), preferred_element_type=F32
-    ).reshape(2, 2, each, kv)
-    kept = lax.dynamic_index_in_dim(term, c, 1, keepdims=False)
-    given = lax.dynamic_index_in_dim(term, 1 - c, 1, keepdims=False).astype(BF)
-    back = lax.dot_general(
-        gathered, weight, (((1,), (1,)), ((), ())), preferred_element_type=F32
-    ).astype(BF)
-
-    term = kept + lax.ppermute(given, "c", SWAP).astype(F32)
-    term = term.reshape(2, 2, each // 2, kv)
+    v_before, v_header, v_sent = nearby(values, y, zh)
+
+    value_grad = summed(dv_own, held(dv_got, [values]), y)
+    near = turns(value_grad, "x", 4)
+    v_sent = after(v_sent, value_grad)
+    v_other = lax.ppermute(v_sent, "zh", SWAP)
+
+    near = [value_grad] + list(held(near, [v_sent]))
+    back, kept, given = grads_call(jnp.stack([x, c]), crossed, weight, near)
+    sibling_term = lax.ppermute(given, "c", SWAP)
+    quarters_of = (2, 2, each // 2, kv)
+    kept, sibling_term = kept.reshape(quarters_of), sibling_term.reshape(quarters_of)
 
     def quarter(at):
-        return lax.dynamic_slice(term, (at % 2, at // 2, 0, 0), (1, 1, each // 2, kv))[0, 0]
-
-    own_quarter = quarter(z)
+        where = (at % 2, at // 2, 0, 0)
+        block = (1, 1, each // 2, kv)
+        mine, theirs = (lax.dynamic_slice(t, where, block)[0, 0] for t in (kept, sibling_term))
+        return mine + theirs.astype(F32)
+
+    total = quarter(z)
     quarters = [quarter((z + step) % 4).astype(BF) for step in (1, 2, 3)]
-
-    v_slots = after(v_slots, back, *quarters)
+    z_terms = [
+        lax.ppermute(sent, ("zh", "zl"), turned(4, step))
+        for step, sent in zip((1, 2, 3), quarters)
+    ]
+
+    (v_other,) = held([v_other], quarters)
+    v_slots = placed(values, v_before, v_header, v_other, zh)
     dq, dk_slots = scores_call(q, k_slots, g, v_slots, probs)
-    dk_before, dk_header = parted(dk_slots, y, zh)
-
-    total = own_quarter
-    for step, sent in zip((1, 2, 3), quarters):
-        total = total + lax.ppermute(sent, ("zh", "zl"), turned(4, step)).astype(F32)
+
+    for term in z_terms:
+        total = total + term.astype(F32)
     mine = total.astype(BF)
-    first, second, third = (lax.ppermute(mine, "y", turned(4, n)).astype(F32) for n in (1, 2, 3))
+    dk_header, dk_sent = parted(dk_slots, zh)
+    dk_other = lax.ppermute(dk_sent, "zh", SWAP)
+
+    terms = turns(mine, "y", 4)
+    first, second, third = (term.astype(F32) for term in terms)
     total = ((mine.astype(F32) + second) + (first + third)).astype(BF)
     other = lax.ppermute(total, "zh", SWAP)
+
+    dk_own, dk_before, dk_header = joined(dk_slots, dk_header, dk_other, y, zh)
+    dk_got = returned(dk_before, dk_header)
+    (other,) = held([other], [dk_before, dk_header])
     grad_weight = jnp.where(
         zh == 0, jnp.concatenate([total, other]), jnp.concatenate([other, total])
     ).astype(F32)
@@ -288,7 +351,7 @@
         [back[i][:, p * two : (p + 1) * two] for p in range(2) for i in range(4)], axis=1
     )
 
-    key_grad = collected(dk_slots, dk_before, dk_header, y, zh).astype(BF)
+    key_grad = summed(dk_own, dk_got, y)
     return dq[None], key_grad[None], grad_input[None], grad_weight
 
 

time: 123 us -> 114 us (0.927)
  local copies, waits for them, and re-layouts: 12.5 us -> 3.37 us
  Pallas kernels: 11.6 us -> 17.4 us
  matrix products: 5.39 us -> 0.84 us
  waiting for transfers between devices: 19.4 us -> 16.9 us
  starting transfers between devices: 58.6 us -> 60.1 us
    unnamed x37 -> x41, local copies, waits for them, and re-layouts: 6.98 us -> 0.26 us
    dot_general x3 -> x1, matrix products: 5.39 us -> 0.84 us  [on_device(): jnp.dot(after(crossed, dv_sent), weight, preferred_element_type=F32)]
    all_to_all x1, waiting for transfers between devices: 0.01 us -> 4.26 us  [on_device(): lax.all_to_all(after(by_x, k_sent), 'x', 0, 0).reshape(4 * ROWS, 4 * each)]
    pallas_call x0 -> x1, Pallas kernels: none -> 3.6 us  [grads_call(): pl.pallas_call(grads_kernel, grid_spec=pltpu.PrefetchScalarGridSpec(num_s...]
    ppermute x29, waiting for transfers between devices: 14.8 us -> 11.9 us  [the longest x12 3.66 us: turns(): return [lax.ppermute(value, axis, turned(count, n)) for n in steps]]
    add x5 -> x0, other arithmetic: 2.61 us -> none  [the longest x1 1.88 us: on_device(): term = kept + lax.ppermute(given, 'c', SWAP).astype(F32)]
    ppermute x1, waiting for transfers between devices: 3.35 us -> 0.78 us  [on_device(): other = lax.ppermute(total, 'zh', SWAP)]
    convert_element_type x7 -> x6, other arithmetic: 1.08 us -> 3.6 us  [the longest x1 1.97 us: on_device(): quarters = [quarter((z + step) % 4).astype(BF) for step in (1, 2, 3)]]
  transfers between devices with their start and end apart: 34 -> 34, of which waited for: 11 -> 9; matrix products, arithmetic and copies ran while one was open for 19% -> 14% of each run, Pallas kernels for 9% -> 12%
where the time goes in v3:
time: 114 us
  starting transfers between devices  60.1 us (53%)
  Pallas kernels  17.4 us (15%)
  waiting for transfers between devices  16.9 us (15%)
  other arithmetic  14 us (12%)
  local copies, waits for them, and re-layouts  3.37 us (3%)
  between operations  1.15 us (1%)
    ppermute x12, starting transfers between devices, turns(): return [lax.ppermute(value, axis, turned(count, n)) for n in steps]  20.5 us
    pallas_call x1, Pallas kernels, scores_call(): pl.pallas_call(scores_kernel, grid=(KEY_HEADS,), in_specs=[column(ROWS, G...  7.38 us
    pallas_call x1, Pallas kernels, probs_call(): pl.pallas_call(probs_kernel, grid=(KEY_HEADS,), in_specs=[column(ROWS, GR...  6.44 us
    ppermute x3, starting transfers between devices, on_device(): lax.ppermute(sent, ('zh', 'zl'), turned(4, step))  5.53 us
    ppermute x2, starting transfers between devices, returned(): lax.ppermute(before, 'y', turned(4, 3))  5.32 us
    all_to_all x1, starting transfers between devices, on_device(): back = lax.all_to_all(back.reshape(4, ROWS, 4 * each), 'x', 0, 0)  5.14 us
    all_to_all x1, starting transfers between devices, on_device(): lax.all_to_all(after(by_x, k_sent), 'x', 0, 0).reshape(4 * ROWS, 4 * each)  4.96 us
    all_to_all x1, waiting for transfers between devices, on_device(): lax.all_to_all(after(by_x, k_sent), 'x', 0, 0).reshape(4 * ROWS, 4 * each)  4.26 us
  transfers between devices with their start and end apart: 34, of which 9 were waited for; matrix products, arithmetic and copies ran while one was open for 14% of the time, Pallas kernels for 12%

profile of v3, /device:TPU:2, one launch (start us, length us, event | category | flops | bytes accessed | tf_op | source)
XLA Modules:
  0.0 113.8 jit_solution(7956373592776032634)
XLA Ops:
  0.6 1.6 %collective-permute-start = (bf16[128,512]{1,0:T(8,128)(2,1)}, bf16[128,512]{1,0:T(8,128)(2,1)S(1)}, u32[]{:S(2)}, u32[]{:S(2)}) collective-permute-start(bf16[128,512]{1,0:T(8,128)(2,1)} %bitcast.91), channel_id=1, source_target_pairs={{0,32},{32,64},{64,96},{96,0},{1,33},{33,65},{65,97},{97,1},{2,34}... | collective-permute-start | bytes 393224 | tf_op jit(solution)/shard_map/ppermute | solution.py:197
  2.3 2.9 %collective-permute-start.1 = (bf16[128,512]{1,0:T(8,128)(2,1)}, bf16[128,512]{1,0:T(8,128)(2,1)S(1)}, u32[]{:S(2)}, u32[]{:S(2)}) collective-permute-start(bf16[128,512]{1,0:T(8,128)(2,1)} %bitcast.92), channel_id=1, source_target_pairs={{0,64},{32,96},{64,0},{96,32},{1,65},{33,97},{65,1},{97,33},{2,66}... | collective-permute-start | bytes 393224 | tf_op jit(solution)/shard_map/ppermute | solution.py:197
  5.2 1.3 %collective-permute-start.2 = (bf16[128,512]{1,0:T(8,128)(2,1)}, bf16[128,512]{1,0:T(8,128)(2,1)S(1)}, u32[]{:S(2)}, u32[]{:S(2)}) collective-permute-start(bf16[128,512]{1,0:T(8,128)(2,1)} %bitcast.93), channel_id=1, source_target_pairs={{0,96},{32,0},{64,32},{96,64},{1,97},{33,1},{65,33},{97,65},{2,98}... | collective-permute-start | bytes 393224 | tf_op jit(solution)/shard_map/ppermute | solution.py:197
  6.5 1.9 %collective-permute-start.4 = (bf16[320,512]{1,0:T(8,128)(2,1)}, bf16[320,512]{1,0:T(8,128)(2,1)S(1)}, u32[]{:S(2)}, u32[]{:S(2)}) collective-permute-start(bf16[320,512]{1,0:T(8,128)(2,1)} %param.9), channel_id=1, source_target_pairs={{0,8},{8,0},{1,9},{9,1},{2,10},{10,2},{3,11},{11,3},{4,12},{12,4},... | collective-permute-start | bytes 983048 | tf_op jit(solution)/shard_map/ppermute | solution.py:270
  8.4 0.7 compare_reduce_fusion
  9.1 0.7 fusion.37
  9.8 1.5 %fusion.41 = (bf16[128,640]{1,0:T(8,128)(2,1)S(1)}, bf16[128,640]{1,0:T(8,128)(2,1)S(1)}, bf16[128,640]{1,0:T(8,128)(2,1)S(1)}, bf16[128,640]{1,0:T(8,128)(2,1)S...) fusion(bf16[128,5120]{1,0:T(8,128)(2,1)} %bitcast.82), kind=kLoop, calls=%fused_computation.107 | loop fusion | bytes 2621440 | tf_op jit(solution)/shard_map/slice | solution.py:263
  11.6 1.2 %pad_maximum_fusion = bf16[4,128,1280]{2,1,0:T(8,128)(2,1)} fusion(bf16[1,128,1280]{2,1,0:T(8,128)(2,1)S(1)} %get-tuple-element.93, bf16[1,128,1280]{2,1,0:T(8,128)(2,1)S(1)} %get-tuple-element.92, bf16[1,128,1280]{2,1,0:T(8,128)(2,1)S(1)} %get-tuple-element.91, bf16[1,128,1280]{2,1,0:T(8,128)(2,1)S(1)} %get-tuple-element.90), kind=kLoop, calls=%fused_computation | loop fusion | flops 1966080 | bytes 2621440 | tf_op jit(solution)/shard_map/stack | solution.py:260
  13.2 3.7 %collective-permute-start.3 = (bf16[256,512]{1,0:T(8,128)(2,1)S(1)}, bf16[256,512]{1,0:T(8,128)(2,1)S(1)}, u32[]{:S(2)}, u32[]{:S(2)}) collective-permute-start(bf16[256,512]{1,0:T(8,128)(2,1)S(1)} %pad_maximum_fusion.1), channel_id=1, source_target_pairs={{0,16},{16,0},{1,17},{17,1},{2,18},{18,2},{3,19},{19,3},{4,20},{20... | collective-permute-start | bytes 786440 | tf_op jit(solution)/shard_map/ppermute | solution.py:257
  17.0 5.0 %all-to-all-start = ((bf16[4,128,1280]{2,1,0:T(8,128)(2,1)}), bf16[4,128,1280]{2,1,0:T(8,128)(2,1)S(1)}, u32[]{:S(2)}, u32[]{:S(2)}) async-start(bf16[4,128,1280]{2,1,0:T(8,128)(2,1)} %pad_maximum_fusion), calls=%async_computation | async-start | bytes 2621440 | tf_op jit(solution)/shard_map/all_to_all | solution.py:269
  22.3 2.1 %collective-permute-done.3 = bf16[256,512]{1,0:T(8,128)(2,1)S(1)} collective-permute-done((bf16[256,512]{1,0:T(8,128)(2,1)S(1)}, bf16[256,512]{1,0:T(8,128)(2,1)S(1)}, u32[]{:S(2)}, u32[]{:S(2)}) %collective-permute-start.3) | collective-permute-done | bytes 262176 | tf_op jit(solution)/shard_map/ppermute | solution.py:257
  24.6 6.4 %probs.1 = (bf16[4,512,1024]{2,1,0:T(8,128)(2,1)}, f32[512,512]{1,0:T(8,128)S(1)}) custom-call(bf16[128,4096]{1,0:T(8,128)(2,1)S(1)} %bitcast.79, bf16[512,512]{1,0:T(8,128)(2,1)S(1)} %constant_dynamic-update-slice_fusion.k_ref, bf16[128,4096]{1,0:T(8,128)(2,1)S(1)} %bitcast.81, f32[512,128]{1,0:T(8,128)S(1)} %add_select_fusion.bias_ref), custom_call_target="tpu_custom_call" | custom-call | flops 1073741824 | bytes 8388608 | tf_op jit(solution)/shard_map/probs/pallas_call | solution.py:68
  31.0 0.7 fusion.44
  31.8 0.7 pad_maximum_fusion.2
  32.7 4.3 %all-to-all-done = bf16[4,128,1280]{2,1,0:T(8,128)(2,1)S(1)} async-done(((bf16[4,128,1280]{2,1,0:T(8,128)(2,1)}), bf16[4,128,1280]{2,1,0:T(8,128)(2,1)S(1)}, u32[]{:S(2)}, u32[]{:S(2)}) %all-to-all-start) | async-done | bytes 1310752 | tf_op jit(solution)/shard_map/all_to_all | solution.py:269
  37.3 0.8 fusion.48
  38.3 3.5 %collective-permute-start.7 = (bf16[128,512]{1,0:T(8,128)(2,1)S(1)}, bf16[128,512]{1,0:T(8,128)(2,1)S(1)}, u32[]{:S(2)}, u32[]{:S(2)}) collective-permute-start(bf16[128,512]{1,0:T(8,128)(2,1)S(1)} %get-tuple-element.78), channel_id=1, source_target_pairs={{0,4},{2,6},{4,0},{6,2},{1,5},{3,7},{5,1},{7,3},{8,12},{10,14},{12... | collective-permute-start | bytes 393224 | tf_op jit(solution)/shard_map/ppermute | solution.py:291
  42.4 2.5 %collective-permute-done.9 = bf16[256,512]{1,0:T(8,128)(2,1)S(1)} collective-permute-done((bf16[256,512]{1,0:T(8,128)(2,1)S(1)}, bf16[256,512]{1,0:T(8,128)(2,1)S(1)}, u32[]{:S(2)}, u32[]{:S(2)}) %collective-permute-start.9) | collective-permute-done | bytes 262176 | tf_op jit(solution)/shard_map/ppermute | solution.py:283
  44.9 1.2 %collective-permute-start.14 = (bf16[128,512]{1,0:T(8,128)(2,1)S(1)}, bf16[128,512]{1,0:T(8,128)(2,1)S(1)}, u32[]{:S(2)}, u32[]{:S(2)}) collective-permute-start(bf16[128,512]{1,0:T(8,128)(2,1)S(1)} %get-tuple-element.52), channel_id=1, source_target_pairs={{0,64},{32,96},{64,0},{96,32},{1,65},{33,97},{65,1},{97,33},{2,66}... | collective-permute-start | bytes 393224 | tf_op jit(solution)/shard_map/ppermute | solution.py:237
  46.1 1.0 collective-permute-start.15
  47.1 2.3 %collective-permute-start.13 = (bf16[128,512]{1,0:T(8,128)(2,1)S(1)}, bf16[128,512]{1,0:T(8,128)(2,1)S(1)}, u32[]{:S(2)}, u32[]{:S(2)}) collective-permute-start(bf16[128,512]{1,0:T(8,128)(2,1)S(1)} %fusion.10), channel_id=1, source_target_pairs={{0,96},{32,0},{64,32},{96,64},{1,97},{33,1},{65,33},{97,65},{2,98}... | collective-permute-start | bytes 393224 | tf_op jit(solution)/shard_map/ppermute | solution.py:236
  49.6 2.5 %collective-permute-start.11 = (bf16[128,512]{1,0:T(8,128)(2,1)S(1)}, bf16[128,512]{1,0:T(8,128)(2,1)S(1)}, u32[]{:S(2)}, u32[]{:S(2)}) collective-permute-start(bf16[128,512]{1,0:T(8,128)(2,1)S(1)} %fusion.26), channel_id=1, source_target_pairs={{0,64},{32,96},{64,0},{96,32},{1,65},{33,97},{65,1},{97,33},{2,66}... | collective-permute-start | bytes 393224 | tf_op jit(solution)/shard_map/ppermute | solution.py:197
  52.1 1.5 %collective-permute-done.13 = bf16[128,512]{1,0:T(8,128)(2,1)S(1)} collective-permute-done((bf16[128,512]{1,0:T(8,128)(2,1)S(1)}, bf16[128,512]{1,0:T(8,128)(2,1)S(1)}, u32[]{:S(2)}, u32[]{:S(2)}) %collective-permute-start.13) | collective-permute-done | bytes 131104 | tf_op jit(solution)/shard_map/ppermute | solution.py:236
  53.7 3.3 %collective-permute-start.12 = (bf16[128,512]{1,0:T(8,128)(2,1)S(1)}, bf16[128,512]{1,0:T(8,128)(2,1)S(1)}, u32[]{:S(2)}, u32[]{:S(2)}) collective-permute-start(bf16[128,512]{1,0:T(8,128)(2,1)S(1)} %fusion.26), channel_id=1, source_target_pairs={{0,96},{32,0},{64,32},{96,64},{1,97},{33,1},{65,33},{97,65},{2,98}... | collective-permute-start | bytes 393224 | tf_op jit(solution)/shard_map/ppermute | solution.py:197
  57.4 3.3 %collective-permute-start.18 = (bf16[128,512]{1,0:T(8,128)(2,1)S(1)}, bf16[128,512]{1,0:T(8,128)(2,1)S(1)}, u32[]{:S(2)}, u32[]{:S(2)}) collective-permute-start(bf16[128,512]{1,0:T(8,128)(2,1)S(1)} %fusion.15.refs_0_), channel_id=1, source_target_pairs={{0,4},{2,6},{4,0},{6,2},{1,5},{3,7},{5,1},{7,3},{8,12},{10,14},{12... | collective-permute-start | bytes 393224 | tf_op jit(solution)/shard_map/ppermute | solution.py:197
  61.4 0.7 pad_maximum_fusion.3
  62.2 1.7 %collective-permute-done.18.refs_2_ = bf16[128,512]{1,0:T(8,128)(2,1)S(1)} collective-permute-done((bf16[128,512]{1,0:T(8,128)(2,1)S(1)}, bf16[128,512]{1,0:T(8,128)(2,1)S(1)}, u32[]{:S(2)}, u32[]{:S(2)}) %collective-permute-start.18) | collective-permute-done | bytes 131104 | tf_op jit(solution)/shard_map/ppermute | solution.py:197
  63.9 1.8 %collective-permute-done.19.refs_3_ = bf16[128,512]{1,0:T(8,128)(2,1)S(1)} collective-permute-done((bf16[128,512]{1,0:T(8,128)(2,1)S(1)}, bf16[128,512]{1,0:T(8,128)(2,1)S(1)}, u32[]{:S(2)}, u32[]{:S(2)}) %collective-permute-start.19) | collective-permute-done | bytes 131104 | tf_op jit(solution)/shard_map/ppermute | solution.py:197
  65.7 3.6 %grads.1 = (bf16[512,1280]{1,0:T(8,128)(2,1)}, f32[2,320,512]{2,1,0:T(8,128)}, bf16[2,320,512]{2,1,0:T(8,128)(2,1)}) custom-call(s32[2]{0:T(128)S(1)} %pad_add_fusion.at_ref, bf16[512,1280]{1,0:T(8,128)(2,1)S(1)} %bitcast.75, bf16[1280,512]{1,0:T(8,128)(2,1)S(1)} %bitcast.77, bf16[128,512]{1,0:T(8,128)(2,1)S(1)} %fusion.15.refs_0_, ...), custom_call_target="tpu_custom_call" | custom-call | flops 1342177280 | bytes 8388608 | tf_op jit(solution)/shard_map/grads/pallas_call | solution.py:154
  69.3 0.9 collective-permute-start.16
  70.2 5.1 %all-to-all-start.1 = ((bf16[4,128,1280]{2,1,0:T(8,128)(2,1)}), bf16[4,128,1280]{2,1,0:T(8,128)(2,1)S(1)}, u32[]{:S(2)}, u32[]{:S(2)}) async-start(bf16[4,128,1280]{2,1,0:T(8,128)(2,1)} %bitcast.83), calls=%async_computation.1 | async-start | bytes 2621440 | tf_op jit(solution)/shard_map/all_to_all | solution.py:349
  75.4 2.0 %fusion.29 = (bf16[160,512]{1,0:T(8,128)(2,1)}, bf16[160,512]{1,0:T(8,128)(2,1)}, bf16[160,512]{1,0:T(8,128)(2,1)}) fusion(f32[2,2,160,512]{3,2,1,0:T(8,128)S(1)} %bitcast.85, s32[]{:T(128)S(6)} %select_n.328, s32[]{:T(128)S(6)} %select_n.330, bf16[2,2,160,512]{3,2,1,0:T(8,128)(2,1)} %bitcast.26, s32[]{:T(128)S(6)} %select_n.323, s32[]{:T(128)S(6)} %select_n.325, ...), kind=kLoop, calls=%fused_computation.66 | loop fusion | flops 737280 | bytes 1966104 | tf_op jit(solution)/shard_map/convert_element_type | solution.py:321
  77.4 1.0 collective-permute-start.25
  78.4 3.5 %collective-permute-start.26 = (bf16[160,512]{1,0:T(8,128)(2,1)}, bf16[160,512]{1,0:T(8,128)(2,1)}, u32[]{:S(2)}, u32[]{:S(2)}) collective-permute-start(bf16[160,512]{1,0:T(8,128)(2,1)} %get-tuple-element.57), channel_id=1, source_target_pairs={{0,16},{8,24},{16,0},{24,8},{1,17},{9,25},{17,1},{25,9},{2,18},{10... | collective-permute-start | bytes 491528 | tf_op jit(solution)/shard_map/ppermute | solution.py:323
  81.9 1.0 collective-permute-start.27
  83.0 7.4 %scores.1 = (bf16[128,4096]{1,0:T(8,128)(2,1)}, f32[512,512]{1,0:T(8,128)S(1)}) custom-call(bf16[128,4096]{1,0:T(8,128)(2,1)} %bitcast.78, bf16[512,512]{1,0:T(8,128)(2,1)S(1)} %constant_dynamic-update-slice_fusion.k_ref, bf16[128,4096]{1,0:T(8,128)(2,1)} %bitcast.80, bf16[512,512]{1,0:T(8,128)(2,1)S(1)} %constant_dynamic-update-slice_fusion.1.v_ref, ...), custom_call_target="tpu_custom_call" | custom-call | flops 1610612736 | bytes 8388608 | tf_op jit(solution)/shard_map/scores/pallas_call | solution.py:94
  90.5 0.7 collective-permute-start.21
  91.2 1.3 %fusion.3 = bf16[160,512]{1,0:T(8,128)(2,1)S(1)} fusion(bf16[160,512]{1,0:T(8,128)(2,1)} %collective-permute-done.27, bf16[160,512]{1,0:T(8,128)(2,1)} %collective-permute-done.26, bf16[160,512]{1,0:T(8,128)(2,1)} %collective-permute-done.25, f32[2,2,160,512]{3,2,1,0:T(8,128)} %bitcast.84, s32[]{:T(128)S(6)} %select_n.342, s32[]{:T(128)S(6)} %select_n.344, ...), kind=kLoop, calls=%fused_computation.21 | loop fusion | flops 737280 | bytes 1146888 | tf_op jit(solution)/shard_map/convert_element_type | solution.py:333
  92.6 1.3 %collective-permute-start.28 = (bf16[160,512]{1,0:T(8,128)(2,1)S(1)}, bf16[160,512]{1,0:T(8,128)(2,1)S(1)}, u32[]{:S(2)}, u32[]{:S(2)}) collective-permute-start(bf16[160,512]{1,0:T(8,128)(2,1)S(1)} %fusion.3), channel_id=1, source_target_pairs={{0,64},{32,96},{64,0},{96,32},{1,65},{33,97},{65,1},{97,33},{2,66}... | collective-permute-start | bytes 491528 | tf_op jit(solution)/shard_map/ppermute | solution.py:197
  93.8 3.2 %collective-permute-start.30 = (bf16[160,512]{1,0:T(8,128)(2,1)S(1)}, bf16[160,512]{1,0:T(8,128)(2,1)S(1)}, u32[]{:S(2)}, u32[]{:S(2)}) collective-permute-start(bf16[160,512]{1,0:T(8,128)(2,1)S(1)} %fusion.3), channel_id=1, source_target_pairs={{0,96},{32,0},{64,32},{96,64},{1,97},{33,1},{65,33},{97,65},{2,98}... | collective-permute-start | bytes 491528 | tf_op jit(solution)/shard_map/ppermute | solution.py:197
  97.1 2.1 %collective-permute-done.21 = bf16[256,512]{1,0:T(8,128)(2,1)S(1)} collective-permute-done((bf16[256,512]{1,0:T(8,128)(2,1)S(1)}, bf16[256,512]{1,0:T(8,128)(2,1)S(1)}, u32[]{:S(2)}, u32[]{:S(2)}) %collective-permute-start.21) | collective-permute-done | bytes 262176 | tf_op jit(solution)/shard_map/ppermute | solution.py:335
  99.1 0.7 fusion.23
  99.9 0.7 convert_element_type.175
  101.4 3.0 %collective-permute-start.22 = (bf16[128,512]{1,0:T(8,128)(2,1)}, bf16[128,512]{1,0:T(8,128)(2,1)}, u32[]{:S(2)}, u32[]{:S(2)}) collective-permute-start(bf16[128,512]{1,0:T(8,128)(2,1)} %get-tuple-element.50), channel_id=1, source_target_pairs={{0,96},{32,0},{64,32},{96,64},{1,97},{33,1},{65,33},{97,65},{2,98}... | collective-permute-start | bytes 393224 | tf_op jit(solution)/shard_map/ppermute | solution.py:236
  104.5 3.9 %collective-permute-start.31 = (bf16[160,512]{1,0:T(8,128)(2,1)S(1)}, bf16[160,512]{1,0:T(8,128)(2,1)}, u32[]{:S(2)}, u32[]{:S(2)}) collective-permute-start(bf16[160,512]{1,0:T(8,128)(2,1)S(1)} %add_convert_fusion), channel_id=1, source_target_pairs={{0,16},{16,0},{1,17},{17,1},{2,18},{18,2},{3,19},{19,3},{4,20},{20... | collective-permute-start | bytes 491528 | tf_op jit(solution)/shard_map/ppermute | solution.py:340
  108.8 2.3 %fusion.33 = bf16[1,128,512]{2,1,0:T(8,128)(2,1)} fusion(bf16[128,512]{1,0:T(8,128)(2,1)} %collective-permute-done.24, bf16[128,512]{1,0:T(8,128)(2,1)} %collective-permute-done.23, bf16[128,512]{1,0:T(8,128)(2,1)} %collective-permute-done.22, f32[128,512]{1,0:T(8,128)S(1)} %get-tuple-element.51, f32[512,512]{1,0:T(8,128)S(1)} %get-tuple-element.47, ...), kind=kLoop, calls=%fused_computation.85 | loop fusion | flops 851968 | bytes 1179650 | tf_op jit(solution)/shard_map/broadcast_in_dim | solution.py:355
  111.1 0.8 collective-permute-done.31
  111.9 1.9 %fusion = f32[320,512]{1,0:T(8,128)} fusion(bf16[160,512]{1,0:T(8,128)(2,1)} %collective-permute-done.31, bf16[160,512]{1,0:T(8,128)(2,1)S(1)} %add_convert_fusion, pred[]{:T(512)S(6)} %eq.83), kind=kLoop, calls=%fused_computation.17 | loop fusion | flops 1638400 | bytes 983041 | tf_op jit(solution)/shard_map/convert_element_type | solution.py:347
  (111 shorter events, 5.1 us)
Async XLA Ops:
  0.6 12.5 %collective-permute-start = (bf16[128,512]{1,0:T(8,128)(2,1)}, bf16[128,512]{1,0:T(8,128)(2,1)S(1)}, u32[]{:S(2)}, u32[]{:S(2)}) collective-permute-start(bf16[128,512]{1,0:T(8,128)(2,1)} %bitcast.91), channel_id=1, source_target_pairs={{0,32},{32,64},{64,96},{96,0},{1,33},{33,65},{65,97},{97,1},{2,34}... | collective-permute-start | bytes 393224 | tf_op jit(solution)/shard_map/ppermute | solution.py:197
  2.3 10.9 %collective-permute-start.1 = (bf16[128,512]{1,0:T(8,128)(2,1)}, bf16[128,512]{1,0:T(8,128)(2,1)S(1)}, u32[]{:S(2)}, u32[]{:S(2)}) collective-permute-start(bf16[128,512]{1,0:T(8,128)(2,1)} %bitcast.92), channel_id=1, source_target_pairs={{0,64},{32,96},{64,0},{96,32},{1,65},{33,97},{65,1},{97,33},{2,66}... | collective-permute-start | bytes 393224 | tf_op jit(solution)/shard_map/ppermute | solution.py:197
  5.2 8.0 %collective-permute-start.2 = (bf16[128,512]{1,0:T(8,128)(2,1)}, bf16[128,512]{1,0:T(8,128)(2,1)S(1)}, u32[]{:S(2)}, u32[]{:S(2)}) collective-permute-start(bf16[128,512]{1,0:T(8,128)(2,1)} %bitcast.93), channel_id=1, source_target_pairs={{0,96},{32,0},{64,32},{96,64},{1,97},{33,1},{65,33},{97,65},{2,98}... | collective-permute-start | bytes 393224 | tf_op jit(solution)/shard_map/ppermute | solution.py:197
  6.5 15.4 %collective-permute-start.4 = (bf16[320,512]{1,0:T(8,128)(2,1)}, bf16[320,512]{1,0:T(8,128)(2,1)S(1)}, u32[]{:S(2)}, u32[]{:S(2)}) collective-permute-start(bf16[320,512]{1,0:T(8,128)(2,1)} %param.9), channel_id=1, source_target_pairs={{0,8},{8,0},{1,9},{9,1},{2,10},{10,2},{3,11},{11,3},{4,12},{12,4},... | collective-permute-start | bytes 983048 | tf_op jit(solution)/shard_map/ppermute | solution.py:270
  9.8 1.5 %copy-start.14 = (s32[1,1024]{1,0:T(1,128)S(1)}, s32[1,1024]{1,0:T(1,128)}, u32[]{:S(2)}) copy-start(s32[1,1024]{1,0:T(1,128)} %param.11) | copy-start | bytes 12292
  11.5 1.6 %copy-start.9 = (bf16[1,128,512]{2,1,0:T(8,128)(2,1)S(1)}, bf16[1,128,512]{2,1,0:T(8,128)(2,1)}, u32[]{:S(2)}) copy-start(bf16[1,128,512]{2,1,0:T(8,128)(2,1)} %param.8) | copy-start | bytes 393220
  13.2 11.2 %collective-permute-start.3 = (bf16[256,512]{1,0:T(8,128)(2,1)S(1)}, bf16[256,512]{1,0:T(8,128)(2,1)S(1)}, u32[]{:S(2)}, u32[]{:S(2)}) collective-permute-start(bf16[256,512]{1,0:T(8,128)(2,1)S(1)} %pad_maximum_fusion.1), channel_id=1, source_target_pairs={{0,16},{16,0},{1,17},{17,1},{2,18},{18,2},{3,19},{19,3},{4,20},{20... | collective-permute-start | bytes 786440 | tf_op jit(solution)/shard_map/ppermute | solution.py:257
  17.0 5.0 %copy-start.5 = (bf16[320,512]{1,0:T(8,128)(2,1)S(1)}, bf16[320,512]{1,0:T(8,128)(2,1)}, u32[]{:S(2)}) copy-start(bf16[320,512]{1,0:T(8,128)(2,1)} %param.9) | copy-start | bytes 983044
  17.0 20.0 %all-to-all-start = ((bf16[4,128,1280]{2,1,0:T(8,128)(2,1)}), bf16[4,128,1280]{2,1,0:T(8,128)(2,1)S(1)}, u32[]{:S(2)}, u32[]{:S(2)}) async-start(bf16[4,128,1280]{2,1,0:T(8,128)(2,1)} %pad_maximum_fusion), calls=%async_computation | async-start | bytes 2621440 | tf_op jit(solution)/shard_map/all_to_all | solution.py:269
  22.1 10.5 %collective-permute-start.5 = (bf16[2,320,512]{2,1,0:T(8,128)(2,1)S(1)}, bf16[2,320,512]{2,1,0:T(8,128)(2,1)S(1)}, u32[]{:S(2)}, u32[]{:S(2)}) collective-permute-start(bf16[2,320,512]{2,1,0:T(8,128)(2,1)S(1)} %maximum_select_fusion.2), channel_id=1, source_target_pairs={{0,1},{1,0},{2,3},{3,2},{4,5},{5,4},{6,7},{7,6},{8,9},{9,8},{10,11... | collective-permute-start | bytes 1966088 | tf_op jit(solution)/shard_map/ppermute | solution.py:274
  22.2 2.4 %copy-start = (bf16[1,128,4096]{2,1,0:T(8,128)(2,1)S(1)}, bf16[1,128,4096]{2,1,0:T(8,128)(2,1)}, u32[]{:S(2)}) copy-start(bf16[1,128,4096]{2,1,0:T(8,128)(2,1)} %param.7) | copy-start | bytes 3145732
  22.2 2.4 %copy-start.1 = (bf16[1,128,4096]{2,1,0:T(8,128)(2,1)S(1)}, bf16[1,128,4096]{2,1,0:T(8,128)(2,1)}, u32[]{:S(2)}) copy-start(bf16[1,128,4096]{2,1,0:T(8,128)(2,1)} %param.10) | copy-start | bytes 3145732
  32.5 4.5 %copy-start.12 = (bf16[256,512]{1,0:T(8,128)(2,1)S(1)}, bf16[256,512]{1,0:T(8,128)(2,1)}, u32[]{:S(2)}) copy-start(bf16[256,512]{1,0:T(8,128)(2,1)} %pad_maximum_fusion.2) | copy-start | bytes 786436
  37.0 7.9 %collective-permute-start.9 = (bf16[256,512]{1,0:T(8,128)(2,1)S(1)}, bf16[256,512]{1,0:T(8,128)(2,1)S(1)}, u32[]{:S(2)}, u32[]{:S(2)}) collective-permute-start(bf16[256,512]{1,0:T(8,128)(2,1)S(1)} %copy-done.12), channel_id=1, source_target_pairs={{0,16},{16,0},{1,17},{17,1},{2,18},{18,2},{3,19},{19,3},{4,20},{20... | collective-permute-start | bytes 786440 | tf_op jit(solution)/shard_map/ppermute | solution.py:283
  37.3 7.6 %copy-start.3 = (f32[512,512]{1,0:T(8,128)S(1)}, f32[512,512]{1,0:T(8,128)}, u32[]{:S(2)}) copy-start(f32[512,512]{1,0:T(8,128)} %copy-done.2) | copy-start | bytes 3145732
  38.1 8.9 %copy-start.8 = (f32[64,512]{1,0:T(8,128)S(1)}, f32[64,512]{1,0:T(8,128)}, u32[]{:S(2)}) copy-start(f32[64,512]{1,0:T(8,128)} %get-tuple-element.75) | copy-start | bytes 393220
  38.2 8.9 %collective-permute-start.6 = (bf16[128,512]{1,0:T(8,128)(2,1)S(1)}, bf16[128,512]{1,0:T(8,128)(2,1)S(1)}, u32[]{:S(2)}, u32[]{:S(2)}) collective-permute-start(bf16[128,512]{1,0:T(8,128)(2,1)S(1)} %get-tuple-element.79), channel_id=1, source_target_pairs={{0,2},{2,4},{4,6},{6,0},{1,3},{3,5},{5,7},{7,1},{8,10},{10,12},{12... | collective-permute-start | bytes 393224 | tf_op jit(solution)/shard_map/ppermute | solution.py:291
  38.3 11.1 %collective-permute-start.7 = (bf16[128,512]{1,0:T(8,128)(2,1)S(1)}, bf16[128,512]{1,0:T(8,128)(2,1)S(1)}, u32[]{:S(2)}, u32[]{:S(2)}) collective-permute-start(bf16[128,512]{1,0:T(8,128)(2,1)S(1)} %get-tuple-element.78), channel_id=1, source_target_pairs={{0,4},{2,6},{4,0},{6,2},{1,5},{3,7},{5,1},{7,3},{8,12},{10,14},{12... | collective-permute-start | bytes 393224 | tf_op jit(solution)/shard_map/ppermute | solution.py:291
  41.8 7.6 %collective-permute-start.8 = (bf16[128,512]{1,0:T(8,128)(2,1)S(1)}, bf16[128,512]{1,0:T(8,128)(2,1)S(1)}, u32[]{:S(2)}, u32[]{:S(2)}) collective-permute-start(bf16[128,512]{1,0:T(8,128)(2,1)S(1)} %get-tuple-element.77), channel_id=1, source_target_pairs={{0,6},{2,0},{4,2},{6,4},{1,7},{3,1},{5,3},{7,5},{8,14},{10,8},{12,... | collective-permute-start | bytes 393224 | tf_op jit(solution)/shard_map/ppermute | solution.py:291
  44.9 12.1 %collective-permute-start.14 = (bf16[128,512]{1,0:T(8,128)(2,1)S(1)}, bf16[128,512]{1,0:T(8,128)(2,1)S(1)}, u32[]{:S(2)}, u32[]{:S(2)}) collective-permute-start(bf16[128,512]{1,0:T(8,128)(2,1)S(1)} %get-tuple-element.52), channel_id=1, source_target_pairs={{0,64},{32,96},{64,0},{96,32},{1,65},{33,97},{65,1},{97,33},{2,66}... | collective-permute-start | bytes 393224 | tf_op jit(solution)/shard_map/ppermute | solution.py:237
  46.1 10.9 %collective-permute-start.15 = (bf16[128,512]{1,0:T(8,128)(2,1)S(1)}, bf16[128,512]{1,0:T(8,128)(2,1)S(1)}, u32[]{:S(2)}, u32[]{:S(2)}) collective-permute-start(bf16[128,512]{1,0:T(8,128)(2,1)S(1)} %get-tuple-element.52), channel_id=1, source_target_pairs={{0,32},{32,64},{64,96},{96,0},{1,33},{33,65},{65,97},{97,1},{2,34}... | collective-permute-start | bytes 393224 | tf_op jit(solution)/shard_map/ppermute | solution.py:238
  47.1 6.5 %collective-permute-start.13 = (bf16[128,512]{1,0:T(8,128)(2,1)S(1)}, bf16[128,512]{1,0:T(8,128)(2,1)S(1)}, u32[]{:S(2)}, u32[]{:S(2)}) collective-permute-start(bf16[128,512]{1,0:T(8,128)(2,1)S(1)} %fusion.10), channel_id=1, source_target_pairs={{0,96},{32,0},{64,32},{96,64},{1,97},{33,1},{65,33},{97,65},{2,98}... | collective-permute-start | bytes 393224 | tf_op jit(solution)/shard_map/ppermute | solution.py:236
  49.5 16.2 %copy-start.6 = (bf16[128,512]{1,0:T(8,128)(2,1)}, bf16[128,512]{1,0:T(8,128)(2,1)S(1)}, u32[]{:S(2)}) copy-start(bf16[128,512]{1,0:T(8,128)(2,1)S(1)} %fusion.26) | copy-start | bytes 393220
  49.5 11.2 %collective-permute-start.10 = (bf16[128,512]{1,0:T(8,128)(2,1)S(1)}, bf16[128,512]{1,0:T(8,128)(2,1)S(1)}, u32[]{:S(2)}, u32[]{:S(2)}) collective-permute-start(bf16[128,512]{1,0:T(8,128)(2,1)S(1)} %fusion.26), channel_id=1, source_target_pairs={{0,32},{32,64},{64,96},{96,0},{1,33},{33,65},{65,97},{97,1},{2,34}... | collective-permute-start | bytes 393224 | tf_op jit(solution)/shard_map/ppermute | solution.py:197
  49.6 11.7 %collective-permute-start.11 = (bf16[128,512]{1,0:T(8,128)(2,1)S(1)}, bf16[128,512]{1,0:T(8,128)(2,1)S(1)}, u32[]{:S(2)}, u32[]{:S(2)}) collective-permute-start(bf16[128,512]{1,0:T(8,128)(2,1)S(1)} %fusion.26), channel_id=1, source_target_pairs={{0,64},{32,96},{64,0},{96,32},{1,65},{33,97},{65,1},{97,33},{2,66}... | collective-permute-start | bytes 393224 | tf_op jit(solution)/shard_map/ppermute | solution.py:197
  53.7 7.7 %collective-permute-start.12 = (bf16[128,512]{1,0:T(8,128)(2,1)S(1)}, bf16[128,512]{1,0:T(8,128)(2,1)S(1)}, u32[]{:S(2)}, u32[]{:S(2)}) collective-permute-start(bf16[128,512]{1,0:T(8,128)(2,1)S(1)} %fusion.26), channel_id=1, source_target_pairs={{0,96},{32,0},{64,32},{96,64},{1,97},{33,1},{65,33},{97,65},{2,98}... | collective-permute-start | bytes 393224 | tf_op jit(solution)/shard_map/ppermute | solution.py:197
  57.2 5.0 %collective-permute-start.17 = (bf16[128,512]{1,0:T(8,128)(2,1)S(1)}, bf16[128,512]{1,0:T(8,128)(2,1)S(1)}, u32[]{:S(2)}, u32[]{:S(2)}) collective-permute-start(bf16[128,512]{1,0:T(8,128)(2,1)S(1)} %fusion.15.refs_0_), channel_id=1, source_target_pairs={{0,2},{2,4},{4,6},{6,0},{1,3},{3,5},{5,7},{7,1},{8,10},{10,12},{12... | collective-permute-start | bytes 393224 | tf_op jit(solution)/shard_map/ppermute | solution.py:197
  57.4 6.5 %collective-permute-start.18 = (bf16[128,512]{1,0:T(8,128)(2,1)S(1)}, bf16[128,512]{1,0:T(8,128)(2,1)S(1)}, u32[]{:S(2)}, u32[]{:S(2)}) collective-permute-start(bf16[128,512]{1,0:T(8,128)(2,1)S(1)} %fusion.15.refs_0_), channel_id=1, source_target_pairs={{0,4},{2,6},{4,0},{6,2},{1,5},{3,7},{5,1},{7,3},{8,12},{10,14},{12... | collective-permute-start | bytes 393224 | tf_op jit(solution)/shard_map/ppermute | solution.py:197
  60.8 5.0 %copy-start.10 = (bf16[128,512]{1,0:T(8,128)(2,1)}, bf16[128,512]{1,0:T(8,128)(2,1)S(1)}, u32[]{:S(2)}) copy-start(bf16[128,512]{1,0:T(8,128)(2,1)S(1)} %collective-permute-done.10) | copy-start | bytes 393220
  60.8 5.0 %collective-permute-start.19 = (bf16[128,512]{1,0:T(8,128)(2,1)S(1)}, bf16[128,512]{1,0:T(8,128)(2,1)S(1)}, u32[]{:S(2)}, u32[]{:S(2)}) collective-permute-start(bf16[128,512]{1,0:T(8,128)(2,1)S(1)} %fusion.15.refs_0_), channel_id=1, source_target_pairs={{0,6},{2,0},{4,2},{6,4},{1,7},{3,1},{5,3},{7,5},{8,14},{10,8},{12,... | collective-permute-start | bytes 393224 | tf_op jit(solution)/shard_map/ppermute | solution.py:197
  69.3 6.0 %collective-permute-start.20 = (bf16[2,320,512]{2,1,0:T(8,128)(2,1)}, bf16[2,320,512]{2,1,0:T(8,128)(2,1)}, u32[]{:S(2)}, u32[]{:S(2)}) collective-permute-start(bf16[2,320,512]{2,1,0:T(8,128)(2,1)} %get-tuple-element.43), channel_id=1, source_target_pairs={{0,1},{1,0},{2,3},{3,2},{4,5},{5,4},{6,7},{7,6},{8,9},{9,8},{10,11... | collective-permute-start | bytes 1966088 | tf_op jit(solution)/shard_map/ppermute | solution.py:310
  69.3 13.5 %collective-permute-start.16 = (bf16[256,512]{1,0:T(8,128)(2,1)}, bf16[256,512]{1,0:T(8,128)(2,1)S(1)}, u32[]{:S(2)}, u32[]{:S(2)}) collective-permute-start(bf16[256,512]{1,0:T(8,128)(2,1)} %pad_maximum_fusion.3), channel_id=1, source_target_pairs={{0,16},{16,0},{1,17},{17,1},{2,18},{18,2},{3,19},{19,3},{4,20},{20... | collective-permute-start | bytes 786440 | tf_op jit(solution)/shard_map/ppermute | solution.py:306
  70.2 5.2 %copy-start.4 = (f32[2,320,512]{2,1,0:T(8,128)S(1)}, f32[2,320,512]{2,1,0:T(8,128)}, u32[]{:S(2)}) copy-start(f32[2,320,512]{2,1,0:T(8,128)} %get-tuple-element.42) | copy-start | bytes 3932164
  70.2 38.2 %all-to-all-start.1 = ((bf16[4,128,1280]{2,1,0:T(8,128)(2,1)}), bf16[4,128,1280]{2,1,0:T(8,128)(2,1)S(1)}, u32[]{:S(2)}, u32[]{:S(2)}) async-start(bf16[4,128,1280]{2,1,0:T(8,128)(2,1)} %bitcast.83), calls=%async_computation.1 | async-start | bytes 2621440 | tf_op jit(solution)/shard_map/all_to_all | solution.py:349
  75.4 7.6 %copy-start.11 = (bf16[128,512]{1,0:T(8,128)(2,1)S(1)}, bf16[128,512]{1,0:T(8,128)(2,1)}, u32[]{:S(2)}) copy-start(bf16[128,512]{1,0:T(8,128)(2,1)} %copy-done.10) | copy-start | bytes 393220
  75.4 7.6 %copy-start.7 = (bf16[128,512]{1,0:T(8,128)(2,1)S(1)}, bf16[128,512]{1,0:T(8,128)(2,1)}, u32[]{:S(2)}) copy-start(bf16[128,512]{1,0:T(8,128)(2,1)} %copy-done.6) | copy-start | bytes 393220
  77.4 13.9 %collective-permute-start.25 = (bf16[160,512]{1,0:T(8,128)(2,1)}, bf16[160,512]{1,0:T(8,128)(2,1)}, u32[]{:S(2)}, u32[]{:S(2)}) collective-permute-start(bf16[160,512]{1,0:T(8,128)(2,1)} %get-tuple-element.58), channel_id=1, source_target_pairs={{0,8},{8,16},{16,24},{24,0},{1,9},{9,17},{17,25},{25,1},{2,10},{10... | collective-permute-start | bytes 491528 | tf_op jit(solution)/shard_map/ppermute | solution.py:323
  78.4 12.9 %collective-permute-start.26 = (bf16[160,512]{1,0:T(8,128)(2,1)}, bf16[160,512]{1,0:T(8,128)(2,1)}, u32[]{:S(2)}, u32[]{:S(2)}) collective-permute-start(bf16[160,512]{1,0:T(8,128)(2,1)} %get-tuple-element.57), channel_id=1, source_target_pairs={{0,16},{8,24},{16,0},{24,8},{1,17},{9,25},{17,1},{25,9},{2,18},{10... | collective-permute-start | bytes 491528 | tf_op jit(solution)/shard_map/ppermute | solution.py:323
  81.9 9.4 %collective-permute-start.27 = (bf16[160,512]{1,0:T(8,128)(2,1)}, bf16[160,512]{1,0:T(8,128)(2,1)}, u32[]{:S(2)}, u32[]{:S(2)}) collective-permute-start(bf16[160,512]{1,0:T(8,128)(2,1)} %get-tuple-element.56), channel_id=1, source_target_pairs={{0,24},{8,0},{16,8},{24,16},{1,25},{9,1},{17,9},{25,17},{2,26},{10... | collective-permute-start | bytes 491528 | tf_op jit(solution)/shard_map/ppermute | solution.py:323
  90.5 8.6 %collective-permute-start.21 = (bf16[256,512]{1,0:T(8,128)(2,1)S(1)}, bf16[256,512]{1,0:T(8,128)(2,1)S(1)}, u32[]{:S(2)}, u32[]{:S(2)}) collective-permute-start(bf16[256,512]{1,0:T(8,128)(2,1)S(1)} %pad_maximum_fusion.4), channel_id=1, source_target_pairs={{0,16},{16,0},{1,17},{17,1},{2,18},{18,2},{3,19},{19,3},{4,20},{20... | collective-permute-start | bytes 786440 | tf_op jit(solution)/shard_map/ppermute | solution.py:335
  92.6 8.8 %collective-permute-start.28 = (bf16[160,512]{1,0:T(8,128)(2,1)S(1)}, bf16[160,512]{1,0:T(8,128)(2,1)S(1)}, u32[]{:S(2)}, u32[]{:S(2)}) collective-permute-start(bf16[160,512]{1,0:T(8,128)(2,1)S(1)} %fusion.3), channel_id=1, source_target_pairs={{0,64},{32,96},{64,0},{96,32},{1,65},{33,97},{65,1},{97,33},{2,66}... | collective-permute-start | bytes 491528 | tf_op jit(solution)/shard_map/ppermute | solution.py:197
  93.8 10.6 %collective-permute-start.29 = (bf16[160,512]{1,0:T(8,128)(2,1)S(1)}, bf16[160,512]{1,0:T(8,128)(2,1)S(1)}, u32[]{:S(2)}, u32[]{:S(2)}) collective-permute-start(bf16[160,512]{1,0:T(8,128)(2,1)S(1)} %fusion.3), channel_id=1, source_target_pairs={{0,32},{32,64},{64,96},{96,0},{1,33},{33,65},{65,97},{97,1},{2,34}... | collective-permute-start | bytes 491528 | tf_op jit(solution)/shard_map/ppermute | solution.py:197
  93.8 10.6 %collective-permute-start.30 = (bf16[160,512]{1,0:T(8,128)(2,1)S(1)}, bf16[160,512]{1,0:T(8,128)(2,1)S(1)}, u32[]{:S(2)}, u32[]{:S(2)}) collective-permute-start(bf16[160,512]{1,0:T(8,128)(2,1)S(1)} %fusion.3), channel_id=1, source_target_pairs={{0,96},{32,0},{64,32},{96,64},{1,97},{33,1},{65,33},{97,65},{2,98}... | collective-permute-start | bytes 491528 | tf_op jit(solution)/shard_map/ppermute | solution.py:197
  100.5 8.3 %collective-permute-start.23 = (bf16[128,512]{1,0:T(8,128)(2,1)}, bf16[128,512]{1,0:T(8,128)(2,1)}, u32[]{:S(2)}, u32[]{:S(2)}) collective-permute-start(bf16[128,512]{1,0:T(8,128)(2,1)} %convert_element_type.175), channel_id=1, source_target_pairs={{0,64},{32,96},{64,0},{96,32},{1,65},{33,97},{65,1},{97,33},{2,66}... | collective-permute-start | bytes 393224 | tf_op jit(solution)/shard_map/ppermute | solution.py:237
  101.2 7.6 %collective-permute-start.24 = (bf16[128,512]{1,0:T(8,128)(2,1)}, bf16[128,512]{1,0:T(8,128)(2,1)}, u32[]{:S(2)}, u32[]{:S(2)}) collective-permute-start(bf16[128,512]{1,0:T(8,128)(2,1)} %convert_element_type.175), channel_id=1, source_target_pairs={{0,32},{32,64},{64,96},{96,0},{1,33},{33,65},{65,97},{97,1},{2,34}... | collective-permute-start | bytes 393224 | tf_op jit(solution)/shard_map/ppermute | solution.py:238
  101.4 7.4 %collective-permute-start.22 = (bf16[128,512]{1,0:T(8,128)(2,1)}, bf16[128,512]{1,0:T(8,128)(2,1)}, u32[]{:S(2)}, u32[]{:S(2)}) collective-permute-start(bf16[128,512]{1,0:T(8,128)(2,1)} %get-tuple-element.50), channel_id=1, source_target_pairs={{0,96},{32,0},{64,32},{96,64},{1,97},{33,1},{65,33},{97,65},{2,98}... | collective-permute-start | bytes 393224 | tf_op jit(solution)/shard_map/ppermute | solution.py:236
  104.5 7.4 %collective-permute-start.31 = (bf16[160,512]{1,0:T(8,128)(2,1)S(1)}, bf16[160,512]{1,0:T(8,128)(2,1)}, u32[]{:S(2)}, u32[]{:S(2)}) collective-permute-start(bf16[160,512]{1,0:T(8,128)(2,1)S(1)} %add_convert_fusion), channel_id=1, source_target_pairs={{0,16},{16,0},{1,17},{17,1},{2,18},{18,2},{3,19},{19,3},{4,20},{20... | collective-permute-start | bytes 491528 | tf_op jit(solution)/shard_map/ppermute | solution.py:340
  108.8 5.0 %copy-start.13 = (bf16[128,5120]{1,0:T(8,128)(2,1)}, bf16[128,5120]{1,0:T(8,128)(2,1)S(1)}, u32[]{:S(2)}) copy-start(bf16[128,5120]{1,0:T(8,128)(2,1)S(1)} %slice_dynamic-update-slice_fusion) | copy-start | bytes 3932164
  (1 other events, 1.5 us)

commit v4 on v3

--- a/solution.py
+++ b/solution.py
@@ -84,7 +84,7 @@
         ],
         compiler_params=pltpu.CompilerParams(vmem_limit_bytes=24 << 20),
         cost_estimate=pl.CostEstimate(
-            flops=4 * SLOTS * ROWS * 32 * HEAD, bytes_accessed=8 << 20, transcendentals=SLOTS * ROWS * 32
+            flops=SLOTS * ROWS, bytes_accessed=SLOTS * ROWS, transcendentals=0
         ),
         name="probs",
     )(q, k, g, bias)
@@ -276,10 +276,9 @@
         c == 0, jnp.stack([planes, sibling], 1), jnp.stack([sibling, planes], 1)
     ).reshape(4 * each, kv)
 
-    bias = slot_bias(passage_index[0], s)
+    bias = slot_bias(after(passage_index, k_sent)[0], s)
     probs, dv_slots = probs_call(q, k_slots, g, bias)
     dv_header, dv_sent = parted(dv_slots, zh)
-    dv_sent = after(dv_sent, crossed)
     dv_other = lax.ppermute(dv_sent, "zh", SWAP)
 
     part = jnp.dot(
@@ -347,6 +346,7 @@
     ).astype(F32)
 
     back = lax.all_to_all(back.reshape(4, ROWS, 4 * each), "x", 0, 0)
+    (back,) = held([back], [dk_before, dk_header, total])
     grad_input = jnp.concatenate(
         [back[i][:, p * two : (p + 1) * two] for p in range(2) for i in range(4)], axis=1
     )

time: 114 us -> 113 us (level)
  other arithmetic: 14 us -> 8.86 us
  waiting for transfers between devices: 16.9 us -> 18.8 us
  matrix products: 0.84 us -> 2.24 us
    ppermute x1, waiting for transfers between devices: 2.48 us -> 0.01 us  [on_device(): dv_other = lax.ppermute(dv_sent, 'zh', SWAP)]
    ppermute x12, waiting for transfers between devices: 3.66 us -> 5.27 us  [turns(): return [lax.ppermute(value, axis, turned(count, n)) for n in steps]]
    ppermute x1, waiting for transfers between devices: 2.06 us -> 3.48 us  [on_device(): dk_other = lax.ppermute(dk_sent, 'zh', SWAP)]
    dot_general x1, matrix products: 0.84 us -> 2.24 us  [on_device(): jnp.dot(after(crossed, dv_sent), weight, preferred_element_type=F32)]
    convert_element_type x4, other arithmetic: 1.5 us -> 0.19 us  [joined(): return (own, before.astype(BF), header.astype(BF))]
    broadcast_in_dim x1, other arithmetic: 2.25 us -> 0.96 us  [on_device(): return (dq[None], key_grad[None], grad_input[None], grad_weight)]
    squeeze x1, local copies, waits for them, and re-layouts: 0.09 us -> 1.36 us  [on_device(): back[i][:, p * two:(p + 1) * two]]
    ppermute x2, starting transfers between devices: 1.78 us -> 3.03 us  [returned(): lax.ppermute(header, 'y', turned(4, 2))]
  transfers between devices with their start and end apart: 34 -> 34, of which waited for: 9 -> 9; matrix products, arithmetic and copies ran while one was open for 14% -> 12% of each run, Pallas kernels for 12% -> 12%
where the time goes in v4:
time: 113 us; the launch traced here: 112 us
  starting transfers between devices  59.1 us (52%)
  waiting for transfers between devices  18.8 us (17%)
  Pallas kernels  18.2 us (16%)
  other arithmetic  8.86 us (8%)
  local copies, waits for them, and re-layouts  4.01 us (4%)
  matrix products  2.24 us (2%)
  between operations  1.17 us (1%)
    ppermute x12, starting transfers between devices, turns(): return [lax.ppermute(value, axis, turned(count, n)) for n in steps]  19.6 us
    pallas_call x1, Pallas kernels, scores_call(): pl.pallas_call(scores_kernel, grid=(KEY_HEADS,), in_specs=[column(ROWS, G...  7.39 us
    pallas_call x1, Pallas kernels, probs_call(): pl.pallas_call(probs_kernel, grid=(KEY_HEADS,), in_specs=[column(ROWS, GR...  6.32 us
    ppermute x3, starting transfers between devices, on_device(): lax.ppermute(sent, ('zh', 'zl'), turned(4, step))  5.71 us
    ppermute x12, waiting for transfers between devices, turns(): return [lax.ppermute(value, axis, turned(count, n)) for n in steps]  5.27 us
    all_to_all x1, starting transfers between devices, on_device(): lax.all_to_all(after(by_x, k_sent), 'x', 0, 0).reshape(4 * ROWS, 4 * each)  4.97 us
    ppermute x2, starting transfers between devices, returned(): lax.ppermute(before, 'y', turned(4, 3))  4.95 us
    all_to_all x1, starting transfers between devices, on_device(): back = lax.all_to_all(back.reshape(4, ROWS, 4 * each), 'x', 0, 0)  4.83 us
  transfers between devices with their start and end apart: 34, of which 9 were waited for; matrix products, arithmetic and copies ran while one was open for 12% of the time, Pallas kernels for 12%

profile of v4, /device:TPU:2, one launch (start us, length us, event | category | flops | bytes accessed | tf_op | source)
XLA Modules:
  0.0 112.4 jit_solution(16924087054884210458)
XLA Ops:
  0.6 1.6 %collective-permute-start = (bf16[128,512]{1,0:T(8,128)(2,1)}, bf16[128,512]{1,0:T(8,128)(2,1)S(1)}, u32[]{:S(2)}, u32[]{:S(2)}) collective-permute-start(bf16[128,512]{1,0:T(8,128)(2,1)} %bitcast.90), channel_id=1, source_target_pairs={{0,32},{32,64},{64,96},{96,0},{1,33},{33,65},{65,97},{97,1},{2,34}... | collective-permute-start | bytes 393224 | tf_op jit(solution)/shard_map/ppermute | solution.py:197
  2.3 2.9 %collective-permute-start.1 = (bf16[128,512]{1,0:T(8,128)(2,1)}, bf16[128,512]{1,0:T(8,128)(2,1)S(1)}, u32[]{:S(2)}, u32[]{:S(2)}) collective-permute-start(bf16[128,512]{1,0:T(8,128)(2,1)} %bitcast.91), channel_id=1, source_target_pairs={{0,64},{32,96},{64,0},{96,32},{1,65},{33,97},{65,1},{97,33},{2,66}... | collective-permute-start | bytes 393224 | tf_op jit(solution)/shard_map/ppermute | solution.py:197
  5.2 1.3 %collective-permute-start.2 = (bf16[128,512]{1,0:T(8,128)(2,1)}, bf16[128,512]{1,0:T(8,128)(2,1)S(1)}, u32[]{:S(2)}, u32[]{:S(2)}) collective-permute-start(bf16[128,512]{1,0:T(8,128)(2,1)} %bitcast.92), channel_id=1, source_target_pairs={{0,96},{32,0},{64,32},{96,64},{1,97},{33,1},{65,33},{97,65},{2,98}... | collective-permute-start | bytes 393224 | tf_op jit(solution)/shard_map/ppermute | solution.py:197
  6.5 1.9 %collective-permute-start.4 = (bf16[320,512]{1,0:T(8,128)(2,1)}, bf16[320,512]{1,0:T(8,128)(2,1)S(1)}, u32[]{:S(2)}, u32[]{:S(2)}) collective-permute-start(bf16[320,512]{1,0:T(8,128)(2,1)} %param.9), channel_id=1, source_target_pairs={{0,8},{8,0},{1,9},{9,1},{2,10},{10,2},{3,11},{11,3},{4,12},{12,4},... | collective-permute-start | bytes 983048 | tf_op jit(solution)/shard_map/ppermute | solution.py:270
  8.4 1.5 %fusion.41 = (bf16[128,640]{1,0:T(8,128)(2,1)S(1)}, bf16[128,640]{1,0:T(8,128)(2,1)S(1)}, bf16[128,640]{1,0:T(8,128)(2,1)S(1)}, bf16[128,640]{1,0:T(8,128)(2,1)S...) fusion(bf16[128,5120]{1,0:T(8,128)(2,1)} %bitcast.81), kind=kLoop, calls=%fused_computation.107 | loop fusion | bytes 2621440 | tf_op jit(solution)/shard_map/slice | solution.py:263
  10.1 1.2 %pad_maximum_fusion = bf16[4,128,1280]{2,1,0:T(8,128)(2,1)} fusion(bf16[1,128,1280]{2,1,0:T(8,128)(2,1)S(1)} %get-tuple-element.95, bf16[1,128,1280]{2,1,0:T(8,128)(2,1)S(1)} %get-tuple-element.94, bf16[1,128,1280]{2,1,0:T(8,128)(2,1)S(1)} %get-tuple-element.93, bf16[1,128,1280]{2,1,0:T(8,128)(2,1)S(1)} %get-tuple-element.92), kind=kLoop, calls=%fused_computation | loop fusion | flops 1966080 | bytes 2621440 | tf_op jit(solution)/shard_map/stack | solution.py:260
  11.5 3.9 %collective-permute-start.3 = (bf16[256,512]{1,0:T(8,128)(2,1)S(1)}, bf16[256,512]{1,0:T(8,128)(2,1)S(1)}, u32[]{:S(2)}, u32[]{:S(2)}) collective-permute-start(bf16[256,512]{1,0:T(8,128)(2,1)S(1)} %pad_maximum_fusion.1), channel_id=1, source_target_pairs={{0,16},{16,0},{1,17},{17,1},{2,18},{18,2},{3,19},{19,3},{4,20},{20... | collective-permute-start | bytes 786440 | tf_op jit(solution)/shard_map/ppermute | solution.py:257
  15.5 5.0 %all-to-all-start = ((bf16[4,128,1280]{2,1,0:T(8,128)(2,1)}), bf16[4,128,1280]{2,1,0:T(8,128)(2,1)}, u32[]{:S(2)}, u32[]{:S(2)}) async-start(bf16[4,128,1280]{2,1,0:T(8,128)(2,1)} %pad_maximum_fusion), calls=%async_computation | async-start | bytes 2621440 | tf_op jit(solution)/shard_map/all_to_all | solution.py:269
  21.2 3.2 %collective-permute-done.3 = bf16[256,512]{1,0:T(8,128)(2,1)S(1)} collective-permute-done((bf16[256,512]{1,0:T(8,128)(2,1)S(1)}, bf16[256,512]{1,0:T(8,128)(2,1)S(1)}, u32[]{:S(2)}, u32[]{:S(2)}) %collective-permute-start.3) | collective-permute-done | bytes 262176 | tf_op jit(solution)/shard_map/ppermute | solution.py:257
  24.6 6.3 %probs.1 = (bf16[4,512,1024]{2,1,0:T(8,128)(2,1)}, f32[512,512]{1,0:T(8,128)S(1)}) custom-call(bf16[128,4096]{1,0:T(8,128)(2,1)S(1)} %bitcast.76, bf16[512,512]{1,0:T(8,128)(2,1)S(1)} %constant_dynamic-update-slice_fusion.k_ref, bf16[128,4096]{1,0:T(8,128)(2,1)S(1)} %bitcast.78, f32[512,128]{1,0:T(8,128)S(1)} %add_select_fusion.bias_ref), custom_call_target="tpu_custom_call" | custom-call | flops 65536 | bytes 65536 | tf_op jit(solution)/shard_map/probs/pallas_call | solution.py:68
  31.1 0.8 copy-done.2
  32.1 4.0 %all-to-all-done = bf16[4,128,1280]{2,1,0:T(8,128)(2,1)} async-done(((bf16[4,128,1280]{2,1,0:T(8,128)(2,1)}), bf16[4,128,1280]{2,1,0:T(8,128)(2,1)}, u32[]{:S(2)}, u32[]{:S(2)}) %all-to-all-start) | async-done | bytes 1310752 | tf_op jit(solution)/shard_map/all_to_all | solution.py:269
  36.1 2.2 %fusion.48 = f32[4,128,512]{2,1,0:T(8,128)S(1)} fusion(bf16[4,128,1280]{2,1,0:T(8,128)(2,1)} %bitcast.11, bf16[1280,512,1]{1,0,2:T(8,128)(2,1)S(1)} %bitcast.79), kind=kOutput, calls=%fused_computation.114 | convolution fusion | flops 671088640 | bytes 3670016 | tf_op jit(solution)/shard_map/dot_general | solution.py:284
  38.5 3.5 %collective-permute-start.7 = (bf16[128,512]{1,0:T(8,128)(2,1)S(1)}, bf16[128,512]{1,0:T(8,128)(2,1)S(1)}, u32[]{:S(2)}, u32[]{:S(2)}) collective-permute-start(bf16[128,512]{1,0:T(8,128)(2,1)S(1)} %get-tuple-element.80), channel_id=1, source_target_pairs={{0,4},{2,6},{4,0},{6,2},{1,5},{3,7},{5,1},{7,3},{8,12},{10,14},{12... | collective-permute-start | bytes 393224 | tf_op jit(solution)/shard_map/ppermute | solution.py:290
  42.0 0.6 collective-permute-start.8
  42.6 2.4 %collective-permute-start.14 = (bf16[128,512]{1,0:T(8,128)(2,1)S(1)}, bf16[128,512]{1,0:T(8,128)(2,1)S(1)}, u32[]{:S(2)}, u32[]{:S(2)}) collective-permute-start(bf16[128,512]{1,0:T(8,128)(2,1)S(1)} %get-tuple-element.54), channel_id=1, source_target_pairs={{0,64},{32,96},{64,0},{96,32},{1,65},{33,97},{65,1},{97,33},{2,66}... | collective-permute-start | bytes 393224 | tf_op jit(solution)/shard_map/ppermute | solution.py:237
  45.0 1.0 collective-permute-start.15
  46.1 2.3 %collective-permute-start.13 = (bf16[128,512]{1,0:T(8,128)(2,1)S(1)}, bf16[128,512]{1,0:T(8,128)(2,1)S(1)}, u32[]{:S(2)}, u32[]{:S(2)}) collective-permute-start(bf16[128,512]{1,0:T(8,128)(2,1)S(1)} %fusion.10), channel_id=1, source_target_pairs={{0,96},{32,0},{64,32},{96,64},{1,97},{33,1},{65,33},{97,65},{2,98}... | collective-permute-start | bytes 393224 | tf_op jit(solution)/shard_map/ppermute | solution.py:236
  48.6 2.5 %collective-permute-start.11 = (bf16[128,512]{1,0:T(8,128)(2,1)S(1)}, bf16[128,512]{1,0:T(8,128)(2,1)S(1)}, u32[]{:S(2)}, u32[]{:S(2)}) collective-permute-start(bf16[128,512]{1,0:T(8,128)(2,1)S(1)} %fusion.26), channel_id=1, source_target_pairs={{0,64},{32,96},{64,0},{96,32},{1,65},{33,97},{65,1},{97,33},{2,66}... | collective-permute-start | bytes 393224 | tf_op jit(solution)/shard_map/ppermute | solution.py:197
  51.0 1.5 %collective-permute-done.13 = bf16[128,512]{1,0:T(8,128)(2,1)S(1)} collective-permute-done((bf16[128,512]{1,0:T(8,128)(2,1)S(1)}, bf16[128,512]{1,0:T(8,128)(2,1)S(1)}, u32[]{:S(2)}, u32[]{:S(2)}) %collective-permute-start.13) | collective-permute-done | bytes 131104 | tf_op jit(solution)/shard_map/ppermute | solution.py:236
  52.5 3.6 %collective-permute-start.12 = (bf16[128,512]{1,0:T(8,128)(2,1)S(1)}, bf16[128,512]{1,0:T(8,128)(2,1)S(1)}, u32[]{:S(2)}, u32[]{:S(2)}) collective-permute-start(bf16[128,512]{1,0:T(8,128)(2,1)S(1)} %fusion.26), channel_id=1, source_target_pairs={{0,96},{32,0},{64,32},{96,64},{1,97},{33,1},{65,33},{97,65},{2,98}... | collective-permute-start | bytes 393224 | tf_op jit(solution)/shard_map/ppermute | solution.py:197
  56.3 1.5 %collective-permute-start.17 = (bf16[128,512]{1,0:T(8,128)(2,1)S(1)}, bf16[128,512]{1,0:T(8,128)(2,1)S(1)}, u32[]{:S(2)}, u32[]{:S(2)}) collective-permute-start(bf16[128,512]{1,0:T(8,128)(2,1)S(1)} %fusion.15.refs_0_), channel_id=1, source_target_pairs={{0,2},{2,4},{4,6},{6,0},{1,3},{3,5},{5,7},{7,1},{8,10},{10,12},{12... | collective-permute-start | bytes 393224 | tf_op jit(solution)/shard_map/ppermute | solution.py:197
  57.8 1.5 %collective-permute-start.18 = (bf16[128,512]{1,0:T(8,128)(2,1)S(1)}, bf16[128,512]{1,0:T(8,128)(2,1)S(1)}, u32[]{:S(2)}, u32[]{:S(2)}) collective-permute-start(bf16[128,512]{1,0:T(8,128)(2,1)S(1)} %fusion.15.refs_0_), channel_id=1, source_target_pairs={{0,4},{2,6},{4,0},{6,2},{1,5},{3,7},{5,1},{7,3},{8,12},{10,14},{12... | collective-permute-start | bytes 393224 | tf_op jit(solution)/shard_map/ppermute | solution.py:197
  59.3 0.6 collective-permute-start.19
  60.0 0.7 pad_maximum_fusion.3
  60.7 0.6 collective-permute-done.17.refs_1_
  61.3 3.1 %collective-permute-done.18.refs_2_ = bf16[128,512]{1,0:T(8,128)(2,1)S(1)} collective-permute-done((bf16[128,512]{1,0:T(8,128)(2,1)S(1)}, bf16[128,512]{1,0:T(8,128)(2,1)S(1)}, u32[]{:S(2)}, u32[]{:S(2)}) %collective-permute-start.18) | collective-permute-done | bytes 131104 | tf_op jit(solution)/shard_map/ppermute | solution.py:197
  64.4 1.3 %collective-permute-done.19.refs_3_ = bf16[128,512]{1,0:T(8,128)(2,1)S(1)} collective-permute-done((bf16[128,512]{1,0:T(8,128)(2,1)S(1)}, bf16[128,512]{1,0:T(8,128)(2,1)S(1)}, u32[]{:S(2)}, u32[]{:S(2)}) %collective-permute-start.19) | collective-permute-done | bytes 131104 | tf_op jit(solution)/shard_map/ppermute | solution.py:197
  65.7 4.5 %grads.1 = (bf16[512,1280]{1,0:T(8,128)(2,1)}, f32[2,320,512]{2,1,0:T(8,128)}, bf16[2,320,512]{2,1,0:T(8,128)(2,1)S(1)}) custom-call(s32[2]{0:T(128)S(1)} %pad_add_fusion.at_ref, bf16[512,1280]{1,0:T(8,128)(2,1)} %bitcast.8.crossed_ref, bf16[1280,512]{1,0:T(8,128)(2,1)S(1)} %bitcast.80, bf16[128,512]{1,0:T(8,128)(2,1)S(1)} %fusion.15.refs_0_, ...), custom_call_target="tpu_custom_call" | custom-call | flops 1342177280 | bytes 8388608 | tf_op jit(solution)/shard_map/grads/pallas_call | solution.py:154
  70.4 4.8 %all-to-all-start.1 = ((bf16[4,128,1280]{2,1,0:T(8,128)(2,1)}), bf16[4,128,1280]{2,1,0:T(8,128)(2,1)}, u32[]{:S(2)}, u32[]{:S(2)}) async-start(bf16[4,128,1280]{2,1,0:T(8,128)(2,1)} %bitcast.82), calls=%async_computation.1 | async-start | bytes 2621440 | tf_op jit(solution)/shard_map/all_to_all | solution.py:348
  75.3 1.9 %fusion.29 = (bf16[160,512]{1,0:T(8,128)(2,1)}, bf16[160,512]{1,0:T(8,128)(2,1)}, bf16[160,512]{1,0:T(8,128)(2,1)}) fusion(f32[2,2,160,512]{3,2,1,0:T(8,128)S(1)} %bitcast.83, s32[]{:T(128)S(6)} %select_n.328, s32[]{:T(128)S(6)} %select_n.330, bf16[2,2,160,512]{3,2,1,0:T(8,128)(2,1)} %bitcast.26, s32[]{:T(128)S(6)} %select_n.323, s32[]{:T(128)S(6)} %select_n.325, ...), kind=kLoop, calls=%fused_computation.66 | loop fusion | flops 737280 | bytes 1966104 | tf_op jit(solution)/shard_map/convert_element_type | solution.py:320
  77.2 1.2 %collective-permute-start.25 = (bf16[160,512]{1,0:T(8,128)(2,1)}, bf16[160,512]{1,0:T(8,128)(2,1)}, u32[]{:S(2)}, u32[]{:S(2)}) collective-permute-start(bf16[160,512]{1,0:T(8,128)(2,1)} %get-tuple-element.60), channel_id=1, source_target_pairs={{0,8},{8,16},{16,24},{24,0},{1,9},{9,17},{17,25},{25,1},{2,10},{10... | collective-permute-start | bytes 491528 | tf_op jit(solution)/shard_map/ppermute | solution.py:322
  78.3 3.6 %collective-permute-start.26 = (bf16[160,512]{1,0:T(8,128)(2,1)}, bf16[160,512]{1,0:T(8,128)(2,1)}, u32[]{:S(2)}, u32[]{:S(2)}) collective-permute-start(bf16[160,512]{1,0:T(8,128)(2,1)} %get-tuple-element.59), channel_id=1, source_target_pairs={{0,16},{8,24},{16,0},{24,8},{1,17},{9,25},{17,1},{25,9},{2,18},{10... | collective-permute-start | bytes 491528 | tf_op jit(solution)/shard_map/ppermute | solution.py:322
  81.9 1.0 collective-permute-start.27
  83.0 7.4 %scores.1 = (bf16[128,4096]{1,0:T(8,128)(2,1)}, f32[512,512]{1,0:T(8,128)S(1)}) custom-call(bf16[128,4096]{1,0:T(8,128)(2,1)} %bitcast.75, bf16[512,512]{1,0:T(8,128)(2,1)S(1)} %constant_dynamic-update-slice_fusion.k_ref, bf16[128,4096]{1,0:T(8,128)(2,1)} %bitcast.77, bf16[512,512]{1,0:T(8,128)(2,1)S(1)} %constant_dynamic-update-slice_fusion.1.v_ref, ...), custom_call_target="tpu_custom_call" | custom-call | flops 1610612736 | bytes 8388608 | tf_op jit(solution)/shard_map/scores/pallas_call | solution.py:94
  90.5 0.5 collective-permute-start.21
  91.1 1.3 %fusion.3 = bf16[160,512]{1,0:T(8,128)(2,1)S(1)} fusion(bf16[160,512]{1,0:T(8,128)(2,1)} %collective-permute-done.27, bf16[160,512]{1,0:T(8,128)(2,1)} %collective-permute-done.26, bf16[160,512]{1,0:T(8,128)(2,1)} %collective-permute-done.25, f32[2,2,160,512]{3,2,1,0:T(8,128)S(1)} %bitcast.84, s32[]{:T(128)S(6)} %select_n.341, s32[]{:T(128)S(6)} %select_n.343, ...), kind=kLoop, calls=%fused_computation.17 | loop fusion | flops 737280 | bytes 1146888 | tf_op jit(solution)/shard_map/convert_element_type | solution.py:332
  92.3 0.6 collective-permute-start.28
  93.3 2.9 %collective-permute-start.30 = (bf16[160,512]{1,0:T(8,128)(2,1)S(1)}, bf16[160,512]{1,0:T(8,128)(2,1)S(1)}, u32[]{:S(2)}, u32[]{:S(2)}) collective-permute-start(bf16[160,512]{1,0:T(8,128)(2,1)S(1)} %fusion.3), channel_id=1, source_target_pairs={{0,96},{32,0},{64,32},{96,64},{1,97},{33,1},{65,33},{97,65},{2,98}... | collective-permute-start | bytes 491528 | tf_op jit(solution)/shard_map/ppermute | solution.py:197
  96.2 3.5 %collective-permute-done.21 = bf16[256,512]{1,0:T(8,128)(2,1)S(1)} collective-permute-done((bf16[256,512]{1,0:T(8,128)(2,1)S(1)}, bf16[256,512]{1,0:T(8,128)(2,1)S(1)}, u32[]{:S(2)}, u32[]{:S(2)}) %collective-permute-start.21) | collective-permute-done | bytes 262176 | tf_op jit(solution)/shard_map/ppermute | solution.py:334
  99.8 0.6 collective-permute-start.23
  100.7 0.3 collective-permute-done.28
  101.1 2.6 %collective-permute-start.22 = (bf16[128,512]{1,0:T(8,128)(2,1)S(1)}, bf16[128,512]{1,0:T(8,128)(2,1)S(1)}, u32[]{:S(2)}, u32[]{:S(2)}) collective-permute-start(bf16[128,512]{1,0:T(8,128)(2,1)S(1)} %get-tuple-element.52), channel_id=1, source_target_pairs={{0,96},{32,0},{64,32},{96,64},{1,97},{33,1},{65,33},{97,65},{2,98}... | collective-permute-start | bytes 393224 | tf_op jit(solution)/shard_map/ppermute | solution.py:236
  103.8 3.8 %collective-permute-start.31 = (bf16[160,512]{1,0:T(8,128)(2,1)S(1)}, bf16[160,512]{1,0:T(8,128)(2,1)S(1)}, u32[]{:S(2)}, u32[]{:S(2)}) collective-permute-start(bf16[160,512]{1,0:T(8,128)(2,1)S(1)} %add_convert_fusion), channel_id=1, source_target_pairs={{0,16},{16,0},{1,17},{17,1},{2,18},{18,2},{3,19},{19,3},{4,20},{20... | collective-permute-start | bytes 491528 | tf_op jit(solution)/shard_map/ppermute | solution.py:339
  107.6 1.4 %slice_bitcast_fusion = (bf16[128,1280]{1,0:T(8,128)(2,1)S(1)}, bf16[128,1280]{1,0:T(8,128)(2,1)S(1)}, bf16[128,1280]{1,0:T(8,128)(2,1)S(1)}, bf16[128,1280]{1,0:T(8,128)(2,1)S(1)}) fusion(bf16[4,128,1280]{2,1,0:T(8,128)(2,1)} %all-to-all-done.1), kind=kLoop, calls=%fused_computation.18 | loop fusion | bytes 2621440 | tf_op jit(solution)/shard_map/squeeze | solution.py:351
  109.2 1.0 fusion.33
  110.2 1.3 %collective-permute-done.31 = bf16[160,512]{1,0:T(8,128)(2,1)S(1)} collective-permute-done((bf16[160,512]{1,0:T(8,128)(2,1)S(1)}, bf16[160,512]{1,0:T(8,128)(2,1)S(1)}, u32[]{:S(2)}, u32[]{:S(2)}) %collective-permute-start.31) | collective-permute-done | bytes 163872 | tf_op jit(solution)/shard_map/ppermute | solution.py:339
  111.5 0.9 fusion
  (99 shorter events, 3.5 us)
Async XLA Ops:
  0.6 10.8 %collective-permute-start = (bf16[128,512]{1,0:T(8,128)(2,1)}, bf16[128,512]{1,0:T(8,128)(2,1)S(1)}, u32[]{:S(2)}, u32[]{:S(2)}) collective-permute-start(bf16[128,512]{1,0:T(8,128)(2,1)} %bitcast.90), channel_id=1, source_target_pairs={{0,32},{32,64},{64,96},{96,0},{1,33},{33,65},{65,97},{97,1},{2,34}... | collective-permute-start | bytes 393224 | tf_op jit(solution)/shard_map/ppermute | solution.py:197
  2.3 9.2 %collective-permute-start.1 = (bf16[128,512]{1,0:T(8,128)(2,1)}, bf16[128,512]{1,0:T(8,128)(2,1)S(1)}, u32[]{:S(2)}, u32[]{:S(2)}) collective-permute-start(bf16[128,512]{1,0:T(8,128)(2,1)} %bitcast.91), channel_id=1, source_target_pairs={{0,64},{32,96},{64,0},{96,32},{1,65},{33,97},{65,1},{97,33},{2,66}... | collective-permute-start | bytes 393224 | tf_op jit(solution)/shard_map/ppermute | solution.py:197
  5.2 6.3 %collective-permute-start.2 = (bf16[128,512]{1,0:T(8,128)(2,1)}, bf16[128,512]{1,0:T(8,128)(2,1)S(1)}, u32[]{:S(2)}, u32[]{:S(2)}) collective-permute-start(bf16[128,512]{1,0:T(8,128)(2,1)} %bitcast.92), channel_id=1, source_target_pairs={{0,96},{32,0},{64,32},{96,64},{1,97},{33,1},{65,33},{97,65},{2,98}... | collective-permute-start | bytes 393224 | tf_op jit(solution)/shard_map/ppermute | solution.py:197
  6.5 14.3 %collective-permute-start.4 = (bf16[320,512]{1,0:T(8,128)(2,1)}, bf16[320,512]{1,0:T(8,128)(2,1)S(1)}, u32[]{:S(2)}, u32[]{:S(2)}) collective-permute-start(bf16[320,512]{1,0:T(8,128)(2,1)} %param.9), channel_id=1, source_target_pairs={{0,8},{8,0},{1,9},{9,1},{2,10},{10,2},{3,11},{11,3},{4,12},{12,4},... | collective-permute-start | bytes 983048 | tf_op jit(solution)/shard_map/ppermute | solution.py:270
  10.1 1.4 %copy-start.6 = (bf16[1,128,512]{2,1,0:T(8,128)(2,1)S(1)}, bf16[1,128,512]{2,1,0:T(8,128)(2,1)}, u32[]{:S(2)}) copy-start(bf16[1,128,512]{2,1,0:T(8,128)(2,1)} %param.8) | copy-start | bytes 393220
  11.3 4.1 %copy-start.8 = (s32[1,1024]{1,0:T(1,128)S(1)}, s32[1,1024]{1,0:T(1,128)}, u32[]{:S(2)}) copy-start(s32[1,1024]{1,0:T(1,128)} %param.11) | copy-start | bytes 12292
  11.5 12.9 %collective-permute-start.3 = (bf16[256,512]{1,0:T(8,128)(2,1)S(1)}, bf16[256,512]{1,0:T(8,128)(2,1)S(1)}, u32[]{:S(2)}, u32[]{:S(2)}) collective-permute-start(bf16[256,512]{1,0:T(8,128)(2,1)S(1)} %pad_maximum_fusion.1), channel_id=1, source_target_pairs={{0,16},{16,0},{1,17},{17,1},{2,18},{18,2},{3,19},{19,3},{4,20},{20... | collective-permute-start | bytes 786440 | tf_op jit(solution)/shard_map/ppermute | solution.py:257
  15.5 5.4 %copy-start.5 = (bf16[320,512]{1,0:T(8,128)(2,1)S(1)}, bf16[320,512]{1,0:T(8,128)(2,1)}, u32[]{:S(2)}) copy-start(bf16[320,512]{1,0:T(8,128)(2,1)} %param.9) | copy-start | bytes 983044
  15.5 20.6 %all-to-all-start = ((bf16[4,128,1280]{2,1,0:T(8,128)(2,1)}), bf16[4,128,1280]{2,1,0:T(8,128)(2,1)}, u32[]{:S(2)}, u32[]{:S(2)}) async-start(bf16[4,128,1280]{2,1,0:T(8,128)(2,1)} %pad_maximum_fusion), calls=%async_computation | async-start | bytes 2621440 | tf_op jit(solution)/shard_map/all_to_all | solution.py:269
  21.0 10.1 %collective-permute-start.5 = (bf16[2,320,512]{2,1,0:T(8,128)(2,1)S(1)}, bf16[2,320,512]{2,1,0:T(8,128)(2,1)S(1)}, u32[]{:S(2)}, u32[]{:S(2)}) collective-permute-start(bf16[2,320,512]{2,1,0:T(8,128)(2,1)S(1)} %maximum_select_fusion.2), channel_id=1, source_target_pairs={{0,1},{1,0},{2,3},{3,2},{4,5},{5,4},{6,7},{7,6},{8,9},{9,8},{10,11... | collective-permute-start | bytes 1966088 | tf_op jit(solution)/shard_map/ppermute | solution.py:274
  21.1 3.5 %copy-start = (bf16[1,128,4096]{2,1,0:T(8,128)(2,1)S(1)}, bf16[1,128,4096]{2,1,0:T(8,128)(2,1)}, u32[]{:S(2)}) copy-start(bf16[1,128,4096]{2,1,0:T(8,128)(2,1)} %param.7) | copy-start | bytes 3145732
  21.1 3.5 %copy-start.1 = (bf16[1,128,4096]{2,1,0:T(8,128)(2,1)S(1)}, bf16[1,128,4096]{2,1,0:T(8,128)(2,1)}, u32[]{:S(2)}) copy-start(bf16[1,128,4096]{2,1,0:T(8,128)(2,1)} %param.10) | copy-start | bytes 3145732
  30.9 1.0 copy-start.2
  31.0 11.6 %collective-permute-start.9 = (bf16[256,512]{1,0:T(8,128)(2,1)S(1)}, bf16[256,512]{1,0:T(8,128)(2,1)S(1)}, u32[]{:S(2)}, u32[]{:S(2)}) collective-permute-start(bf16[256,512]{1,0:T(8,128)(2,1)S(1)} %pad_maximum_fusion.2), channel_id=1, source_target_pairs={{0,16},{16,0},{1,17},{17,1},{2,18},{18,2},{3,19},{19,3},{4,20},{20... | collective-permute-start | bytes 786440 | tf_op jit(solution)/shard_map/ppermute | solution.py:282
  36.1 6.5 %copy-start.3 = (f32[512,512]{1,0:T(8,128)S(1)}, f32[512,512]{1,0:T(8,128)}, u32[]{:S(2)}) copy-start(f32[512,512]{1,0:T(8,128)} %copy-done.2) | copy-start | bytes 3145732
  38.4 7.6 %collective-permute-start.6 = (bf16[128,512]{1,0:T(8,128)(2,1)S(1)}, bf16[128,512]{1,0:T(8,128)(2,1)S(1)}, u32[]{:S(2)}, u32[]{:S(2)}) collective-permute-start(bf16[128,512]{1,0:T(8,128)(2,1)S(1)} %get-tuple-element.81), channel_id=1, source_target_pairs={{0,2},{2,4},{4,6},{6,0},{1,3},{3,5},{5,7},{7,1},{8,10},{10,12},{12... | collective-permute-start | bytes 393224 | tf_op jit(solution)/shard_map/ppermute | solution.py:290
  38.5 9.9 %collective-permute-start.7 = (bf16[128,512]{1,0:T(8,128)(2,1)S(1)}, bf16[128,512]{1,0:T(8,128)(2,1)S(1)}, u32[]{:S(2)}, u32[]{:S(2)}) collective-permute-start(bf16[128,512]{1,0:T(8,128)(2,1)S(1)} %get-tuple-element.80), channel_id=1, source_target_pairs={{0,4},{2,6},{4,0},{6,2},{1,5},{3,7},{5,1},{7,3},{8,12},{10,14},{12... | collective-permute-start | bytes 393224 | tf_op jit(solution)/shard_map/ppermute | solution.py:290
  42.0 6.4 %collective-permute-start.8 = (bf16[128,512]{1,0:T(8,128)(2,1)S(1)}, bf16[128,512]{1,0:T(8,128)(2,1)S(1)}, u32[]{:S(2)}, u32[]{:S(2)}) collective-permute-start(bf16[128,512]{1,0:T(8,128)(2,1)S(1)} %get-tuple-element.79), channel_id=1, source_target_pairs={{0,6},{2,0},{4,2},{6,4},{1,7},{3,1},{5,3},{7,5},{8,14},{10,8},{12,... | collective-permute-start | bytes 393224 | tf_op jit(solution)/shard_map/ppermute | solution.py:290
  42.6 13.5 %collective-permute-start.14 = (bf16[128,512]{1,0:T(8,128)(2,1)S(1)}, bf16[128,512]{1,0:T(8,128)(2,1)S(1)}, u32[]{:S(2)}, u32[]{:S(2)}) collective-permute-start(bf16[128,512]{1,0:T(8,128)(2,1)S(1)} %get-tuple-element.54), channel_id=1, source_target_pairs={{0,64},{32,96},{64,0},{96,32},{1,65},{33,97},{65,1},{97,33},{2,66}... | collective-permute-start | bytes 393224 | tf_op jit(solution)/shard_map/ppermute | solution.py:237
  45.0 11.1 %collective-permute-start.15 = (bf16[128,512]{1,0:T(8,128)(2,1)S(1)}, bf16[128,512]{1,0:T(8,128)(2,1)S(1)}, u32[]{:S(2)}, u32[]{:S(2)}) collective-permute-start(bf16[128,512]{1,0:T(8,128)(2,1)S(1)} %get-tuple-element.54), channel_id=1, source_target_pairs={{0,32},{32,64},{64,96},{96,0},{1,33},{33,65},{65,97},{97,1},{2,34}... | collective-permute-start | bytes 393224 | tf_op jit(solution)/shard_map/ppermute | solution.py:238
  46.1 6.4 %collective-permute-start.13 = (bf16[128,512]{1,0:T(8,128)(2,1)S(1)}, bf16[128,512]{1,0:T(8,128)(2,1)S(1)}, u32[]{:S(2)}, u32[]{:S(2)}) collective-permute-start(bf16[128,512]{1,0:T(8,128)(2,1)S(1)} %fusion.10), channel_id=1, source_target_pairs={{0,96},{32,0},{64,32},{96,64},{1,97},{33,1},{65,33},{97,65},{2,98}... | collective-permute-start | bytes 393224 | tf_op jit(solution)/shard_map/ppermute | solution.py:236
  48.5 10.9 %collective-permute-start.10 = (bf16[128,512]{1,0:T(8,128)(2,1)S(1)}, bf16[128,512]{1,0:T(8,128)(2,1)S(1)}, u32[]{:S(2)}, u32[]{:S(2)}) collective-permute-start(bf16[128,512]{1,0:T(8,128)(2,1)S(1)} %fusion.26), channel_id=1, source_target_pairs={{0,32},{32,64},{64,96},{96,0},{1,33},{33,65},{65,97},{97,1},{2,34}... | collective-permute-start | bytes 393224 | tf_op jit(solution)/shard_map/ppermute | solution.py:197
  48.6 11.4 %collective-permute-start.11 = (bf16[128,512]{1,0:T(8,128)(2,1)S(1)}, bf16[128,512]{1,0:T(8,128)(2,1)S(1)}, u32[]{:S(2)}, u32[]{:S(2)}) collective-permute-start(bf16[128,512]{1,0:T(8,128)(2,1)S(1)} %fusion.26), channel_id=1, source_target_pairs={{0,64},{32,96},{64,0},{96,32},{1,65},{33,97},{65,1},{97,33},{2,66}... | collective-permute-start | bytes 393224 | tf_op jit(solution)/shard_map/ppermute | solution.py:197
  52.5 7.5 %collective-permute-start.12 = (bf16[128,512]{1,0:T(8,128)(2,1)S(1)}, bf16[128,512]{1,0:T(8,128)(2,1)S(1)}, u32[]{:S(2)}, u32[]{:S(2)}) collective-permute-start(bf16[128,512]{1,0:T(8,128)(2,1)S(1)} %fusion.26), channel_id=1, source_target_pairs={{0,96},{32,0},{64,32},{96,64},{1,97},{33,1},{65,33},{97,65},{2,98}... | collective-permute-start | bytes 393224 | tf_op jit(solution)/shard_map/ppermute | solution.py:197
  56.3 5.0 %collective-permute-start.17 = (bf16[128,512]{1,0:T(8,128)(2,1)S(1)}, bf16[128,512]{1,0:T(8,128)(2,1)S(1)}, u32[]{:S(2)}, u32[]{:S(2)}) collective-permute-start(bf16[128,512]{1,0:T(8,128)(2,1)S(1)} %fusion.15.refs_0_), channel_id=1, source_target_pairs={{0,2},{2,4},{4,6},{6,0},{1,3},{3,5},{5,7},{7,1},{8,10},{10,12},{12... | collective-permute-start | bytes 393224 | tf_op jit(solution)/shard_map/ppermute | solution.py:197
  57.8 6.6 %collective-permute-start.18 = (bf16[128,512]{1,0:T(8,128)(2,1)S(1)}, bf16[128,512]{1,0:T(8,128)(2,1)S(1)}, u32[]{:S(2)}, u32[]{:S(2)}) collective-permute-start(bf16[128,512]{1,0:T(8,128)(2,1)S(1)} %fusion.15.refs_0_), channel_id=1, source_target_pairs={{0,4},{2,6},{4,0},{6,2},{1,5},{3,7},{5,1},{7,3},{8,12},{10,14},{12... | collective-permute-start | bytes 393224 | tf_op jit(solution)/shard_map/ppermute | solution.py:197
  59.3 6.3 %collective-permute-start.19 = (bf16[128,512]{1,0:T(8,128)(2,1)S(1)}, bf16[128,512]{1,0:T(8,128)(2,1)S(1)}, u32[]{:S(2)}, u32[]{:S(2)}) collective-permute-start(bf16[128,512]{1,0:T(8,128)(2,1)S(1)} %fusion.15.refs_0_), channel_id=1, source_target_pairs={{0,6},{2,0},{4,2},{6,4},{1,7},{3,1},{5,3},{7,5},{8,14},{10,8},{12,... | collective-permute-start | bytes 393224 | tf_op jit(solution)/shard_map/ppermute | solution.py:197
  70.2 5.1 %collective-permute-start.20 = (bf16[2,320,512]{2,1,0:T(8,128)(2,1)S(1)}, bf16[2,320,512]{2,1,0:T(8,128)(2,1)}, u32[]{:S(2)}, u32[]{:S(2)}) collective-permute-start(bf16[2,320,512]{2,1,0:T(8,128)(2,1)S(1)} %get-tuple-element.44), channel_id=1, source_target_pairs={{0,1},{1,0},{2,3},{3,2},{4,5},{5,4},{6,7},{7,6},{8,9},{9,8},{10,11... | collective-permute-start | bytes 1966088 | tf_op jit(solution)/shard_map/ppermute | solution.py:309
  70.2 12.7 %collective-permute-start.16 = (bf16[256,512]{1,0:T(8,128)(2,1)}, bf16[256,512]{1,0:T(8,128)(2,1)S(1)}, u32[]{:S(2)}, u32[]{:S(2)}) collective-permute-start(bf16[256,512]{1,0:T(8,128)(2,1)} %pad_maximum_fusion.3), channel_id=1, source_target_pairs={{0,16},{16,0},{1,17},{17,1},{2,18},{18,2},{3,19},{19,3},{4,20},{20... | collective-permute-start | bytes 786440 | tf_op jit(solution)/shard_map/ppermute | solution.py:305
  70.4 4.8 %copy-start.4 = (f32[2,320,512]{2,1,0:T(8,128)S(1)}, f32[2,320,512]{2,1,0:T(8,128)}, u32[]{:S(2)}) copy-start(f32[2,320,512]{2,1,0:T(8,128)} %get-tuple-element.43) | copy-start | bytes 3932164
  70.4 37.1 %all-to-all-start.1 = ((bf16[4,128,1280]{2,1,0:T(8,128)(2,1)}), bf16[4,128,1280]{2,1,0:T(8,128)(2,1)}, u32[]{:S(2)}, u32[]{:S(2)}) async-start(bf16[4,128,1280]{2,1,0:T(8,128)(2,1)} %bitcast.82), calls=%async_computation.1 | async-start | bytes 2621440 | tf_op jit(solution)/shard_map/all_to_all | solution.py:348
  77.2 13.9 %collective-permute-start.25 = (bf16[160,512]{1,0:T(8,128)(2,1)}, bf16[160,512]{1,0:T(8,128)(2,1)}, u32[]{:S(2)}, u32[]{:S(2)}) collective-permute-start(bf16[160,512]{1,0:T(8,128)(2,1)} %get-tuple-element.60), channel_id=1, source_target_pairs={{0,8},{8,16},{16,24},{24,0},{1,9},{9,17},{17,25},{25,1},{2,10},{10... | collective-permute-start | bytes 491528 | tf_op jit(solution)/shard_map/ppermute | solution.py:322
  78.3 12.7 %collective-permute-start.26 = (bf16[160,512]{1,0:T(8,128)(2,1)}, bf16[160,512]{1,0:T(8,128)(2,1)}, u32[]{:S(2)}, u32[]{:S(2)}) collective-permute-start(bf16[160,512]{1,0:T(8,128)(2,1)} %get-tuple-element.59), channel_id=1, source_target_pairs={{0,16},{8,24},{16,0},{24,8},{1,17},{9,25},{17,1},{25,9},{2,18},{10... | collective-permute-start | bytes 491528 | tf_op jit(solution)/shard_map/ppermute | solution.py:322
  81.9 9.2 %collective-permute-start.27 = (bf16[160,512]{1,0:T(8,128)(2,1)}, bf16[160,512]{1,0:T(8,128)(2,1)}, u32[]{:S(2)}, u32[]{:S(2)}) collective-permute-start(bf16[160,512]{1,0:T(8,128)(2,1)} %get-tuple-element.58), channel_id=1, source_target_pairs={{0,24},{8,0},{16,8},{24,16},{1,25},{9,1},{17,9},{25,17},{2,26},{10... | collective-permute-start | bytes 491528 | tf_op jit(solution)/shard_map/ppermute | solution.py:322
  90.5 9.2 %collective-permute-start.21 = (bf16[256,512]{1,0:T(8,128)(2,1)S(1)}, bf16[256,512]{1,0:T(8,128)(2,1)S(1)}, u32[]{:S(2)}, u32[]{:S(2)}) collective-permute-start(bf16[256,512]{1,0:T(8,128)(2,1)S(1)} %pad_maximum_fusion.4), channel_id=1, source_target_pairs={{0,16},{16,0},{1,17},{17,1},{2,18},{18,2},{3,19},{19,3},{4,20},{20... | collective-permute-start | bytes 786440 | tf_op jit(solution)/shard_map/ppermute | solution.py:334
  92.3 8.7 %collective-permute-start.28 = (bf16[160,512]{1,0:T(8,128)(2,1)S(1)}, bf16[160,512]{1,0:T(8,128)(2,1)S(1)}, u32[]{:S(2)}, u32[]{:S(2)}) collective-permute-start(bf16[160,512]{1,0:T(8,128)(2,1)S(1)} %fusion.3), channel_id=1, source_target_pairs={{0,64},{32,96},{64,0},{96,32},{1,65},{33,97},{65,1},{97,33},{2,66}... | collective-permute-start | bytes 491528 | tf_op jit(solution)/shard_map/ppermute | solution.py:197
  93.0 10.7 %collective-permute-start.29 = (bf16[160,512]{1,0:T(8,128)(2,1)S(1)}, bf16[160,512]{1,0:T(8,128)(2,1)S(1)}, u32[]{:S(2)}, u32[]{:S(2)}) collective-permute-start(bf16[160,512]{1,0:T(8,128)(2,1)S(1)} %fusion.3), channel_id=1, source_target_pairs={{0,32},{32,64},{64,96},{96,0},{1,33},{33,65},{65,97},{97,1},{2,34}... | collective-permute-start | bytes 491528 | tf_op jit(solution)/shard_map/ppermute | solution.py:197
  93.3 10.4 %collective-permute-start.30 = (bf16[160,512]{1,0:T(8,128)(2,1)S(1)}, bf16[160,512]{1,0:T(8,128)(2,1)S(1)}, u32[]{:S(2)}, u32[]{:S(2)}) collective-permute-start(bf16[160,512]{1,0:T(8,128)(2,1)S(1)} %fusion.3), channel_id=1, source_target_pairs={{0,96},{32,0},{64,32},{96,64},{1,97},{33,1},{65,33},{97,65},{2,98}... | collective-permute-start | bytes 491528 | tf_op jit(solution)/shard_map/ppermute | solution.py:197
  99.8 9.4 %collective-permute-start.23 = (bf16[128,512]{1,0:T(8,128)(2,1)S(1)}, bf16[128,512]{1,0:T(8,128)(2,1)S(1)}, u32[]{:S(2)}, u32[]{:S(2)}) collective-permute-start(bf16[128,512]{1,0:T(8,128)(2,1)S(1)} %convert_element_type.175), channel_id=1, source_target_pairs={{0,64},{32,96},{64,0},{96,32},{1,65},{33,97},{65,1},{97,33},{2,66}... | collective-permute-start | bytes 393224 | tf_op jit(solution)/shard_map/ppermute | solution.py:237
  100.4 8.7 %collective-permute-start.24 = (bf16[128,512]{1,0:T(8,128)(2,1)S(1)}, bf16[128,512]{1,0:T(8,128)(2,1)S(1)}, u32[]{:S(2)}, u32[]{:S(2)}) collective-permute-start(bf16[128,512]{1,0:T(8,128)(2,1)S(1)} %convert_element_type.175), channel_id=1, source_target_pairs={{0,32},{32,64},{64,96},{96,0},{1,33},{33,65},{65,97},{97,1},{2,34}... | collective-permute-start | bytes 393224 | tf_op jit(solution)/shard_map/ppermute | solution.py:238
  101.1 8.1 %collective-permute-start.22 = (bf16[128,512]{1,0:T(8,128)(2,1)S(1)}, bf16[128,512]{1,0:T(8,128)(2,1)S(1)}, u32[]{:S(2)}, u32[]{:S(2)}) collective-permute-start(bf16[128,512]{1,0:T(8,128)(2,1)S(1)} %get-tuple-element.52), channel_id=1, source_target_pairs={{0,96},{32,0},{64,32},{96,64},{1,97},{33,1},{65,33},{97,65},{2,98}... | collective-permute-start | bytes 393224 | tf_op jit(solution)/shard_map/ppermute | solution.py:236
  103.8 7.7 %collective-permute-start.31 = (bf16[160,512]{1,0:T(8,128)(2,1)S(1)}, bf16[160,512]{1,0:T(8,128)(2,1)S(1)}, u32[]{:S(2)}, u32[]{:S(2)}) collective-permute-start(bf16[160,512]{1,0:T(8,128)(2,1)S(1)} %add_convert_fusion), channel_id=1, source_target_pairs={{0,16},{16,0},{1,17},{17,1},{2,18},{18,2},{3,19},{19,3},{4,20},{20... | collective-permute-start | bytes 491528 | tf_op jit(solution)/shard_map/ppermute | solution.py:339
  109.2 3.2 %copy-start.7 = (bf16[128,5120]{1,0:T(8,128)(2,1)}, bf16[128,5120]{1,0:T(8,128)(2,1)S(1)}, u32[]{:S(2)}) copy-start(bf16[128,5120]{1,0:T(8,128)(2,1)S(1)} %slice_dynamic-update-slice_fusion) | copy-start | bytes 3932164

commit v5 on v4

--- a/solution.py
+++ b/solution.py
@@ -33,7 +33,7 @@
     bias = bias_ref[...]
     scores = scores + jnp.concatenate([bias] * GROUP, axis=1)
     highest = jnp.max(scores, axis=0, keepdims=True)
-    weights = jnp.exp((scores - highest) * ROOT)
+    weights = jnp.exp2((scores - highest) * (ROOT * math.log2(math.e)))
     total = jnp.sum(weights, axis=0, keepdims=True)
     probs = (weights * (1.0 / total)).astype(BF)
     p_ref[0] = probs
@@ -193,8 +193,9 @@
     return lax.optimization_barrier((tuple(values), tuple(others)))[0]
 
 
-def turns(value, axis, count, steps=(1, 2, 3)):
-    return [lax.ppermute(value, axis, turned(count, n)) for n in steps]
+def turns(value, axis, count):
+    first, last, second = (lax.ppermute(value, axis, turned(count, n)) for n in (1, 3, 2))
+    return [first, second, last]
 
 
 def nearby(block, y, zh):
@@ -232,11 +233,9 @@
 
 
 def returned(before, header):
-    return [
-        lax.ppermute(before, "y", turned(4, 3)),
-        lax.ppermute(header, "y", turned(4, 2)),
-        lax.ppermute(header, "y", turned(4, 1)),
-    ]
+    from_next = lax.ppermute(before, "y", turned(4, 3))
+    last = lax.ppermute(header, "y", turned(4, 1))
+    return [from_next, lax.ppermute(header, "y", turned(4, 2)), last]
 
 
 def summed(own, got, y):

time: 113 us -> 113 us (level)
  no operation moved by 1% of the time
where the time goes in v5:
time: 113 us; the launch traced here: 112 us
  starting transfers between devices  58.9 us (52%)
  waiting for transfers between devices  19 us (17%)
  Pallas kernels  17.9 us (16%)
  other arithmetic  8.86 us (8%)
  local copies, waits for them, and re-layouts  4.01 us (4%)
  matrix products  2.24 us (2%)
  between operations  1.17 us (1%)
    ppermute x12, starting transfers between devices, turns(): lax.ppermute(value, axis, turned(count, n))  19.6 us
    pallas_call x1, Pallas kernels, scores_call(): pl.pallas_call(scores_kernel, grid=(KEY_HEADS,), in_specs=[column(ROWS, G...  7.38 us
    pallas_call x1, Pallas kernels, probs_call(): pl.pallas_call(probs_kernel, grid=(KEY_HEADS,), in_specs=[column(ROWS, GR...  6.06 us
    ppermute x3, starting transfers between devices, on_device(): lax.ppermute(sent, ('zh', 'zl'), turned(4, step))  5.56 us
    ppermute x12, waiting for transfers between devices, turns(): lax.ppermute(value, axis, turned(count, n))  5.38 us
    all_to_all x1, starting transfers between devices, on_device(): lax.all_to_all(after(by_x, k_sent), 'x', 0, 0).reshape(4 * ROWS, 4 * each)  4.97 us
    all_to_all x1, starting transfers between devices, on_device(): back = lax.all_to_all(back.reshape(4, ROWS, 4 * each), 'x', 0, 0)  4.83 us
    ppermute x2, starting transfers between devices, returned(): from_next = lax.ppermute(before, 'y', turned(4, 3))  4.72 us
  transfers between devices with their start and end apart: 34, of which 9 were waited for; matrix products, arithmetic and copies ran while one was open for 12% of the time, Pallas kernels for 12%

profile of v5, /device:TPU:2, one launch (start us, length us, event | category | flops | bytes accessed | tf_op | source)
XLA Modules:
  0.0 112.1 jit_solution(16600134644840508657)
XLA Ops:
  0.6 1.6 %collective-permute-start = (bf16[128,512]{1,0:T(8,128)(2,1)}, bf16[128,512]{1,0:T(8,128)(2,1)S(1)}, u32[]{:S(2)}, u32[]{:S(2)}) collective-permute-start(bf16[128,512]{1,0:T(8,128)(2,1)} %bitcast.90), channel_id=1, source_target_pairs={{0,32},{32,64},{64,96},{96,0},{1,33},{33,65},{65,97},{97,1},{2,34}... | collective-permute-start | bytes 393224 | tf_op jit(solution)/shard_map/ppermute | solution.py:197
  2.3 2.9 %collective-permute-start.1 = (bf16[128,512]{1,0:T(8,128)(2,1)}, bf16[128,512]{1,0:T(8,128)(2,1)S(1)}, u32[]{:S(2)}, u32[]{:S(2)}) collective-permute-start(bf16[128,512]{1,0:T(8,128)(2,1)} %bitcast.91), channel_id=1, source_target_pairs={{0,64},{32,96},{64,0},{96,32},{1,65},{33,97},{65,1},{97,33},{2,66}... | collective-permute-start | bytes 393224 | tf_op jit(solution)/shard_map/ppermute | solution.py:197
  5.2 1.3 %collective-permute-start.2 = (bf16[128,512]{1,0:T(8,128)(2,1)}, bf16[128,512]{1,0:T(8,128)(2,1)S(1)}, u32[]{:S(2)}, u32[]{:S(2)}) collective-permute-start(bf16[128,512]{1,0:T(8,128)(2,1)} %bitcast.92), channel_id=1, source_target_pairs={{0,96},{32,0},{64,32},{96,64},{1,97},{33,1},{65,33},{97,65},{2,98}... | collective-permute-start | bytes 393224 | tf_op jit(solution)/shard_map/ppermute | solution.py:197
  6.5 1.9 %collective-permute-start.4 = (bf16[320,512]{1,0:T(8,128)(2,1)}, bf16[320,512]{1,0:T(8,128)(2,1)S(1)}, u32[]{:S(2)}, u32[]{:S(2)}) collective-permute-start(bf16[320,512]{1,0:T(8,128)(2,1)} %param.9), channel_id=1, source_target_pairs={{0,8},{8,0},{1,9},{9,1},{2,10},{10,2},{3,11},{11,3},{4,12},{12,4},... | collective-permute-start | bytes 983048 | tf_op jit(solution)/shard_map/ppermute | solution.py:269
  8.4 1.5 %fusion.41 = (bf16[128,640]{1,0:T(8,128)(2,1)S(1)}, bf16[128,640]{1,0:T(8,128)(2,1)S(1)}, bf16[128,640]{1,0:T(8,128)(2,1)S(1)}, bf16[128,640]{1,0:T(8,128)(2,1)S...) fusion(bf16[128,5120]{1,0:T(8,128)(2,1)} %bitcast.81), kind=kLoop, calls=%fused_computation.107 | loop fusion | bytes 2621440 | tf_op jit(solution)/shard_map/slice | solution.py:262
  10.1 1.2 %pad_maximum_fusion = bf16[4,128,1280]{2,1,0:T(8,128)(2,1)} fusion(bf16[1,128,1280]{2,1,0:T(8,128)(2,1)S(1)} %get-tuple-element.95, bf16[1,128,1280]{2,1,0:T(8,128)(2,1)S(1)} %get-tuple-element.94, bf16[1,128,1280]{2,1,0:T(8,128)(2,1)S(1)} %get-tuple-element.93, bf16[1,128,1280]{2,1,0:T(8,128)(2,1)S(1)} %get-tuple-element.92), kind=kLoop, calls=%fused_computation | loop fusion | flops 1966080 | bytes 2621440 | tf_op jit(solution)/shard_map/stack | solution.py:259
  11.5 3.9 %collective-permute-start.3 = (bf16[256,512]{1,0:T(8,128)(2,1)S(1)}, bf16[256,512]{1,0:T(8,128)(2,1)S(1)}, u32[]{:S(2)}, u32[]{:S(2)}) collective-permute-start(bf16[256,512]{1,0:T(8,128)(2,1)S(1)} %pad_maximum_fusion.1), channel_id=1, source_target_pairs={{0,16},{16,0},{1,17},{17,1},{2,18},{18,2},{3,19},{19,3},{4,20},{20... | collective-permute-start | bytes 786440 | tf_op jit(solution)/shard_map/ppermute | solution.py:256
  15.5 5.0 %all-to-all-start = ((bf16[4,128,1280]{2,1,0:T(8,128)(2,1)}), bf16[4,128,1280]{2,1,0:T(8,128)(2,1)}, u32[]{:S(2)}, u32[]{:S(2)}) async-start(bf16[4,128,1280]{2,1,0:T(8,128)(2,1)} %pad_maximum_fusion), calls=%async_computation | async-start | bytes 2621440 | tf_op jit(solution)/shard_map/all_to_all | solution.py:268
  21.2 3.2 %collective-permute-done.3 = bf16[256,512]{1,0:T(8,128)(2,1)S(1)} collective-permute-done((bf16[256,512]{1,0:T(8,128)(2,1)S(1)}, bf16[256,512]{1,0:T(8,128)(2,1)S(1)}, u32[]{:S(2)}, u32[]{:S(2)}) %collective-permute-start.3) | collective-permute-done | bytes 262176 | tf_op jit(solution)/shard_map/ppermute | solution.py:256
  24.6 6.1 %probs.1 = (bf16[4,512,1024]{2,1,0:T(8,128)(2,1)}, f32[512,512]{1,0:T(8,128)S(1)}) custom-call(bf16[128,4096]{1,0:T(8,128)(2,1)S(1)} %bitcast.76, bf16[512,512]{1,0:T(8,128)(2,1)S(1)} %constant_dynamic-update-slice_fusion.k_ref, bf16[128,4096]{1,0:T(8,128)(2,1)S(1)} %bitcast.78, f32[512,128]{1,0:T(8,128)S(1)} %add_select_fusion.bias_ref), custom_call_target="tpu_custom_call" | custom-call | flops 65536 | bytes 65536 | tf_op jit(solution)/shard_map/probs/pallas_call | solution.py:68
  30.8 0.8 copy-done.2
  31.8 4.3 %all-to-all-done = bf16[4,128,1280]{2,1,0:T(8,128)(2,1)} async-done(((bf16[4,128,1280]{2,1,0:T(8,128)(2,1)}), bf16[4,128,1280]{2,1,0:T(8,128)(2,1)}, u32[]{:S(2)}, u32[]{:S(2)}) %all-to-all-start) | async-done | bytes 1310752 | tf_op jit(solution)/shard_map/all_to_all | solution.py:268
  36.1 2.2 %fusion.48 = f32[4,128,512]{2,1,0:T(8,128)S(1)} fusion(bf16[4,128,1280]{2,1,0:T(8,128)(2,1)} %bitcast.11, bf16[1280,512,1]{1,0,2:T(8,128)(2,1)S(1)} %bitcast.79), kind=kOutput, calls=%fused_computation.114 | convolution fusion | flops 671088640 | bytes 3670016 | tf_op jit(solution)/shard_map/dot_general | solution.py:283
  38.5 3.5 %collective-permute-start.7 = (bf16[128,512]{1,0:T(8,128)(2,1)S(1)}, bf16[128,512]{1,0:T(8,128)(2,1)S(1)}, u32[]{:S(2)}, u32[]{:S(2)}) collective-permute-start(bf16[128,512]{1,0:T(8,128)(2,1)S(1)} %get-tuple-element.80), channel_id=1, source_target_pairs={{0,4},{2,6},{4,0},{6,2},{1,5},{3,7},{5,1},{7,3},{8,12},{10,14},{12... | collective-permute-start | bytes 393224 | tf_op jit(solution)/shard_map/ppermute | solution.py:289
  42.0 0.6 collective-permute-start.8
  42.6 2.4 %collective-permute-start.14 = (bf16[128,512]{1,0:T(8,128)(2,1)S(1)}, bf16[128,512]{1,0:T(8,128)(2,1)S(1)}, u32[]{:S(2)}, u32[]{:S(2)}) collective-permute-start(bf16[128,512]{1,0:T(8,128)(2,1)S(1)} %get-tuple-element.54), channel_id=1, source_target_pairs={{0,64},{32,96},{64,0},{96,32},{1,65},{33,97},{65,1},{97,33},{2,66}... | collective-permute-start | bytes 393224 | tf_op jit(solution)/shard_map/ppermute | solution.py:238
  45.0 1.0 collective-permute-start.15
  46.1 2.3 %collective-permute-start.13 = (bf16[128,512]{1,0:T(8,128)(2,1)S(1)}, bf16[128,512]{1,0:T(8,128)(2,1)S(1)}, u32[]{:S(2)}, u32[]{:S(2)}) collective-permute-start(bf16[128,512]{1,0:T(8,128)(2,1)S(1)} %fusion.10), channel_id=1, source_target_pairs={{0,96},{32,0},{64,32},{96,64},{1,97},{33,1},{65,33},{97,65},{2,98}... | collective-permute-start | bytes 393224 | tf_op jit(solution)/shard_map/ppermute | solution.py:236
  48.6 2.5 %collective-permute-start.11 = (bf16[128,512]{1,0:T(8,128)(2,1)S(1)}, bf16[128,512]{1,0:T(8,128)(2,1)S(1)}, u32[]{:S(2)}, u32[]{:S(2)}) collective-permute-start(bf16[128,512]{1,0:T(8,128)(2,1)S(1)} %fusion.26), channel_id=1, source_target_pairs={{0,64},{32,96},{64,0},{96,32},{1,65},{33,97},{65,1},{97,33},{2,66}... | collective-permute-start | bytes 393224 | tf_op jit(solution)/shard_map/ppermute | solution.py:197
  51.0 1.5 %collective-permute-done.13 = bf16[128,512]{1,0:T(8,128)(2,1)S(1)} collective-permute-done((bf16[128,512]{1,0:T(8,128)(2,1)S(1)}, bf16[128,512]{1,0:T(8,128)(2,1)S(1)}, u32[]{:S(2)}, u32[]{:S(2)}) %collective-permute-start.13) | collective-permute-done | bytes 131104 | tf_op jit(solution)/shard_map/ppermute | solution.py:236
  52.5 3.7 %collective-permute-start.12 = (bf16[128,512]{1,0:T(8,128)(2,1)S(1)}, bf16[128,512]{1,0:T(8,128)(2,1)S(1)}, u32[]{:S(2)}, u32[]{:S(2)}) collective-permute-start(bf16[128,512]{1,0:T(8,128)(2,1)S(1)} %fusion.26), channel_id=1, source_target_pairs={{0,96},{32,0},{64,32},{96,64},{1,97},{33,1},{65,33},{97,65},{2,98}... | collective-permute-start | bytes 393224 | tf_op jit(solution)/shard_map/ppermute | solution.py:197
  56.3 1.5 %collective-permute-start.17 = (bf16[128,512]{1,0:T(8,128)(2,1)S(1)}, bf16[128,512]{1,0:T(8,128)(2,1)S(1)}, u32[]{:S(2)}, u32[]{:S(2)}) collective-permute-start(bf16[128,512]{1,0:T(8,128)(2,1)S(1)} %fusion.15.refs_0_), channel_id=1, source_target_pairs={{0,2},{2,4},{4,6},{6,0},{1,3},{3,5},{5,7},{7,1},{8,10},{10,12},{12... | collective-permute-start | bytes 393224 | tf_op jit(solution)/shard_map/ppermute | solution.py:197
  57.8 1.5 %collective-permute-start.18 = (bf16[128,512]{1,0:T(8,128)(2,1)S(1)}, bf16[128,512]{1,0:T(8,128)(2,1)S(1)}, u32[]{:S(2)}, u32[]{:S(2)}) collective-permute-start(bf16[128,512]{1,0:T(8,128)(2,1)S(1)} %fusion.15.refs_0_), channel_id=1, source_target_pairs={{0,4},{2,6},{4,0},{6,2},{1,5},{3,7},{5,1},{7,3},{8,12},{10,14},{12... | collective-permute-start | bytes 393224 | tf_op jit(solution)/shard_map/ppermute | solution.py:197
  59.3 0.7 collective-permute-start.19
  60.1 0.7 pad_maximum_fusion.3
  60.8 0.6 collective-permute-done.17.refs_1_
  61.3 3.1 %collective-permute-done.18.refs_2_ = bf16[128,512]{1,0:T(8,128)(2,1)S(1)} collective-permute-done((bf16[128,512]{1,0:T(8,128)(2,1)S(1)}, bf16[128,512]{1,0:T(8,128)(2,1)S(1)}, u32[]{:S(2)}, u32[]{:S(2)}) %collective-permute-start.18) | collective-permute-done | bytes 131104 | tf_op jit(solution)/shard_map/ppermute | solution.py:197
  64.4 1.3 %collective-permute-done.19.refs_3_ = bf16[128,512]{1,0:T(8,128)(2,1)S(1)} collective-permute-done((bf16[128,512]{1,0:T(8,128)(2,1)S(1)}, bf16[128,512]{1,0:T(8,128)(2,1)S(1)}, u32[]{:S(2)}, u32[]{:S(2)}) %collective-permute-start.19) | collective-permute-done | bytes 131104 | tf_op jit(solution)/shard_map/ppermute | solution.py:197
  65.7 4.5 %grads.1 = (bf16[512,1280]{1,0:T(8,128)(2,1)}, f32[2,320,512]{2,1,0:T(8,128)}, bf16[2,320,512]{2,1,0:T(8,128)(2,1)S(1)}) custom-call(s32[2]{0:T(128)S(1)} %pad_add_fusion.at_ref, bf16[512,1280]{1,0:T(8,128)(2,1)} %bitcast.8.crossed_ref, bf16[1280,512]{1,0:T(8,128)(2,1)S(1)} %bitcast.80, bf16[128,512]{1,0:T(8,128)(2,1)S(1)} %fusion.15.refs_0_, ...), custom_call_target="tpu_custom_call" | custom-call | flops 1342177280 | bytes 8388608 | tf_op jit(solution)/shard_map/grads/pallas_call | solution.py:154
  70.4 4.8 %all-to-all-start.1 = ((bf16[4,128,1280]{2,1,0:T(8,128)(2,1)}), bf16[4,128,1280]{2,1,0:T(8,128)(2,1)}, u32[]{:S(2)}, u32[]{:S(2)}) async-start(bf16[4,128,1280]{2,1,0:T(8,128)(2,1)} %bitcast.82), calls=%async_computation.1 | async-start | bytes 2621440 | tf_op jit(solution)/shard_map/all_to_all | solution.py:347
  75.3 1.9 %fusion.29 = (bf16[160,512]{1,0:T(8,128)(2,1)}, bf16[160,512]{1,0:T(8,128)(2,1)}, bf16[160,512]{1,0:T(8,128)(2,1)}) fusion(f32[2,2,160,512]{3,2,1,0:T(8,128)S(1)} %bitcast.83, s32[]{:T(128)S(6)} %select_n.328, s32[]{:T(128)S(6)} %select_n.330, bf16[2,2,160,512]{3,2,1,0:T(8,128)(2,1)} %bitcast.26, s32[]{:T(128)S(6)} %select_n.323, s32[]{:T(128)S(6)} %select_n.325, ...), kind=kLoop, calls=%fused_computation.66 | loop fusion | flops 737280 | bytes 1966104 | tf_op jit(solution)/shard_map/convert_element_type | solution.py:319
  77.2 1.0 collective-permute-start.25
  78.2 3.6 %collective-permute-start.26 = (bf16[160,512]{1,0:T(8,128)(2,1)}, bf16[160,512]{1,0:T(8,128)(2,1)}, u32[]{:S(2)}, u32[]{:S(2)}) collective-permute-start(bf16[160,512]{1,0:T(8,128)(2,1)} %get-tuple-element.59), channel_id=1, source_target_pairs={{0,16},{8,24},{16,0},{24,8},{1,17},{9,25},{17,1},{25,9},{2,18},{10... | collective-permute-start | bytes 491528 | tf_op jit(solution)/shard_map/ppermute | solution.py:321
  81.7 1.0 collective-permute-start.27
  82.9 7.4 %scores.1 = (bf16[128,4096]{1,0:T(8,128)(2,1)}, f32[512,512]{1,0:T(8,128)S(1)}) custom-call(bf16[128,4096]{1,0:T(8,128)(2,1)} %bitcast.75, bf16[512,512]{1,0:T(8,128)(2,1)S(1)} %constant_dynamic-update-slice_fusion.k_ref, bf16[128,4096]{1,0:T(8,128)(2,1)} %bitcast.77, bf16[512,512]{1,0:T(8,128)(2,1)S(1)} %constant_dynamic-update-slice_fusion.1.v_ref, ...), custom_call_target="tpu_custom_call" | custom-call | flops 1610612736 | bytes 8388608 | tf_op jit(solution)/shard_map/scores/pallas_call | solution.py:94
  90.4 0.7 collective-permute-start.21
  91.0 1.3 %fusion.3 = bf16[160,512]{1,0:T(8,128)(2,1)S(1)} fusion(bf16[160,512]{1,0:T(8,128)(2,1)} %collective-permute-done.27, bf16[160,512]{1,0:T(8,128)(2,1)} %collective-permute-done.26, bf16[160,512]{1,0:T(8,128)(2,1)} %collective-permute-done.25, f32[2,2,160,512]{3,2,1,0:T(8,128)S(1)} %bitcast.84, s32[]{:T(128)S(6)} %select_n.341, s32[]{:T(128)S(6)} %select_n.343, ...), kind=kLoop, calls=%fused_computation.17 | loop fusion | flops 737280 | bytes 1146888 | tf_op jit(solution)/shard_map/convert_element_type | solution.py:331
  92.3 0.6 collective-permute-start.28
  93.3 2.9 %collective-permute-start.30 = (bf16[160,512]{1,0:T(8,128)(2,1)S(1)}, bf16[160,512]{1,0:T(8,128)(2,1)S(1)}, u32[]{:S(2)}, u32[]{:S(2)}) collective-permute-start(bf16[160,512]{1,0:T(8,128)(2,1)S(1)} %fusion.3), channel_id=1, source_target_pairs={{0,96},{32,0},{64,32},{96,64},{1,97},{33,1},{65,33},{97,65},{2,98}... | collective-permute-start | bytes 491528 | tf_op jit(solution)/shard_map/ppermute | solution.py:197
  96.1 3.4 %collective-permute-done.21 = bf16[256,512]{1,0:T(8,128)(2,1)S(1)} collective-permute-done((bf16[256,512]{1,0:T(8,128)(2,1)S(1)}, bf16[256,512]{1,0:T(8,128)(2,1)S(1)}, u32[]{:S(2)}, u32[]{:S(2)}) %collective-permute-start.21) | collective-permute-done | bytes 262176 | tf_op jit(solution)/shard_map/ppermute | solution.py:333
  99.7 0.5 collective-permute-start.23
  100.6 0.4 collective-permute-done.28
  101.0 2.4 %collective-permute-start.22 = (bf16[128,512]{1,0:T(8,128)(2,1)S(1)}, bf16[128,512]{1,0:T(8,128)(2,1)S(1)}, u32[]{:S(2)}, u32[]{:S(2)}) collective-permute-start(bf16[128,512]{1,0:T(8,128)(2,1)S(1)} %get-tuple-element.52), channel_id=1, source_target_pairs={{0,96},{32,0},{64,32},{96,64},{1,97},{33,1},{65,33},{97,65},{2,98}... | collective-permute-start | bytes 393224 | tf_op jit(solution)/shard_map/ppermute | solution.py:236
  103.5 3.8 %collective-permute-start.31 = (bf16[160,512]{1,0:T(8,128)(2,1)S(1)}, bf16[160,512]{1,0:T(8,128)(2,1)S(1)}, u32[]{:S(2)}, u32[]{:S(2)}) collective-permute-start(bf16[160,512]{1,0:T(8,128)(2,1)S(1)} %add_convert_fusion), channel_id=1, source_target_pairs={{0,16},{16,0},{1,17},{17,1},{2,18},{18,2},{3,19},{19,3},{4,20},{20... | collective-permute-start | bytes 491528 | tf_op jit(solution)/shard_map/ppermute | solution.py:338
  107.4 1.4 %slice_bitcast_fusion = (bf16[128,1280]{1,0:T(8,128)(2,1)S(1)}, bf16[128,1280]{1,0:T(8,128)(2,1)S(1)}, bf16[128,1280]{1,0:T(8,128)(2,1)S(1)}, bf16[128,1280]{1,0:T(8,128)(2,1)S(1)}) fusion(bf16[4,128,1280]{2,1,0:T(8,128)(2,1)} %all-to-all-done.1), kind=kLoop, calls=%fused_computation.18 | loop fusion | bytes 2621440 | tf_op jit(solution)/shard_map/squeeze | solution.py:350
  109.0 1.0 fusion.33
  110.0 1.2 %collective-permute-done.31 = bf16[160,512]{1,0:T(8,128)(2,1)S(1)} collective-permute-done((bf16[160,512]{1,0:T(8,128)(2,1)S(1)}, bf16[160,512]{1,0:T(8,128)(2,1)S(1)}, u32[]{:S(2)}, u32[]{:S(2)}) %collective-permute-start.31) | collective-permute-done | bytes 163872 | tf_op jit(solution)/shard_map/ppermute | solution.py:338
  111.2 0.9 fusion
  (99 shorter events, 3.6 us)
Async XLA Ops:
  0.6 10.8 %collective-permute-start = (bf16[128,512]{1,0:T(8,128)(2,1)}, bf16[128,512]{1,0:T(8,128)(2,1)S(1)}, u32[]{:S(2)}, u32[]{:S(2)}) collective-permute-start(bf16[128,512]{1,0:T(8,128)(2,1)} %bitcast.90), channel_id=1, source_target_pairs={{0,32},{32,64},{64,96},{96,0},{1,33},{33,65},{65,97},{97,1},{2,34}... | collective-permute-start | bytes 393224 | tf_op jit(solution)/shard_map/ppermute | solution.py:197
  2.3 9.2 %collective-permute-start.1 = (bf16[128,512]{1,0:T(8,128)(2,1)}, bf16[128,512]{1,0:T(8,128)(2,1)S(1)}, u32[]{:S(2)}, u32[]{:S(2)}) collective-permute-start(bf16[128,512]{1,0:T(8,128)(2,1)} %bitcast.91), channel_id=1, source_target_pairs={{0,64},{32,96},{64,0},{96,32},{1,65},{33,97},{65,1},{97,33},{2,66}... | collective-permute-start | bytes 393224 | tf_op jit(solution)/shard_map/ppermute | solution.py:197
  5.2 6.3 %collective-permute-start.2 = (bf16[128,512]{1,0:T(8,128)(2,1)}, bf16[128,512]{1,0:T(8,128)(2,1)S(1)}, u32[]{:S(2)}, u32[]{:S(2)}) collective-permute-start(bf16[128,512]{1,0:T(8,128)(2,1)} %bitcast.92), channel_id=1, source_target_pairs={{0,96},{32,0},{64,32},{96,64},{1,97},{33,1},{65,33},{97,65},{2,98}... | collective-permute-start | bytes 393224 | tf_op jit(solution)/shard_map/ppermute | solution.py:197
  6.5 14.3 %collective-permute-start.4 = (bf16[320,512]{1,0:T(8,128)(2,1)}, bf16[320,512]{1,0:T(8,128)(2,1)S(1)}, u32[]{:S(2)}, u32[]{:S(2)}) collective-permute-start(bf16[320,512]{1,0:T(8,128)(2,1)} %param.9), channel_id=1, source_target_pairs={{0,8},{8,0},{1,9},{9,1},{2,10},{10,2},{3,11},{11,3},{4,12},{12,4},... | collective-permute-start | bytes 983048 | tf_op jit(solution)/shard_map/ppermute | solution.py:269
  10.1 1.4 %copy-start.6 = (bf16[1,128,512]{2,1,0:T(8,128)(2,1)S(1)}, bf16[1,128,512]{2,1,0:T(8,128)(2,1)}, u32[]{:S(2)}) copy-start(bf16[1,128,512]{2,1,0:T(8,128)(2,1)} %param.8) | copy-start | bytes 393220
  11.3 4.1 %copy-start.8 = (s32[1,1024]{1,0:T(1,128)S(1)}, s32[1,1024]{1,0:T(1,128)}, u32[]{:S(2)}) copy-start(s32[1,1024]{1,0:T(1,128)} %param.11) | copy-start | bytes 12292
  11.5 12.9 %collective-permute-start.3 = (bf16[256,512]{1,0:T(8,128)(2,1)S(1)}, bf16[256,512]{1,0:T(8,128)(2,1)S(1)}, u32[]{:S(2)}, u32[]{:S(2)}) collective-permute-start(bf16[256,512]{1,0:T(8,128)(2,1)S(1)} %pad_maximum_fusion.1), channel_id=1, source_target_pairs={{0,16},{16,0},{1,17},{17,1},{2,18},{18,2},{3,19},{19,3},{4,20},{20... | collective-permute-start | bytes 786440 | tf_op jit(solution)/shard_map/ppermute | solution.py:256
  15.5 5.4 %copy-start.5 = (bf16[320,512]{1,0:T(8,128)(2,1)S(1)}, bf16[320,512]{1,0:T(8,128)(2,1)}, u32[]{:S(2)}) copy-start(bf16[320,512]{1,0:T(8,128)(2,1)} %param.9) | copy-start | bytes 983044
  15.5 20.6 %all-to-all-start = ((bf16[4,128,1280]{2,1,0:T(8,128)(2,1)}), bf16[4,128,1280]{2,1,0:T(8,128)(2,1)}, u32[]{:S(2)}, u32[]{:S(2)}) async-start(bf16[4,128,1280]{2,1,0:T(8,128)(2,1)} %pad_maximum_fusion), calls=%async_computation | async-start | bytes 2621440 | tf_op jit(solution)/shard_map/all_to_all | solution.py:268
  21.0 9.8 %collective-permute-start.5 = (bf16[2,320,512]{2,1,0:T(8,128)(2,1)S(1)}, bf16[2,320,512]{2,1,0:T(8,128)(2,1)S(1)}, u32[]{:S(2)}, u32[]{:S(2)}) collective-permute-start(bf16[2,320,512]{2,1,0:T(8,128)(2,1)S(1)} %maximum_select_fusion.2), channel_id=1, source_target_pairs={{0,1},{1,0},{2,3},{3,2},{4,5},{5,4},{6,7},{7,6},{8,9},{9,8},{10,11... | collective-permute-start | bytes 1966088 | tf_op jit(solution)/shard_map/ppermute | solution.py:273
  21.1 3.5 %copy-start = (bf16[1,128,4096]{2,1,0:T(8,128)(2,1)S(1)}, bf16[1,128,4096]{2,1,0:T(8,128)(2,1)}, u32[]{:S(2)}) copy-start(bf16[1,128,4096]{2,1,0:T(8,128)(2,1)} %param.7) | copy-start | bytes 3145732
  21.1 3.5 %copy-start.1 = (bf16[1,128,4096]{2,1,0:T(8,128)(2,1)S(1)}, bf16[1,128,4096]{2,1,0:T(8,128)(2,1)}, u32[]{:S(2)}) copy-start(bf16[1,128,4096]{2,1,0:T(8,128)(2,1)} %param.10) | copy-start | bytes 3145732
  30.6 1.0 copy-start.2
  30.7 11.8 %collective-permute-start.9 = (bf16[256,512]{1,0:T(8,128)(2,1)S(1)}, bf16[256,512]{1,0:T(8,128)(2,1)S(1)}, u32[]{:S(2)}, u32[]{:S(2)}) collective-permute-start(bf16[256,512]{1,0:T(8,128)(2,1)S(1)} %pad_maximum_fusion.2), channel_id=1, source_target_pairs={{0,16},{16,0},{1,17},{17,1},{2,18},{18,2},{3,19},{19,3},{4,20},{20... | collective-permute-start | bytes 786440 | tf_op jit(solution)/shard_map/ppermute | solution.py:281
  36.1 6.5 %copy-start.3 = (f32[512,512]{1,0:T(8,128)S(1)}, f32[512,512]{1,0:T(8,128)}, u32[]{:S(2)}) copy-start(f32[512,512]{1,0:T(8,128)} %copy-done.2) | copy-start | bytes 3145732
  38.4 7.6 %collective-permute-start.6 = (bf16[128,512]{1,0:T(8,128)(2,1)S(1)}, bf16[128,512]{1,0:T(8,128)(2,1)S(1)}, u32[]{:S(2)}, u32[]{:S(2)}) collective-permute-start(bf16[128,512]{1,0:T(8,128)(2,1)S(1)} %get-tuple-element.81), channel_id=1, source_target_pairs={{0,2},{2,4},{4,6},{6,0},{1,3},{3,5},{5,7},{7,1},{8,10},{10,12},{12... | collective-permute-start | bytes 393224 | tf_op jit(solution)/shard_map/ppermute | solution.py:289
  38.5 9.9 %collective-permute-start.7 = (bf16[128,512]{1,0:T(8,128)(2,1)S(1)}, bf16[128,512]{1,0:T(8,128)(2,1)S(1)}, u32[]{:S(2)}, u32[]{:S(2)}) collective-permute-start(bf16[128,512]{1,0:T(8,128)(2,1)S(1)} %get-tuple-element.80), channel_id=1, source_target_pairs={{0,4},{2,6},{4,0},{6,2},{1,5},{3,7},{5,1},{7,3},{8,12},{10,14},{12... | collective-permute-start | bytes 393224 | tf_op jit(solution)/shard_map/ppermute | solution.py:289
  42.0 6.4 %collective-permute-start.8 = (bf16[128,512]{1,0:T(8,128)(2,1)S(1)}, bf16[128,512]{1,0:T(8,128)(2,1)S(1)}, u32[]{:S(2)}, u32[]{:S(2)}) collective-permute-start(bf16[128,512]{1,0:T(8,128)(2,1)S(1)} %get-tuple-element.79), channel_id=1, source_target_pairs={{0,6},{2,0},{4,2},{6,4},{1,7},{3,1},{5,3},{7,5},{8,14},{10,8},{12,... | collective-permute-start | bytes 393224 | tf_op jit(solution)/shard_map/ppermute | solution.py:289
  42.6 13.5 %collective-permute-start.14 = (bf16[128,512]{1,0:T(8,128)(2,1)S(1)}, bf16[128,512]{1,0:T(8,128)(2,1)S(1)}, u32[]{:S(2)}, u32[]{:S(2)}) collective-permute-start(bf16[128,512]{1,0:T(8,128)(2,1)S(1)} %get-tuple-element.54), channel_id=1, source_target_pairs={{0,64},{32,96},{64,0},{96,32},{1,65},{33,97},{65,1},{97,33},{2,66}... | collective-permute-start | bytes 393224 | tf_op jit(solution)/shard_map/ppermute | solution.py:238
  45.0 11.2 %collective-permute-start.15 = (bf16[128,512]{1,0:T(8,128)(2,1)S(1)}, bf16[128,512]{1,0:T(8,128)(2,1)S(1)}, u32[]{:S(2)}, u32[]{:S(2)}) collective-permute-start(bf16[128,512]{1,0:T(8,128)(2,1)S(1)} %get-tuple-element.54), channel_id=1, source_target_pairs={{0,32},{32,64},{64,96},{96,0},{1,33},{33,65},{65,97},{97,1},{2,34}... | collective-permute-start | bytes 393224 | tf_op jit(solution)/shard_map/ppermute | solution.py:237
  46.1 6.4 %collective-permute-start.13 = (bf16[128,512]{1,0:T(8,128)(2,1)S(1)}, bf16[128,512]{1,0:T(8,128)(2,1)S(1)}, u32[]{:S(2)}, u32[]{:S(2)}) collective-permute-start(bf16[128,512]{1,0:T(8,128)(2,1)S(1)} %fusion.10), channel_id=1, source_target_pairs={{0,96},{32,0},{64,32},{96,64},{1,97},{33,1},{65,33},{97,65},{2,98}... | collective-permute-start | bytes 393224 | tf_op jit(solution)/shard_map/ppermute | solution.py:236
  48.5 10.9 %collective-permute-start.10 = (bf16[128,512]{1,0:T(8,128)(2,1)S(1)}, bf16[128,512]{1,0:T(8,128)(2,1)S(1)}, u32[]{:S(2)}, u32[]{:S(2)}) collective-permute-start(bf16[128,512]{1,0:T(8,128)(2,1)S(1)} %fusion.26), channel_id=1, source_target_pairs={{0,32},{32,64},{64,96},{96,0},{1,33},{33,65},{65,97},{97,1},{2,34}... | collective-permute-start | bytes 393224 | tf_op jit(solution)/shard_map/ppermute | solution.py:197
  48.6 11.5 %collective-permute-start.11 = (bf16[128,512]{1,0:T(8,128)(2,1)S(1)}, bf16[128,512]{1,0:T(8,128)(2,1)S(1)}, u32[]{:S(2)}, u32[]{:S(2)}) collective-permute-start(bf16[128,512]{1,0:T(8,128)(2,1)S(1)} %fusion.26), channel_id=1, source_target_pairs={{0,64},{32,96},{64,0},{96,32},{1,65},{33,97},{65,1},{97,33},{2,66}... | collective-permute-start | bytes 393224 | tf_op jit(solution)/shard_map/ppermute | solution.py:197
  52.5 7.5 %collective-permute-start.12 = (bf16[128,512]{1,0:T(8,128)(2,1)S(1)}, bf16[128,512]{1,0:T(8,128)(2,1)S(1)}, u32[]{:S(2)}, u32[]{:S(2)}) collective-permute-start(bf16[128,512]{1,0:T(8,128)(2,1)S(1)} %fusion.26), channel_id=1, source_target_pairs={{0,96},{32,0},{64,32},{96,64},{1,97},{33,1},{65,33},{97,65},{2,98}... | collective-permute-start | bytes 393224 | tf_op jit(solution)/shard_map/ppermute | solution.py:197
  56.3 5.0 %collective-permute-start.17 = (bf16[128,512]{1,0:T(8,128)(2,1)S(1)}, bf16[128,512]{1,0:T(8,128)(2,1)S(1)}, u32[]{:S(2)}, u32[]{:S(2)}) collective-permute-start(bf16[128,512]{1,0:T(8,128)(2,1)S(1)} %fusion.15.refs_0_), channel_id=1, source_target_pairs={{0,2},{2,4},{4,6},{6,0},{1,3},{3,5},{5,7},{7,1},{8,10},{10,12},{12... | collective-permute-start | bytes 393224 | tf_op jit(solution)/shard_map/ppermute | solution.py:197
  57.8 6.6 %collective-permute-start.18 = (bf16[128,512]{1,0:T(8,128)(2,1)S(1)}, bf16[128,512]{1,0:T(8,128)(2,1)S(1)}, u32[]{:S(2)}, u32[]{:S(2)}) collective-permute-start(bf16[128,512]{1,0:T(8,128)(2,1)S(1)} %fusion.15.refs_0_), channel_id=1, source_target_pairs={{0,4},{2,6},{4,0},{6,2},{1,5},{3,7},{5,1},{7,3},{8,12},{10,14},{12... | collective-permute-start | bytes 393224 | tf_op jit(solution)/shard_map/ppermute | solution.py:197
  59.3 6.4 %collective-permute-start.19 = (bf16[128,512]{1,0:T(8,128)(2,1)S(1)}, bf16[128,512]{1,0:T(8,128)(2,1)S(1)}, u32[]{:S(2)}, u32[]{:S(2)}) collective-permute-start(bf16[128,512]{1,0:T(8,128)(2,1)S(1)} %fusion.15.refs_0_), channel_id=1, source_target_pairs={{0,6},{2,0},{4,2},{6,4},{1,7},{3,1},{5,3},{7,5},{8,14},{10,8},{12,... | collective-permute-start | bytes 393224 | tf_op jit(solution)/shard_map/ppermute | solution.py:197
  70.2 5.1 %collective-permute-start.20 = (bf16[2,320,512]{2,1,0:T(8,128)(2,1)S(1)}, bf16[2,320,512]{2,1,0:T(8,128)(2,1)}, u32[]{:S(2)}, u32[]{:S(2)}) collective-permute-start(bf16[2,320,512]{2,1,0:T(8,128)(2,1)S(1)} %get-tuple-element.44), channel_id=1, source_target_pairs={{0,1},{1,0},{2,3},{3,2},{4,5},{5,4},{6,7},{7,6},{8,9},{9,8},{10,11... | collective-permute-start | bytes 1966088 | tf_op jit(solution)/shard_map/ppermute | solution.py:308
  70.2 12.6 %collective-permute-start.16 = (bf16[256,512]{1,0:T(8,128)(2,1)}, bf16[256,512]{1,0:T(8,128)(2,1)S(1)}, u32[]{:S(2)}, u32[]{:S(2)}) collective-permute-start(bf16[256,512]{1,0:T(8,128)(2,1)} %pad_maximum_fusion.3), channel_id=1, source_target_pairs={{0,16},{16,0},{1,17},{17,1},{2,18},{18,2},{3,19},{19,3},{4,20},{20... | collective-permute-start | bytes 786440 | tf_op jit(solution)/shard_map/ppermute | solution.py:304
  70.4 4.8 %copy-start.4 = (f32[2,320,512]{2,1,0:T(8,128)S(1)}, f32[2,320,512]{2,1,0:T(8,128)}, u32[]{:S(2)}) copy-start(f32[2,320,512]{2,1,0:T(8,128)} %get-tuple-element.43) | copy-start | bytes 3932164
  70.4 36.9 %all-to-all-start.1 = ((bf16[4,128,1280]{2,1,0:T(8,128)(2,1)}), bf16[4,128,1280]{2,1,0:T(8,128)(2,1)}, u32[]{:S(2)}, u32[]{:S(2)}) async-start(bf16[4,128,1280]{2,1,0:T(8,128)(2,1)} %bitcast.82), calls=%async_computation.1 | async-start | bytes 2621440 | tf_op jit(solution)/shard_map/all_to_all | solution.py:347
  77.2 13.8 %collective-permute-start.25 = (bf16[160,512]{1,0:T(8,128)(2,1)}, bf16[160,512]{1,0:T(8,128)(2,1)}, u32[]{:S(2)}, u32[]{:S(2)}) collective-permute-start(bf16[160,512]{1,0:T(8,128)(2,1)} %get-tuple-element.60), channel_id=1, source_target_pairs={{0,8},{8,16},{16,24},{24,0},{1,9},{9,17},{17,25},{25,1},{2,10},{10... | collective-permute-start | bytes 491528 | tf_op jit(solution)/shard_map/ppermute | solution.py:321
  78.2 12.9 %collective-permute-start.26 = (bf16[160,512]{1,0:T(8,128)(2,1)}, bf16[160,512]{1,0:T(8,128)(2,1)}, u32[]{:S(2)}, u32[]{:S(2)}) collective-permute-start(bf16[160,512]{1,0:T(8,128)(2,1)} %get-tuple-element.59), channel_id=1, source_target_pairs={{0,16},{8,24},{16,0},{24,8},{1,17},{9,25},{17,1},{25,9},{2,18},{10... | collective-permute-start | bytes 491528 | tf_op jit(solution)/shard_map/ppermute | solution.py:321
  81.7 9.3 %collective-permute-start.27 = (bf16[160,512]{1,0:T(8,128)(2,1)}, bf16[160,512]{1,0:T(8,128)(2,1)}, u32[]{:S(2)}, u32[]{:S(2)}) collective-permute-start(bf16[160,512]{1,0:T(8,128)(2,1)} %get-tuple-element.58), channel_id=1, source_target_pairs={{0,24},{8,0},{16,8},{24,16},{1,25},{9,1},{17,9},{25,17},{2,26},{10... | collective-permute-start | bytes 491528 | tf_op jit(solution)/shard_map/ppermute | solution.py:321
  90.4 9.2 %collective-permute-start.21 = (bf16[256,512]{1,0:T(8,128)(2,1)S(1)}, bf16[256,512]{1,0:T(8,128)(2,1)S(1)}, u32[]{:S(2)}, u32[]{:S(2)}) collective-permute-start(bf16[256,512]{1,0:T(8,128)(2,1)S(1)} %pad_maximum_fusion.4), channel_id=1, source_target_pairs={{0,16},{16,0},{1,17},{17,1},{2,18},{18,2},{3,19},{19,3},{4,20},{20... | collective-permute-start | bytes 786440 | tf_op jit(solution)/shard_map/ppermute | solution.py:333
  92.3 8.7 %collective-permute-start.28 = (bf16[160,512]{1,0:T(8,128)(2,1)S(1)}, bf16[160,512]{1,0:T(8,128)(2,1)S(1)}, u32[]{:S(2)}, u32[]{:S(2)}) collective-permute-start(bf16[160,512]{1,0:T(8,128)(2,1)S(1)} %fusion.3), channel_id=1, source_target_pairs={{0,64},{32,96},{64,0},{96,32},{1,65},{33,97},{65,1},{97,33},{2,66}... | collective-permute-start | bytes 491528 | tf_op jit(solution)/shard_map/ppermute | solution.py:197
  92.9 10.5 %collective-permute-start.29 = (bf16[160,512]{1,0:T(8,128)(2,1)S(1)}, bf16[160,512]{1,0:T(8,128)(2,1)S(1)}, u32[]{:S(2)}, u32[]{:S(2)}) collective-permute-start(bf16[160,512]{1,0:T(8,128)(2,1)S(1)} %fusion.3), channel_id=1, source_target_pairs={{0,32},{32,64},{64,96},{96,0},{1,33},{33,65},{65,97},{97,1},{2,34}... | collective-permute-start | bytes 491528 | tf_op jit(solution)/shard_map/ppermute | solution.py:197
  93.3 10.2 %collective-permute-start.30 = (bf16[160,512]{1,0:T(8,128)(2,1)S(1)}, bf16[160,512]{1,0:T(8,128)(2,1)S(1)}, u32[]{:S(2)}, u32[]{:S(2)}) collective-permute-start(bf16[160,512]{1,0:T(8,128)(2,1)S(1)} %fusion.3), channel_id=1, source_target_pairs={{0,96},{32,0},{64,32},{96,64},{1,97},{33,1},{65,33},{97,65},{2,98}... | collective-permute-start | bytes 491528 | tf_op jit(solution)/shard_map/ppermute | solution.py:197
  99.7 9.3 %collective-permute-start.23 = (bf16[128,512]{1,0:T(8,128)(2,1)S(1)}, bf16[128,512]{1,0:T(8,128)(2,1)S(1)}, u32[]{:S(2)}, u32[]{:S(2)}) collective-permute-start(bf16[128,512]{1,0:T(8,128)(2,1)S(1)} %convert_element_type.175), channel_id=1, source_target_pairs={{0,64},{32,96},{64,0},{96,32},{1,65},{33,97},{65,1},{97,33},{2,66}... | collective-permute-start | bytes 393224 | tf_op jit(solution)/shard_map/ppermute | solution.py:238
  100.2 8.8 %collective-permute-start.24 = (bf16[128,512]{1,0:T(8,128)(2,1)S(1)}, bf16[128,512]{1,0:T(8,128)(2,1)S(1)}, u32[]{:S(2)}, u32[]{:S(2)}) collective-permute-start(bf16[128,512]{1,0:T(8,128)(2,1)S(1)} %convert_element_type.175), channel_id=1, source_target_pairs={{0,32},{32,64},{64,96},{96,0},{1,33},{33,65},{65,97},{97,1},{2,34}... | collective-permute-start | bytes 393224 | tf_op jit(solution)/shard_map/ppermute | solution.py:237
  101.0 8.0 %collective-permute-start.22 = (bf16[128,512]{1,0:T(8,128)(2,1)S(1)}, bf16[128,512]{1,0:T(8,128)(2,1)S(1)}, u32[]{:S(2)}, u32[]{:S(2)}) collective-permute-start(bf16[128,512]{1,0:T(8,128)(2,1)S(1)} %get-tuple-element.52), channel_id=1, source_target_pairs={{0,96},{32,0},{64,32},{96,64},{1,97},{33,1},{65,33},{97,65},{2,98}... | collective-permute-start | bytes 393224 | tf_op jit(solution)/shard_map/ppermute | solution.py:236
  103.5 7.6 %collective-permute-start.31 = (bf16[160,512]{1,0:T(8,128)(2,1)S(1)}, bf16[160,512]{1,0:T(8,128)(2,1)S(1)}, u32[]{:S(2)}, u32[]{:S(2)}) collective-permute-start(bf16[160,512]{1,0:T(8,128)(2,1)S(1)} %add_convert_fusion), channel_id=1, source_target_pairs={{0,16},{16,0},{1,17},{17,1},{2,18},{18,2},{3,19},{19,3},{4,20},{20... | collective-permute-start | bytes 491528 | tf_op jit(solution)/shard_map/ppermute | solution.py:338
  109.0 3.1 %copy-start.7 = (bf16[128,5120]{1,0:T(8,128)(2,1)}, bf16[128,5120]{1,0:T(8,128)(2,1)S(1)}, u32[]{:S(2)}) copy-start(bf16[128,5120]{1,0:T(8,128)(2,1)S(1)} %slice_dynamic-update-slice_fusion) | copy-start | bytes 3932164

commit v6 on v5

--- a/solution.py
+++ b/solution.py
@@ -300,7 +300,6 @@
 
     value_grad = summed(dv_own, held(dv_got, [values]), y)
     near = turns(value_grad, "x", 4)
-    v_sent = after(v_sent, value_grad)
     v_other = lax.ppermute(v_sent, "zh", SWAP)
 
     near = [value_grad] + list(held(near, [v_sent]))

time: 113 us -> 113 us (level)
  no operation moved by 1% of the time
where the time goes in v6:
time: 113 us; the launch traced here: 112 us
  starting transfers between devices  58.9 us (52%)
  waiting for transfers between devices  19 us (17%)
  Pallas kernels  17.9 us (16%)
  other arithmetic  8.86 us (8%)
  local copies, waits for them, and re-layouts  4.01 us (4%)
  matrix products  2.24 us (2%)
  between operations  1.17 us (1%)
    ppermute x12, starting transfers between devices, turns(): lax.ppermute(value, axis, turned(count, n))  19.6 us
    pallas_call x1, Pallas kernels, scores_call(): pl.pallas_call(scores_kernel, grid=(KEY_HEADS,), in_specs=[column(ROWS, G...  7.38 us
    pallas_call x1, Pallas kernels, probs_call(): pl.pallas_call(probs_kernel, grid=(KEY_HEADS,), in_specs=[column(ROWS, GR...  6.06 us
    ppermute x3, starting transfers between devices, on_device(): lax.ppermute(sent, ('zh', 'zl'), turned(4, step))  5.56 us
    ppermute x12, waiting for transfers between devices, turns(): lax.ppermute(value, axis, turned(count, n))  5.38 us
    all_to_all x1, starting transfers between devices, on_device(): lax.all_to_all(after(by_x, k_sent), 'x', 0, 0).reshape(4 * ROWS, 4 * each)  4.97 us
    all_to_all x1, starting transfers between devices, on_device(): back = lax.all_to_all(back.reshape(4, ROWS, 4 * each), 'x', 0, 0)  4.83 us
    ppermute x2, starting transfers between devices, returned(): from_next = lax.ppermute(before, 'y', turned(4, 3))  4.72 us
  transfers between devices with their start and end apart: 34, of which 9 were waited for; matrix products, arithmetic and copies ran while one was open for 12% of the time, Pallas kernels for 12%

profile of v6, /device:TPU:2, one launch (start us, length us, event | category | flops | bytes accessed | tf_op | source)
XLA Modules:
  0.0 112.1 jit_solution(16600134644840508657)
XLA Ops:
  0.6 1.6 %collective-permute-start = (bf16[128,512]{1,0:T(8,128)(2,1)}, bf16[128,512]{1,0:T(8,128)(2,1)S(1)}, u32[]{:S(2)}, u32[]{:S(2)}) collective-permute-start(bf16[128,512]{1,0:T(8,128)(2,1)} %bitcast.90), channel_id=1, source_target_pairs={{0,32},{32,64},{64,96},{96,0},{1,33},{33,65},{65,97},{97,1},{2,34}... | collective-permute-start | bytes 393224 | tf_op jit(solution)/shard_map/ppermute | solution.py:197
  2.3 2.9 %collective-permute-start.1 = (bf16[128,512]{1,0:T(8,128)(2,1)}, bf16[128,512]{1,0:T(8,128)(2,1)S(1)}, u32[]{:S(2)}, u32[]{:S(2)}) collective-permute-start(bf16[128,512]{1,0:T(8,128)(2,1)} %bitcast.91), channel_id=1, source_target_pairs={{0,64},{32,96},{64,0},{96,32},{1,65},{33,97},{65,1},{97,33},{2,66}... | collective-permute-start | bytes 393224 | tf_op jit(solution)/shard_map/ppermute | solution.py:197
  5.2 1.3 %collective-permute-start.2 = (bf16[128,512]{1,0:T(8,128)(2,1)}, bf16[128,512]{1,0:T(8,128)(2,1)S(1)}, u32[]{:S(2)}, u32[]{:S(2)}) collective-permute-start(bf16[128,512]{1,0:T(8,128)(2,1)} %bitcast.92), channel_id=1, source_target_pairs={{0,96},{32,0},{64,32},{96,64},{1,97},{33,1},{65,33},{97,65},{2,98}... | collective-permute-start | bytes 393224 | tf_op jit(solution)/shard_map/ppermute | solution.py:197
  6.5 1.9 %collective-permute-start.4 = (bf16[320,512]{1,0:T(8,128)(2,1)}, bf16[320,512]{1,0:T(8,128)(2,1)S(1)}, u32[]{:S(2)}, u32[]{:S(2)}) collective-permute-start(bf16[320,512]{1,0:T(8,128)(2,1)} %param.9), channel_id=1, source_target_pairs={{0,8},{8,0},{1,9},{9,1},{2,10},{10,2},{3,11},{11,3},{4,12},{12,4},... | collective-permute-start | bytes 983048 | tf_op jit(solution)/shard_map/ppermute | solution.py:269
  8.4 1.5 %fusion.41 = (bf16[128,640]{1,0:T(8,128)(2,1)S(1)}, bf16[128,640]{1,0:T(8,128)(2,1)S(1)}, bf16[128,640]{1,0:T(8,128)(2,1)S(1)}, bf16[128,640]{1,0:T(8,128)(2,1)S...) fusion(bf16[128,5120]{1,0:T(8,128)(2,1)} %bitcast.81), kind=kLoop, calls=%fused_computation.107 | loop fusion | bytes 2621440 | tf_op jit(solution)/shard_map/slice | solution.py:262
  10.1 1.2 %pad_maximum_fusion = bf16[4,128,1280]{2,1,0:T(8,128)(2,1)} fusion(bf16[1,128,1280]{2,1,0:T(8,128)(2,1)S(1)} %get-tuple-element.93, bf16[1,128,1280]{2,1,0:T(8,128)(2,1)S(1)} %get-tuple-element.92, bf16[1,128,1280]{2,1,0:T(8,128)(2,1)S(1)} %get-tuple-element.91, bf16[1,128,1280]{2,1,0:T(8,128)(2,1)S(1)} %get-tuple-element.90), kind=kLoop, calls=%fused_computation | loop fusion | flops 1966080 | bytes 2621440 | tf_op jit(solution)/shard_map/stack | solution.py:259
  11.5 3.9 %collective-permute-start.3 = (bf16[256,512]{1,0:T(8,128)(2,1)S(1)}, bf16[256,512]{1,0:T(8,128)(2,1)S(1)}, u32[]{:S(2)}, u32[]{:S(2)}) collective-permute-start(bf16[256,512]{1,0:T(8,128)(2,1)S(1)} %pad_maximum_fusion.1), channel_id=1, source_target_pairs={{0,16},{16,0},{1,17},{17,1},{2,18},{18,2},{3,19},{19,3},{4,20},{20... | collective-permute-start | bytes 786440 | tf_op jit(solution)/shard_map/ppermute | solution.py:256
  15.5 5.0 %all-to-all-start = ((bf16[4,128,1280]{2,1,0:T(8,128)(2,1)}), bf16[4,128,1280]{2,1,0:T(8,128)(2,1)}, u32[]{:S(2)}, u32[]{:S(2)}) async-start(bf16[4,128,1280]{2,1,0:T(8,128)(2,1)} %pad_maximum_fusion), calls=%async_computation | async-start | bytes 2621440 | tf_op jit(solution)/shard_map/all_to_all | solution.py:268
  21.2 3.2 %collective-permute-done.3 = bf16[256,512]{1,0:T(8,128)(2,1)S(1)} collective-permute-done((bf16[256,512]{1,0:T(8,128)(2,1)S(1)}, bf16[256,512]{1,0:T(8,128)(2,1)S(1)}, u32[]{:S(2)}, u32[]{:S(2)}) %collective-permute-start.3) | collective-permute-done | bytes 262176 | tf_op jit(solution)/shard_map/ppermute | solution.py:256
  24.6 6.1 %probs.1 = (bf16[4,512,1024]{2,1,0:T(8,128)(2,1)}, f32[512,512]{1,0:T(8,128)S(1)}) custom-call(bf16[128,4096]{1,0:T(8,128)(2,1)S(1)} %bitcast.76, bf16[512,512]{1,0:T(8,128)(2,1)S(1)} %constant_dynamic-update-slice_fusion.k_ref, bf16[128,4096]{1,0:T(8,128)(2,1)S(1)} %bitcast.78, f32[512,128]{1,0:T(8,128)S(1)} %add_select_fusion.bias_ref), custom_call_target="tpu_custom_call" | custom-call | flops 65536 | bytes 65536 | tf_op jit(solution)/shard_map/probs/pallas_call | solution.py:68
  30.8 0.8 copy-done.2
  31.8 4.3 %all-to-all-done = bf16[4,128,1280]{2,1,0:T(8,128)(2,1)} async-done(((bf16[4,128,1280]{2,1,0:T(8,128)(2,1)}), bf16[4,128,1280]{2,1,0:T(8,128)(2,1)}, u32[]{:S(2)}, u32[]{:S(2)}) %all-to-all-start) | async-done | bytes 1310752 | tf_op jit(solution)/shard_map/all_to_all | solution.py:268
  36.1 2.2 %fusion.48 = f32[4,128,512]{2,1,0:T(8,128)S(1)} fusion(bf16[4,128,1280]{2,1,0:T(8,128)(2,1)} %bitcast.11, bf16[1280,512,1]{1,0,2:T(8,128)(2,1)S(1)} %bitcast.79), kind=kOutput, calls=%fused_computation.114 | convolution fusion | flops 671088640 | bytes 3670016 | tf_op jit(solution)/shard_map/dot_general | solution.py:283
  38.5 3.5 %collective-permute-start.7 = (bf16[128,512]{1,0:T(8,128)(2,1)S(1)}, bf16[128,512]{1,0:T(8,128)(2,1)S(1)}, u32[]{:S(2)}, u32[]{:S(2)}) collective-permute-start(bf16[128,512]{1,0:T(8,128)(2,1)S(1)} %get-tuple-element.78), channel_id=1, source_target_pairs={{0,4},{2,6},{4,0},{6,2},{1,5},{3,7},{5,1},{7,3},{8,12},{10,14},{12... | collective-permute-start | bytes 393224 | tf_op jit(solution)/shard_map/ppermute | solution.py:289
  42.0 0.6 collective-permute-start.8
  42.6 2.4 %collective-permute-start.15 = (bf16[128,512]{1,0:T(8,128)(2,1)S(1)}, bf16[128,512]{1,0:T(8,128)(2,1)S(1)}, u32[]{:S(2)}, u32[]{:S(2)}) collective-permute-start(bf16[128,512]{1,0:T(8,128)(2,1)S(1)} %get-tuple-element.52), channel_id=1, source_target_pairs={{0,64},{32,96},{64,0},{96,32},{1,65},{33,97},{65,1},{97,33},{2,66}... | collective-permute-start | bytes 393224 | tf_op jit(solution)/shard_map/ppermute | solution.py:238
  45.0 1.0 collective-permute-start.16
  46.1 2.3 %collective-permute-start.14 = (bf16[128,512]{1,0:T(8,128)(2,1)S(1)}, bf16[128,512]{1,0:T(8,128)(2,1)S(1)}, u32[]{:S(2)}, u32[]{:S(2)}) collective-permute-start(bf16[128,512]{1,0:T(8,128)(2,1)S(1)} %fusion.10), channel_id=1, source_target_pairs={{0,96},{32,0},{64,32},{96,64},{1,97},{33,1},{65,33},{97,65},{2,98}... | collective-permute-start | bytes 393224 | tf_op jit(solution)/shard_map/ppermute | solution.py:236
  48.6 2.5 %collective-permute-start.11 = (bf16[128,512]{1,0:T(8,128)(2,1)S(1)}, bf16[128,512]{1,0:T(8,128)(2,1)S(1)}, u32[]{:S(2)}, u32[]{:S(2)}) collective-permute-start(bf16[128,512]{1,0:T(8,128)(2,1)S(1)} %fusion.26), channel_id=1, source_target_pairs={{0,64},{32,96},{64,0},{96,32},{1,65},{33,97},{65,1},{97,33},{2,66}... | collective-permute-start | bytes 393224 | tf_op jit(solution)/shard_map/ppermute | solution.py:197
  51.0 1.5 %collective-permute-done.14 = bf16[128,512]{1,0:T(8,128)(2,1)S(1)} collective-permute-done((bf16[128,512]{1,0:T(8,128)(2,1)S(1)}, bf16[128,512]{1,0:T(8,128)(2,1)S(1)}, u32[]{:S(2)}, u32[]{:S(2)}) %collective-permute-start.14) | collective-permute-done | bytes 131104 | tf_op jit(solution)/shard_map/ppermute | solution.py:236
  52.5 3.7 %collective-permute-start.12 = (bf16[128,512]{1,0:T(8,128)(2,1)S(1)}, bf16[128,512]{1,0:T(8,128)(2,1)S(1)}, u32[]{:S(2)}, u32[]{:S(2)}) collective-permute-start(bf16[128,512]{1,0:T(8,128)(2,1)S(1)} %fusion.26), channel_id=1, source_target_pairs={{0,96},{32,0},{64,32},{96,64},{1,97},{33,1},{65,33},{97,65},{2,98}... | collective-permute-start | bytes 393224 | tf_op jit(solution)/shard_map/ppermute | solution.py:197
  56.3 1.5 %collective-permute-start.17 = (bf16[128,512]{1,0:T(8,128)(2,1)S(1)}, bf16[128,512]{1,0:T(8,128)(2,1)S(1)}, u32[]{:S(2)}, u32[]{:S(2)}) collective-permute-start(bf16[128,512]{1,0:T(8,128)(2,1)S(1)} %fusion.15.refs_0_), channel_id=1, source_target_pairs={{0,2},{2,4},{4,6},{6,0},{1,3},{3,5},{5,7},{7,1},{8,10},{10,12},{12... | collective-permute-start | bytes 393224 | tf_op jit(solution)/shard_map/ppermute | solution.py:197
  57.8 1.5 %collective-permute-start.18 = (bf16[128,512]{1,0:T(8,128)(2,1)S(1)}, bf16[128,512]{1,0:T(8,128)(2,1)S(1)}, u32[]{:S(2)}, u32[]{:S(2)}) collective-permute-start(bf16[128,512]{1,0:T(8,128)(2,1)S(1)} %fusion.15.refs_0_), channel_id=1, source_target_pairs={{0,4},{2,6},{4,0},{6,2},{1,5},{3,7},{5,1},{7,3},{8,12},{10,14},{12... | collective-permute-start | bytes 393224 | tf_op jit(solution)/shard_map/ppermute | solution.py:197
  59.3 0.7 collective-permute-start.19
  60.1 0.7 pad_maximum_fusion.3
  60.8 0.6 collective-permute-done.17.refs_1_
  61.3 3.1 %collective-permute-done.18.refs_2_ = bf16[128,512]{1,0:T(8,128)(2,1)S(1)} collective-permute-done((bf16[128,512]{1,0:T(8,128)(2,1)S(1)}, bf16[128,512]{1,0:T(8,128)(2,1)S(1)}, u32[]{:S(2)}, u32[]{:S(2)}) %collective-permute-start.18) | collective-permute-done | bytes 131104 | tf_op jit(solution)/shard_map/ppermute | solution.py:197
  64.4 1.3 %collective-permute-done.19.refs_3_ = bf16[128,512]{1,0:T(8,128)(2,1)S(1)} collective-permute-done((bf16[128,512]{1,0:T(8,128)(2,1)S(1)}, bf16[128,512]{1,0:T(8,128)(2,1)S(1)}, u32[]{:S(2)}, u32[]{:S(2)}) %collective-permute-start.19) | collective-permute-done | bytes 131104 | tf_op jit(solution)/shard_map/ppermute | solution.py:197
  65.7 4.5 %grads.1 = (bf16[512,1280]{1,0:T(8,128)(2,1)}, f32[2,320,512]{2,1,0:T(8,128)}, bf16[2,320,512]{2,1,0:T(8,128)(2,1)S(1)}) custom-call(s32[2]{0:T(128)S(1)} %pad_add_fusion.at_ref, bf16[512,1280]{1,0:T(8,128)(2,1)} %bitcast.8.crossed_ref, bf16[1280,512]{1,0:T(8,128)(2,1)S(1)} %bitcast.80, bf16[128,512]{1,0:T(8,128)(2,1)S(1)} %fusion.15.refs_0_, ...), custom_call_target="tpu_custom_call" | custom-call | flops 1342177280 | bytes 8388608 | tf_op jit(solution)/shard_map/grads/pallas_call | solution.py:154
  70.4 4.8 %all-to-all-start.1 = ((bf16[4,128,1280]{2,1,0:T(8,128)(2,1)}), bf16[4,128,1280]{2,1,0:T(8,128)(2,1)}, u32[]{:S(2)}, u32[]{:S(2)}) async-start(bf16[4,128,1280]{2,1,0:T(8,128)(2,1)} %bitcast.82), calls=%async_computation.1 | async-start | bytes 2621440 | tf_op jit(solution)/shard_map/all_to_all | solution.py:346
  75.3 1.9 %fusion.29 = (bf16[160,512]{1,0:T(8,128)(2,1)}, bf16[160,512]{1,0:T(8,128)(2,1)}, bf16[160,512]{1,0:T(8,128)(2,1)}) fusion(f32[2,2,160,512]{3,2,1,0:T(8,128)S(1)} %bitcast.83, s32[]{:T(128)S(6)} %select_n.328, s32[]{:T(128)S(6)} %select_n.330, bf16[2,2,160,512]{3,2,1,0:T(8,128)(2,1)} %bitcast.26, s32[]{:T(128)S(6)} %select_n.323, s32[]{:T(128)S(6)} %select_n.325, ...), kind=kLoop, calls=%fused_computation.66 | loop fusion | flops 737280 | bytes 1966104 | tf_op jit(solution)/shard_map/convert_element_type | solution.py:318
  77.2 1.0 collective-permute-start.25
  78.2 3.6 %collective-permute-start.26 = (bf16[160,512]{1,0:T(8,128)(2,1)}, bf16[160,512]{1,0:T(8,128)(2,1)}, u32[]{:S(2)}, u32[]{:S(2)}) collective-permute-start(bf16[160,512]{1,0:T(8,128)(2,1)} %get-tuple-element.57), channel_id=1, source_target_pairs={{0,16},{8,24},{16,0},{24,8},{1,17},{9,25},{17,1},{25,9},{2,18},{10... | collective-permute-start | bytes 491528 | tf_op jit(solution)/shard_map/ppermute | solution.py:320
  81.7 1.0 collective-permute-start.27
  82.9 7.4 %scores.1 = (bf16[128,4096]{1,0:T(8,128)(2,1)}, f32[512,512]{1,0:T(8,128)S(1)}) custom-call(bf16[128,4096]{1,0:T(8,128)(2,1)} %bitcast.75, bf16[512,512]{1,0:T(8,128)(2,1)S(1)} %constant_dynamic-update-slice_fusion.k_ref, bf16[128,4096]{1,0:T(8,128)(2,1)} %bitcast.77, bf16[512,512]{1,0:T(8,128)(2,1)S(1)} %constant_dynamic-update-slice_fusion.1.v_ref, ...), custom_call_target="tpu_custom_call" | custom-call | flops 1610612736 | bytes 8388608 | tf_op jit(solution)/shard_map/scores/pallas_call | solution.py:94
  90.4 0.7 collective-permute-start.21
  91.0 1.3 %fusion.3 = bf16[160,512]{1,0:T(8,128)(2,1)S(1)} fusion(bf16[160,512]{1,0:T(8,128)(2,1)} %collective-permute-done.27, bf16[160,512]{1,0:T(8,128)(2,1)} %collective-permute-done.26, bf16[160,512]{1,0:T(8,128)(2,1)} %collective-permute-done.25, f32[2,2,160,512]{3,2,1,0:T(8,128)S(1)} %bitcast.84, s32[]{:T(128)S(6)} %select_n.341, s32[]{:T(128)S(6)} %select_n.343, ...), kind=kLoop, calls=%fused_computation.17 | loop fusion | flops 737280 | bytes 1146888 | tf_op jit(solution)/shard_map/convert_element_type | solution.py:330
  92.3 0.6 collective-permute-start.28
  93.3 2.9 %collective-permute-start.30 = (bf16[160,512]{1,0:T(8,128)(2,1)S(1)}, bf16[160,512]{1,0:T(8,128)(2,1)S(1)}, u32[]{:S(2)}, u32[]{:S(2)}) collective-permute-start(bf16[160,512]{1,0:T(8,128)(2,1)S(1)} %fusion.3), channel_id=1, source_target_pairs={{0,96},{32,0},{64,32},{96,64},{1,97},{33,1},{65,33},{97,65},{2,98}... | collective-permute-start | bytes 491528 | tf_op jit(solution)/shard_map/ppermute | solution.py:197
  96.1 3.4 %collective-permute-done.21 = bf16[256,512]{1,0:T(8,128)(2,1)S(1)} collective-permute-done((bf16[256,512]{1,0:T(8,128)(2,1)S(1)}, bf16[256,512]{1,0:T(8,128)(2,1)S(1)}, u32[]{:S(2)}, u32[]{:S(2)}) %collective-permute-start.21) | collective-permute-done | bytes 262176 | tf_op jit(solution)/shard_map/ppermute | solution.py:332
  99.7 0.5 collective-permute-start.23
  100.6 0.4 collective-permute-done.28
  101.0 2.4 %collective-permute-start.22 = (bf16[128,512]{1,0:T(8,128)(2,1)S(1)}, bf16[128,512]{1,0:T(8,128)(2,1)S(1)}, u32[]{:S(2)}, u32[]{:S(2)}) collective-permute-start(bf16[128,512]{1,0:T(8,128)(2,1)S(1)} %get-tuple-element.50), channel_id=1, source_target_pairs={{0,96},{32,0},{64,32},{96,64},{1,97},{33,1},{65,33},{97,65},{2,98}... | collective-permute-start | bytes 393224 | tf_op jit(solution)/shard_map/ppermute | solution.py:236
  103.5 3.8 %collective-permute-start.31 = (bf16[160,512]{1,0:T(8,128)(2,1)S(1)}, bf16[160,512]{1,0:T(8,128)(2,1)S(1)}, u32[]{:S(2)}, u32[]{:S(2)}) collective-permute-start(bf16[160,512]{1,0:T(8,128)(2,1)S(1)} %add_convert_fusion), channel_id=1, source_target_pairs={{0,16},{16,0},{1,17},{17,1},{2,18},{18,2},{3,19},{19,3},{4,20},{20... | collective-permute-start | bytes 491528 | tf_op jit(solution)/shard_map/ppermute | solution.py:337
  107.4 1.4 %slice_bitcast_fusion = (bf16[128,1280]{1,0:T(8,128)(2,1)S(1)}, bf16[128,1280]{1,0:T(8,128)(2,1)S(1)}, bf16[128,1280]{1,0:T(8,128)(2,1)S(1)}, bf16[128,1280]{1,0:T(8,128)(2,1)S(1)}) fusion(bf16[4,128,1280]{2,1,0:T(8,128)(2,1)} %all-to-all-done.1), kind=kLoop, calls=%fused_computation.18 | loop fusion | bytes 2621440 | tf_op jit(solution)/shard_map/squeeze | solution.py:349
  109.0 1.0 fusion.33
  110.0 1.2 %collective-permute-done.31 = bf16[160,512]{1,0:T(8,128)(2,1)S(1)} collective-permute-done((bf16[160,512]{1,0:T(8,128)(2,1)S(1)}, bf16[160,512]{1,0:T(8,128)(2,1)S(1)}, u32[]{:S(2)}, u32[]{:S(2)}) %collective-permute-start.31) | collective-permute-done | bytes 163872 | tf_op jit(solution)/shard_map/ppermute | solution.py:337
  111.2 0.9 fusion
  (99 shorter events, 3.6 us)
Async XLA Ops:
  0.6 10.8 %collective-permute-start = (bf16[128,512]{1,0:T(8,128)(2,1)}, bf16[128,512]{1,0:T(8,128)(2,1)S(1)}, u32[]{:S(2)}, u32[]{:S(2)}) collective-permute-start(bf16[128,512]{1,0:T(8,128)(2,1)} %bitcast.90), channel_id=1, source_target_pairs={{0,32},{32,64},{64,96},{96,0},{1,33},{33,65},{65,97},{97,1},{2,34}... | collective-permute-start | bytes 393224 | tf_op jit(solution)/shard_map/ppermute | solution.py:197
  2.3 9.2 %collective-permute-start.1 = (bf16[128,512]{1,0:T(8,128)(2,1)}, bf16[128,512]{1,0:T(8,128)(2,1)S(1)}, u32[]{:S(2)}, u32[]{:S(2)}) collective-permute-start(bf16[128,512]{1,0:T(8,128)(2,1)} %bitcast.91), channel_id=1, source_target_pairs={{0,64},{32,96},{64,0},{96,32},{1,65},{33,97},{65,1},{97,33},{2,66}... | collective-permute-start | bytes 393224 | tf_op jit(solution)/shard_map/ppermute | solution.py:197
  5.2 6.3 %collective-permute-start.2 = (bf16[128,512]{1,0:T(8,128)(2,1)}, bf16[128,512]{1,0:T(8,128)(2,1)S(1)}, u32[]{:S(2)}, u32[]{:S(2)}) collective-permute-start(bf16[128,512]{1,0:T(8,128)(2,1)} %bitcast.92), channel_id=1, source_target_pairs={{0,96},{32,0},{64,32},{96,64},{1,97},{33,1},{65,33},{97,65},{2,98}... | collective-permute-start | bytes 393224 | tf_op jit(solution)/shard_map/ppermute | solution.py:197
  6.5 14.3 %collective-permute-start.4 = (bf16[320,512]{1,0:T(8,128)(2,1)}, bf16[320,512]{1,0:T(8,128)(2,1)S(1)}, u32[]{:S(2)}, u32[]{:S(2)}) collective-permute-start(bf16[320,512]{1,0:T(8,128)(2,1)} %param.9), channel_id=1, source_target_pairs={{0,8},{8,0},{1,9},{9,1},{2,10},{10,2},{3,11},{11,3},{4,12},{12,4},... | collective-permute-start | bytes 983048 | tf_op jit(solution)/shard_map/ppermute | solution.py:269
  10.1 1.4 %copy-start.6 = (bf16[1,128,512]{2,1,0:T(8,128)(2,1)S(1)}, bf16[1,128,512]{2,1,0:T(8,128)(2,1)}, u32[]{:S(2)}) copy-start(bf16[1,128,512]{2,1,0:T(8,128)(2,1)} %param.8) | copy-start | bytes 393220
  11.3 4.1 %copy-start.8 = (s32[1,1024]{1,0:T(1,128)S(1)}, s32[1,1024]{1,0:T(1,128)}, u32[]{:S(2)}) copy-start(s32[1,1024]{1,0:T(1,128)} %param.11) | copy-start | bytes 12292
  11.5 12.9 %collective-permute-start.3 = (bf16[256,512]{1,0:T(8,128)(2,1)S(1)}, bf16[256,512]{1,0:T(8,128)(2,1)S(1)}, u32[]{:S(2)}, u32[]{:S(2)}) collective-permute-start(bf16[256,512]{1,0:T(8,128)(2,1)S(1)} %pad_maximum_fusion.1), channel_id=1, source_target_pairs={{0,16},{16,0},{1,17},{17,1},{2,18},{18,2},{3,19},{19,3},{4,20},{20... | collective-permute-start | bytes 786440 | tf_op jit(solution)/shard_map/ppermute | solution.py:256
  15.5 5.4 %copy-start.5 = (bf16[320,512]{1,0:T(8,128)(2,1)S(1)}, bf16[320,512]{1,0:T(8,128)(2,1)}, u32[]{:S(2)}) copy-start(bf16[320,512]{1,0:T(8,128)(2,1)} %param.9) | copy-start | bytes 983044
  15.5 20.6 %all-to-all-start = ((bf16[4,128,1280]{2,1,0:T(8,128)(2,1)}), bf16[4,128,1280]{2,1,0:T(8,128)(2,1)}, u32[]{:S(2)}, u32[]{:S(2)}) async-start(bf16[4,128,1280]{2,1,0:T(8,128)(2,1)} %pad_maximum_fusion), calls=%async_computation | async-start | bytes 2621440 | tf_op jit(solution)/shard_map/all_to_all | solution.py:268
  21.0 9.8 %collective-permute-start.5 = (bf16[2,320,512]{2,1,0:T(8,128)(2,1)S(1)}, bf16[2,320,512]{2,1,0:T(8,128)(2,1)S(1)}, u32[]{:S(2)}, u32[]{:S(2)}) collective-permute-start(bf16[2,320,512]{2,1,0:T(8,128)(2,1)S(1)} %maximum_select_fusion.2), channel_id=1, source_target_pairs={{0,1},{1,0},{2,3},{3,2},{4,5},{5,4},{6,7},{7,6},{8,9},{9,8},{10,11... | collective-permute-start | bytes 1966088 | tf_op jit(solution)/shard_map/ppermute | solution.py:273
  21.1 3.5 %copy-start = (bf16[1,128,4096]{2,1,0:T(8,128)(2,1)S(1)}, bf16[1,128,4096]{2,1,0:T(8,128)(2,1)}, u32[]{:S(2)}) copy-start(bf16[1,128,4096]{2,1,0:T(8,128)(2,1)} %param.7) | copy-start | bytes 3145732
  21.1 3.5 %copy-start.1 = (bf16[1,128,4096]{2,1,0:T(8,128)(2,1)S(1)}, bf16[1,128,4096]{2,1,0:T(8,128)(2,1)}, u32[]{:S(2)}) copy-start(bf16[1,128,4096]{2,1,0:T(8,128)(2,1)} %param.10) | copy-start | bytes 3145732
  30.6 1.0 copy-start.2
  30.7 11.8 %collective-permute-start.9 = (bf16[256,512]{1,0:T(8,128)(2,1)S(1)}, bf16[256,512]{1,0:T(8,128)(2,1)S(1)}, u32[]{:S(2)}, u32[]{:S(2)}) collective-permute-start(bf16[256,512]{1,0:T(8,128)(2,1)S(1)} %pad_maximum_fusion.2), channel_id=1, source_target_pairs={{0,16},{16,0},{1,17},{17,1},{2,18},{18,2},{3,19},{19,3},{4,20},{20... | collective-permute-start | bytes 786440 | tf_op jit(solution)/shard_map/ppermute | solution.py:281
  36.1 6.5 %copy-start.3 = (f32[512,512]{1,0:T(8,128)S(1)}, f32[512,512]{1,0:T(8,128)}, u32[]{:S(2)}) copy-start(f32[512,512]{1,0:T(8,128)} %copy-done.2) | copy-start | bytes 3145732
  38.4 7.6 %collective-permute-start.6 = (bf16[128,512]{1,0:T(8,128)(2,1)S(1)}, bf16[128,512]{1,0:T(8,128)(2,1)S(1)}, u32[]{:S(2)}, u32[]{:S(2)}) collective-permute-start(bf16[128,512]{1,0:T(8,128)(2,1)S(1)} %get-tuple-element.79), channel_id=1, source_target_pairs={{0,2},{2,4},{4,6},{6,0},{1,3},{3,5},{5,7},{7,1},{8,10},{10,12},{12... | collective-permute-start | bytes 393224 | tf_op jit(solution)/shard_map/ppermute | solution.py:289
  38.5 9.9 %collective-permute-start.7 = (bf16[128,512]{1,0:T(8,128)(2,1)S(1)}, bf16[128,512]{1,0:T(8,128)(2,1)S(1)}, u32[]{:S(2)}, u32[]{:S(2)}) collective-permute-start(bf16[128,512]{1,0:T(8,128)(2,1)S(1)} %get-tuple-element.78), channel_id=1, source_target_pairs={{0,4},{2,6},{4,0},{6,2},{1,5},{3,7},{5,1},{7,3},{8,12},{10,14},{12... | collective-permute-start | bytes 393224 | tf_op jit(solution)/shard_map/ppermute | solution.py:289
  42.0 6.4 %collective-permute-start.8 = (bf16[128,512]{1,0:T(8,128)(2,1)S(1)}, bf16[128,512]{1,0:T(8,128)(2,1)S(1)}, u32[]{:S(2)}, u32[]{:S(2)}) collective-permute-start(bf16[128,512]{1,0:T(8,128)(2,1)S(1)} %get-tuple-element.77), channel_id=1, source_target_pairs={{0,6},{2,0},{4,2},{6,4},{1,7},{3,1},{5,3},{7,5},{8,14},{10,8},{12,... | collective-permute-start | bytes 393224 | tf_op jit(solution)/shard_map/ppermute | solution.py:289
  42.6 13.5 %collective-permute-start.15 = (bf16[128,512]{1,0:T(8,128)(2,1)S(1)}, bf16[128,512]{1,0:T(8,128)(2,1)S(1)}, u32[]{:S(2)}, u32[]{:S(2)}) collective-permute-start(bf16[128,512]{1,0:T(8,128)(2,1)S(1)} %get-tuple-element.52), channel_id=1, source_target_pairs={{0,64},{32,96},{64,0},{96,32},{1,65},{33,97},{65,1},{97,33},{2,66}... | collective-permute-start | bytes 393224 | tf_op jit(solution)/shard_map/ppermute | solution.py:238
  45.0 11.2 %collective-permute-start.16 = (bf16[128,512]{1,0:T(8,128)(2,1)S(1)}, bf16[128,512]{1,0:T(8,128)(2,1)S(1)}, u32[]{:S(2)}, u32[]{:S(2)}) collective-permute-start(bf16[128,512]{1,0:T(8,128)(2,1)S(1)} %get-tuple-element.52), channel_id=1, source_target_pairs={{0,32},{32,64},{64,96},{96,0},{1,33},{33,65},{65,97},{97,1},{2,34}... | collective-permute-start | bytes 393224 | tf_op jit(solution)/shard_map/ppermute | solution.py:237
  46.1 6.4 %collective-permute-start.14 = (bf16[128,512]{1,0:T(8,128)(2,1)S(1)}, bf16[128,512]{1,0:T(8,128)(2,1)S(1)}, u32[]{:S(2)}, u32[]{:S(2)}) collective-permute-start(bf16[128,512]{1,0:T(8,128)(2,1)S(1)} %fusion.10), channel_id=1, source_target_pairs={{0,96},{32,0},{64,32},{96,64},{1,97},{33,1},{65,33},{97,65},{2,98}... | collective-permute-start | bytes 393224 | tf_op jit(solution)/shard_map/ppermute | solution.py:236
  48.5 10.9 %collective-permute-start.10 = (bf16[128,512]{1,0:T(8,128)(2,1)S(1)}, bf16[128,512]{1,0:T(8,128)(2,1)S(1)}, u32[]{:S(2)}, u32[]{:S(2)}) collective-permute-start(bf16[128,512]{1,0:T(8,128)(2,1)S(1)} %fusion.26), channel_id=1, source_target_pairs={{0,32},{32,64},{64,96},{96,0},{1,33},{33,65},{65,97},{97,1},{2,34}... | collective-permute-start | bytes 393224 | tf_op jit(solution)/shard_map/ppermute | solution.py:197
  48.6 11.5 %collective-permute-start.11 = (bf16[128,512]{1,0:T(8,128)(2,1)S(1)}, bf16[128,512]{1,0:T(8,128)(2,1)S(1)}, u32[]{:S(2)}, u32[]{:S(2)}) collective-permute-start(bf16[128,512]{1,0:T(8,128)(2,1)S(1)} %fusion.26), channel_id=1, source_target_pairs={{0,64},{32,96},{64,0},{96,32},{1,65},{33,97},{65,1},{97,33},{2,66}... | collective-permute-start | bytes 393224 | tf_op jit(solution)/shard_map/ppermute | solution.py:197
  52.5 7.5 %collective-permute-start.12 = (bf16[128,512]{1,0:T(8,128)(2,1)S(1)}, bf16[128,512]{1,0:T(8,128)(2,1)S(1)}, u32[]{:S(2)}, u32[]{:S(2)}) collective-permute-start(bf16[128,512]{1,0:T(8,128)(2,1)S(1)} %fusion.26), channel_id=1, source_target_pairs={{0,96},{32,0},{64,32},{96,64},{1,97},{33,1},{65,33},{97,65},{2,98}... | collective-permute-start | bytes 393224 | tf_op jit(solution)/shard_map/ppermute | solution.py:197
  56.3 5.0 %collective-permute-start.17 = (bf16[128,512]{1,0:T(8,128)(2,1)S(1)}, bf16[128,512]{1,0:T(8,128)(2,1)S(1)}, u32[]{:S(2)}, u32[]{:S(2)}) collective-permute-start(bf16[128,512]{1,0:T(8,128)(2,1)S(1)} %fusion.15.refs_0_), channel_id=1, source_target_pairs={{0,2},{2,4},{4,6},{6,0},{1,3},{3,5},{5,7},{7,1},{8,10},{10,12},{12... | collective-permute-start | bytes 393224 | tf_op jit(solution)/shard_map/ppermute | solution.py:197
  57.8 6.6 %collective-permute-start.18 = (bf16[128,512]{1,0:T(8,128)(2,1)S(1)}, bf16[128,512]{1,0:T(8,128)(2,1)S(1)}, u32[]{:S(2)}, u32[]{:S(2)}) collective-permute-start(bf16[128,512]{1,0:T(8,128)(2,1)S(1)} %fusion.15.refs_0_), channel_id=1, source_target_pairs={{0,4},{2,6},{4,0},{6,2},{1,5},{3,7},{5,1},{7,3},{8,12},{10,14},{12... | collective-permute-start | bytes 393224 | tf_op jit(solution)/shard_map/ppermute | solution.py:197
  59.3 6.4 %collective-permute-start.19 = (bf16[128,512]{1,0:T(8,128)(2,1)S(1)}, bf16[128,512]{1,0:T(8,128)(2,1)S(1)}, u32[]{:S(2)}, u32[]{:S(2)}) collective-permute-start(bf16[128,512]{1,0:T(8,128)(2,1)S(1)} %fusion.15.refs_0_), channel_id=1, source_target_pairs={{0,6},{2,0},{4,2},{6,4},{1,7},{3,1},{5,3},{7,5},{8,14},{10,8},{12,... | collective-permute-start | bytes 393224 | tf_op jit(solution)/shard_map/ppermute | solution.py:197
  70.2 5.1 %collective-permute-start.20 = (bf16[2,320,512]{2,1,0:T(8,128)(2,1)S(1)}, bf16[2,320,512]{2,1,0:T(8,128)(2,1)}, u32[]{:S(2)}, u32[]{:S(2)}) collective-permute-start(bf16[2,320,512]{2,1,0:T(8,128)(2,1)S(1)} %get-tuple-element.42), channel_id=1, source_target_pairs={{0,1},{1,0},{2,3},{3,2},{4,5},{5,4},{6,7},{7,6},{8,9},{9,8},{10,11... | collective-permute-start | bytes 1966088 | tf_op jit(solution)/shard_map/ppermute | solution.py:307
  70.2 12.6 %collective-permute-start.13 = (bf16[256,512]{1,0:T(8,128)(2,1)}, bf16[256,512]{1,0:T(8,128)(2,1)S(1)}, u32[]{:S(2)}, u32[]{:S(2)}) collective-permute-start(bf16[256,512]{1,0:T(8,128)(2,1)} %pad_maximum_fusion.3), channel_id=1, source_target_pairs={{0,16},{16,0},{1,17},{17,1},{2,18},{18,2},{3,19},{19,3},{4,20},{20... | collective-permute-start | bytes 786440 | tf_op jit(solution)/shard_map/ppermute | solution.py:303
  70.4 4.8 %copy-start.4 = (f32[2,320,512]{2,1,0:T(8,128)S(1)}, f32[2,320,512]{2,1,0:T(8,128)}, u32[]{:S(2)}) copy-start(f32[2,320,512]{2,1,0:T(8,128)} %get-tuple-element.41) | copy-start | bytes 3932164
  70.4 36.9 %all-to-all-start.1 = ((bf16[4,128,1280]{2,1,0:T(8,128)(2,1)}), bf16[4,128,1280]{2,1,0:T(8,128)(2,1)}, u32[]{:S(2)}, u32[]{:S(2)}) async-start(bf16[4,128,1280]{2,1,0:T(8,128)(2,1)} %bitcast.82), calls=%async_computation.1 | async-start | bytes 2621440 | tf_op jit(solution)/shard_map/all_to_all | solution.py:346
  77.2 13.8 %collective-permute-start.25 = (bf16[160,512]{1,0:T(8,128)(2,1)}, bf16[160,512]{1,0:T(8,128)(2,1)}, u32[]{:S(2)}, u32[]{:S(2)}) collective-permute-start(bf16[160,512]{1,0:T(8,128)(2,1)} %get-tuple-element.58), channel_id=1, source_target_pairs={{0,8},{8,16},{16,24},{24,0},{1,9},{9,17},{17,25},{25,1},{2,10},{10... | collective-permute-start | bytes 491528 | tf_op jit(solution)/shard_map/ppermute | solution.py:320
  78.2 12.9 %collective-permute-start.26 = (bf16[160,512]{1,0:T(8,128)(2,1)}, bf16[160,512]{1,0:T(8,128)(2,1)}, u32[]{:S(2)}, u32[]{:S(2)}) collective-permute-start(bf16[160,512]{1,0:T(8,128)(2,1)} %get-tuple-element.57), channel_id=1, source_target_pairs={{0,16},{8,24},{16,0},{24,8},{1,17},{9,25},{17,1},{25,9},{2,18},{10... | collective-permute-start | bytes 491528 | tf_op jit(solution)/shard_map/ppermute | solution.py:320
  81.7 9.3 %collective-permute-start.27 = (bf16[160,512]{1,0:T(8,128)(2,1)}, bf16[160,512]{1,0:T(8,128)(2,1)}, u32[]{:S(2)}, u32[]{:S(2)}) collective-permute-start(bf16[160,512]{1,0:T(8,128)(2,1)} %get-tuple-element.56), channel_id=1, source_target_pairs={{0,24},{8,0},{16,8},{24,16},{1,25},{9,1},{17,9},{25,17},{2,26},{10... | collective-permute-start | bytes 491528 | tf_op jit(solution)/shard_map/ppermute | solution.py:320
  90.4 9.2 %collective-permute-start.21 = (bf16[256,512]{1,0:T(8,128)(2,1)S(1)}, bf16[256,512]{1,0:T(8,128)(2,1)S(1)}, u32[]{:S(2)}, u32[]{:S(2)}) collective-permute-start(bf16[256,512]{1,0:T(8,128)(2,1)S(1)} %pad_maximum_fusion.4), channel_id=1, source_target_pairs={{0,16},{16,0},{1,17},{17,1},{2,18},{18,2},{3,19},{19,3},{4,20},{20... | collective-permute-start | bytes 786440 | tf_op jit(solution)/shard_map/ppermute | solution.py:332
  92.3 8.7 %collective-permute-start.28 = (bf16[160,512]{1,0:T(8,128)(2,1)S(1)}, bf16[160,512]{1,0:T(8,128)(2,1)S(1)}, u32[]{:S(2)}, u32[]{:S(2)}) collective-permute-start(bf16[160,512]{1,0:T(8,128)(2,1)S(1)} %fusion.3), channel_id=1, source_target_pairs={{0,64},{32,96},{64,0},{96,32},{1,65},{33,97},{65,1},{97,33},{2,66}... | collective-permute-start | bytes 491528 | tf_op jit(solution)/shard_map/ppermute | solution.py:197
  92.9 10.5 %collective-permute-start.29 = (bf16[160,512]{1,0:T(8,128)(2,1)S(1)}, bf16[160,512]{1,0:T(8,128)(2,1)S(1)}, u32[]{:S(2)}, u32[]{:S(2)}) collective-permute-start(bf16[160,512]{1,0:T(8,128)(2,1)S(1)} %fusion.3), channel_id=1, source_target_pairs={{0,32},{32,64},{64,96},{96,0},{1,33},{33,65},{65,97},{97,1},{2,34}... | collective-permute-start | bytes 491528 | tf_op jit(solution)/shard_map/ppermute | solution.py:197
  93.3 10.2 %collective-permute-start.30 = (bf16[160,512]{1,0:T(8,128)(2,1)S(1)}, bf16[160,512]{1,0:T(8,128)(2,1)S(1)}, u32[]{:S(2)}, u32[]{:S(2)}) collective-permute-start(bf16[160,512]{1,0:T(8,128)(2,1)S(1)} %fusion.3), channel_id=1, source_target_pairs={{0,96},{32,0},{64,32},{96,64},{1,97},{33,1},{65,33},{97,65},{2,98}... | collective-permute-start | bytes 491528 | tf_op jit(solution)/shard_map/ppermute | solution.py:197
  99.7 9.3 %collective-permute-start.23 = (bf16[128,512]{1,0:T(8,128)(2,1)S(1)}, bf16[128,512]{1,0:T(8,128)(2,1)S(1)}, u32[]{:S(2)}, u32[]{:S(2)}) collective-permute-start(bf16[128,512]{1,0:T(8,128)(2,1)S(1)} %convert_element_type.175), channel_id=1, source_target_pairs={{0,64},{32,96},{64,0},{96,32},{1,65},{33,97},{65,1},{97,33},{2,66}... | collective-permute-start | bytes 393224 | tf_op jit(solution)/shard_map/ppermute | solution.py:238
  100.2 8.8 %collective-permute-start.24 = (bf16[128,512]{1,0:T(8,128)(2,1)S(1)}, bf16[128,512]{1,0:T(8,128)(2,1)S(1)}, u32[]{:S(2)}, u32[]{:S(2)}) collective-permute-start(bf16[128,512]{1,0:T(8,128)(2,1)S(1)} %convert_element_type.175), channel_id=1, source_target_pairs={{0,32},{32,64},{64,96},{96,0},{1,33},{33,65},{65,97},{97,1},{2,34}... | collective-permute-start | bytes 393224 | tf_op jit(solution)/shard_map/ppermute | solution.py:237
  101.0 8.0 %collective-permute-start.22 = (bf16[128,512]{1,0:T(8,128)(2,1)S(1)}, bf16[128,512]{1,0:T(8,128)(2,1)S(1)}, u32[]{:S(2)}, u32[]{:S(2)}) collective-permute-start(bf16[128,512]{1,0:T(8,128)(2,1)S(1)} %get-tuple-element.50), channel_id=1, source_target_pairs={{0,96},{32,0},{64,32},{96,64},{1,97},{33,1},{65,33},{97,65},{2,98}... | collective-permute-start | bytes 393224 | tf_op jit(solution)/shard_map/ppermute | solution.py:236
  103.5 7.6 %collective-permute-start.31 = (bf16[160,512]{1,0:T(8,128)(2,1)S(1)}, bf16[160,512]{1,0:T(8,128)(2,1)S(1)}, u32[]{:S(2)}, u32[]{:S(2)}) collective-permute-start(bf16[160,512]{1,0:T(8,128)(2,1)S(1)} %add_convert_fusion), channel_id=1, source_target_pairs={{0,16},{16,0},{1,17},{17,1},{2,18},{18,2},{3,19},{19,3},{4,20},{20... | collective-permute-start | bytes 491528 | tf_op jit(solution)/shard_map/ppermute | solution.py:337
  109.0 3.1 %copy-start.7 = (bf16[128,5120]{1,0:T(8,128)(2,1)}, bf16[128,5120]{1,0:T(8,128)(2,1)S(1)}, u32[]{:S(2)}) copy-start(bf16[128,5120]{1,0:T(8,128)(2,1)S(1)} %slice_dynamic-update-slice_fusion) | copy-start | bytes 3932164
